TPU v7x, 32 devices: a whole 2x2x4 slice. The times are simulated.
32 devices in a mesh: groups: 2 (over x), attn: 8 (over z, y), expert: 2 (over core).
Axes of the slice: x: 2, y: 2, z: 4, core: 2. Of those that a mesh axis runs over, the one named last changes fastest.
Arguments:
- hidden_in: bfloat16 [512, 6144], P(('groups', 'attn', 'expert')), parts along dimension 0, may hold values from -6 to 6
- queries: bfloat16 [512, 6144], P(('groups', 'attn', 'expert')), parts along dimension 0, may hold values from -60 to 60
- cache_keys: bfloat16 [512, 64, 1024], P(('groups', 'attn', 'expert')), parts along dimension 0, may hold values from -4 to 4
- cache_values: bfloat16 [512, 64, 1024], P(('groups', 'attn', 'expert')), parts along dimension 0, may hold values from -6 to 6
- new_keys: bfloat16 [512, 1024], P(('groups', 'attn', 'expert')), parts along dimension 0, may hold values from -6 to 6
- new_values: bfloat16 [512, 1024], P(('groups', 'attn', 'expert')), parts along dimension 0, may hold values from -6 to 6
- lengths: int32 [512], P(('groups', 'attn', 'expert')), parts along dimension 0, may hold values from 2 to 64
- expert_ids: int32 [512, 4], P(('groups', 'attn', 'expert')), parts along dimension 0, may hold values from 0 to 15, as said below
- gate_probs: float32 [512, 4], P(('groups', 'attn', 'expert')), parts along dimension 0, may hold values from 0.05 to 1
- w_gate: bfloat16 [2, 6144, 6144], P('expert', None, 'attn'), may hold values from -0.078125 to 0.078125
- w_up: bfloat16 [2, 6144, 6144], P('expert', None, 'attn'), may hold values from -0.078125 to 0.078125
- w_down: bfloat16 [2, 6144, 6144], P('expert', 'attn'), may hold values from -0.078125 to 0.078125
Outputs:
- stream: float32 [512, 6144], P(('groups', 'attn', 'expert')), parts along dimension 0
There are 2 independent parts, one for each index of `groups`. A program takes and returns all parts, laid end to end along the dimension named above; an argument that names none is the same for every part. Nothing has to cross between parts.
Inputs may be any that keep to these rules, and one draw needn't show every extreme that they name: `expert_ids`: each request names 4 different experts. Among the 16 requests of one device exactly 8 name expert 0 and 1 to 8 name expert 1, exactly 8 on some device.
All inputs are finite; a program needn't handle non-finite values.
Results may differ from a plain program's by a relative error of at most 0.0019.
Values may be sent and summed in bfloat16 or wider, within the bound.
No kernel may reach another device: no remote copies, remote signals or barrier semaphores. Data moves between devices by JAX's collectives and lax.ppermute only.
A program may use at most 128 MiB of HBM per device.

v0:
```python
import math

import jax
import jax.numpy as jnp
from jax import lax
from jax.sharding import PartitionSpec as P

HEAD = 128


def body(
    hidden_in,
    queries,
    cache_keys,
    cache_values,
    new_keys,
    new_values,
    lengths,
    expert_ids,
    gate_probs,
    w_gate,
    w_up,
    w_down,
):
    row_count = hidden_in.shape[0]
    feat_width = hidden_in.shape[1]
    cache_span = cache_keys.shape[1]
    kv_width = cache_keys.shape[2]
    kv_heads = kv_width // HEAD
    group_size = queries.shape[1] // kv_width
    score_scale = 1.0 / math.sqrt(HEAD)
    query_heads = queries.reshape(row_count, kv_heads, group_size, HEAD)
    key_cache = cache_keys.reshape(row_count, cache_span, kv_heads, HEAD)
    val_cache = cache_values.reshape(row_count, cache_span, kv_heads, HEAD)
    cached = (
        jnp.einsum("rgjd,rpgd->rgjp", query_heads, key_cache, preferred_element_type=jnp.float32)
        * score_scale
    )
    valid_mask = (jnp.arange(cache_span, dtype=jnp.int32)[None, :] < lengths[:, None])[
        :, None, None, :
    ]
    cached = jnp.where(valid_mask, cached, -1e30)
    own_score = (
        jnp.einsum(
            "rgjd,rgd->rgj",
            query_heads,
            new_keys.reshape(row_count, kv_heads, HEAD),
            preferred_element_type=jnp.float32,
        )
        * score_scale
    )
    top_score = jnp.maximum(jnp.max(cached, -1), own_score)
    cached_exp = jnp.where(valid_mask, jnp.exp(cached - top_score[..., None]), 0.0)
    own_exp = jnp.exp(own_score - top_score)
    denom_sum = jnp.sum(cached_exp, -1) + own_exp
    weights_cache = (cached_exp / denom_sum[..., None]).astype(jnp.bfloat16)
    weights_own = (own_exp / denom_sum).astype(jnp.bfloat16)
    mixed = jnp.einsum(
        "rgjp,rpgd->rgjd", weights_cache, val_cache, preferred_element_type=jnp.float32
    )
    own_values = new_values.astype(jnp.float32).reshape(row_count, kv_heads, 1, HEAD)
    mixed = mixed + weights_own.astype(jnp.float32)[..., None] * own_values
    residual = hidden_in.astype(jnp.float32) + mixed.reshape(row_count, feat_width)
    centre = jnp.mean(residual, -1, keepdims=True)
    centered = residual - centre
    variance = jnp.mean(centered * centered, -1, keepdims=True)
    normed = (centered * lax.rsqrt(variance + 1e-05)).astype(jnp.bfloat16)
    mix_weights = gate_probs / jnp.sum(gate_probs, -1, keepdims=True)
    experts_here = lax.axis_size("expert")
    labels = jnp.arange(experts_here, dtype=jnp.int32)
    matches = expert_ids[None, :, :] == labels[:, None, None]
    coefficient = jnp.sum(jnp.where(matches, mix_weights[None], 0.0), -1)
    chosen = jnp.any(matches, -1)
    slot_rank = jnp.cumsum(chosen.astype(jnp.int32), 1) - 1
    cap_slots = row_count // 2
    selector = (
        slot_rank[:, None, :] == jnp.arange(cap_slots, dtype=jnp.int32)[None, :, None]
    ) & chosen[:, None, :]
    outgoing = jnp.einsum(
        "ejr,rd->ejd", selector.astype(jnp.bfloat16), normed, preferred_element_type=jnp.float32
    ).astype(jnp.bfloat16)
    peer_count = lax.axis_size("attn")
    fanned = jnp.broadcast_to(outgoing[None], (peer_count,) + outgoing.shape).reshape(
        peer_count * experts_here, cap_slots, feat_width
    )
    arrived = lax.all_to_all(fanned, ("attn", "expert"), split_axis=0, concat_axis=0, tiled=True)
    piece_rows = arrived.reshape(peer_count, experts_here, cap_slots, feat_width)
    flat_rows = piece_rows.reshape(-1, feat_width)
    gate_act = jnp.dot(flat_rows, w_gate[0], preferred_element_type=jnp.float32)
    upward = jnp.dot(flat_rows, w_up[0], preferred_element_type=jnp.float32)
    hidden_act = (jax.nn.silu(gate_act) * upward).astype(jnp.bfloat16)
    result = jnp.dot(hidden_act, w_down[0], preferred_element_type=jnp.float32)
    partial_value = result.reshape(piece_rows.shape[:-1] + (feat_width,))
    arrived_back = lax.all_to_all(
        partial_value.reshape(peer_count * experts_here, cap_slots, feat_width).astype(
            jnp.bfloat16
        ),
        ("attn", "expert"),
        split_axis=0,
        concat_axis=0,
        tiled=True,
    ).astype(jnp.float32)
    returned = jnp.sum(arrived_back.reshape(peer_count, experts_here, cap_slots, feat_width), 0)
    weighted = selector.astype(jnp.float32) * coefficient[:, None, :]
    expert_sum = jnp.einsum("ejr,ejd->rd", weighted, returned, precision=lax.Precision.HIGHEST)
    return residual + expert_sum


def solution(mesh):
    placed = (
        P(("groups", "attn", "expert"), None),
        P(("groups", "attn", "expert"), None),
        P(("groups", "attn", "expert"), None, None),
        P(("groups", "attn", "expert"), None, None),
        P(("groups", "attn", "expert"), None),
        P(("groups", "attn", "expert"), None),
        P(("groups", "attn", "expert")),
        P(("groups", "attn", "expert"), None),
        P(("groups", "attn", "expert"), None),
        P("expert", None, "attn"),
        P("expert", None, "attn"),
        P("expert", "attn", None),
    )
    return jax.shard_map(
        body,
        mesh=mesh,
        in_specs=placed,
        out_specs=P(("groups", "attn", "expert"), None),
        check_vma=False,
    )
```

profile of v0, /device:TPU:13, one launch (start us, length us, event | category | flops | bytes accessed | tf_op | source)
XLA Modules:
  0.0 106.7 jit_solution(1486703101764933643)
XLA Ops:
  0.0 0.0 copy-start
  0.0 0.9 iota_compare_fusion.1
  0.9 1.2 %reshape.74 = bf16[16,8,6,128]{3,2,1,0:T(8,128)(2,1)S(1)} reshape(bf16[16,6144]{1,0:T(8,128)(2,1)} %param.13) | data formatting | bytes 393216 | tf_op jit(solution)/shard_map/reshape | solution.py:32
  2.1 0.8 reshape.91
  2.9 0.3 fusion.68
  3.2 0.0 copy-start.2
  3.2 2.9 %fusion.67 = (f32[16,8,6]{2,1,0:T(8,128)S(1)}, f32[16,8,6,64]{3,2,1,0:T(8,128)S(1)}) fusion(bf16[16,8,6,128]{3,2,1,0:T(8,128)(2,1)S(1)} %reshape.74, pred[16,64]{1,0:T(8,128)(4,1)S(1)} %iota_compare_fusion.1, bf16[16,64,1024]{2,1,0:T(8,128)(2,1)} %param.14), kind=kOutput, calls=%fused_computation.64 | convolution fusion | flops 12729600 | bytes 2494464 | tf_op jit(solution)/shard_map/rgjd,rpgd->rgjp/dot_general | solution.py:36
  6.1 0.4 fusion.42
  6.5 0.0 copy-done.2
  6.6 0.0 copy-done
  6.6 0.0 copy-start.1
  6.6 0.9 fusion.24
  7.5 0.0 copy-start.3
  7.5 0.1 reshape.78
  7.7 0.2 fusion.52
  7.8 0.2 multiply_reduce_fusion
  8.1 0.1 copy-done.3
  8.2 0.2 reduce_window_sum.11
  8.4 0.3 convolution_convert_fusion
  8.7 0.1 broadcast_in_dim.57
  8.9 0.0 slice-start
  8.9 42.7 %all_to_all.10 = bf16[16,8,6144]{2,1,0:T(8,128)(2,1)S(1)} all-to-all(bf16[16,8,6144]{2,1,0:T(8,128)(2,1)S(1)} %bitcast.77), channel_id=1, replica_groups=mesh['groups'=2,'attn'=8,'expert'=2] {'attn','expert'}, dimensions={0} | all-to-all | bytes 3145728 | tf_op jit(solution)/shard_map/all_to_all | solution.py:86
  51.6 5.3 %fusion.4 = f32[128,768]{1,0:T(8,128)S(1)} fusion(bf16[1,6144,768]{2,1,0:T(8,128)(2,1)} %param.21, bf16[16,8,6144]{2,1,0:T(8,128)(2,1)S(1)} %all_to_all.10), kind=kOutput, calls=%fused_computation.4 | convolution fusion | flops 1207959552 | bytes 11403264 | tf_op jit(solution)/shard_map/dot_general | solution.py:89
  56.9 0.0 slice-start.5
  56.9 1.5 %fusion.37 = bf16[16,8,768]{2,1,0:T(8,128)(2,1)S(1)} fusion(bf16[1,6144,768]{2,1,0:T(8,128)(2,1)S(1)} %bitcast.74, bf16[16,8,6144]{2,1,0:T(8,128)(2,1)S(1)} %all_to_all.10, f32[128,768]{1,0:T(8,128)S(1)} %fusion.4), kind=kOutput, calls=%fused_computation.24 | convolution fusion | flops 1208549376 | bytes 11599872 | tf_op jit(solution)/shard_map/dot_general | solution.py:90
  58.4 0.8 slice-done.4
  59.2 0.4 slice-done.5
  59.7 2.7 %fusion.6 = bf16[16,8,6144]{2,1,0:T(8,128)(2,1)} fusion(bf16[16,8,768]{2,1,0:T(8,128)(2,1)S(1)} %fusion.37, bf16[1,768,6144]{2,1,0:T(8,128)(2,1)S(1)} %bitcast.76), kind=kOutput, calls=%fused_computation.6 | convolution fusion | flops 1208745984 | bytes 11206656 | tf_op jit(solution)/shard_map/dot_general | solution.py:92
  62.3 5.2 %all-to-all-start.1 = ((bf16[16,8,6144]{2,1,0:T(8,128)(2,1)}), bf16[16,8,6144]{2,1,0:T(8,128)(2,1)}, u32[]{:S(2)}, u32[]{:S(2)}) async-start(bf16[16,8,6144]{2,1,0:T(8,128)(2,1)} %fusion.6), calls=%async_computation.1 | async-start | bytes 3145728 | tf_op jit(solution)/shard_map/all_to_all | solution.py:94
  67.6 36.2 %all-to-all-done.1 = bf16[16,8,6144]{2,1,0:T(8,128)(2,1)} async-done(((bf16[16,8,6144]{2,1,0:T(8,128)(2,1)}), bf16[16,8,6144]{2,1,0:T(8,128)(2,1)}, u32[]{:S(2)}, u32[]{:S(2)}) %all-to-all-start.1) | async-done | bytes 1572896 | tf_op jit(solution)/shard_map/all_to_all | solution.py:94
  103.8 1.7 %convert_reduce_fusion = f32[2,8,6144]{2,1,0:T(8,128)S(1)} fusion(bf16[8,2,8,6144]{3,2,1,0:T(8,128)(2,1)} %bitcast.12), kind=kLoop, calls=%fused_computation.10 | loop fusion | flops 1474560 | bytes 1966080 | tf_op jit(solution)/shard_map/reduce_sum | solution.py:103
  105.5 1.3 %fusion.9 = f32[16,6144]{1,0:T(8,128)} fusion(f32[2,8,6144]{2,1,0:T(8,128)S(1)} %convert_reduce_fusion, f32[16,6144]{1,0:T(8,128)S(1)} %reshape.78, bf16[16,6144]{1,0:T(8,128)(2,1)S(1)} %copy-done.1, f32[2,16]{1,0:T(2,128)S(1)} %select_reduce_fusion, s32[2,16]{1,0:T(2,128)S(1)} %broadcast_add_fusion, pred[2,16]{1,0:T(4,128)(4,1)S(1)} %fusion.62), kind=kOutput, calls=%fused_computation.8 | convolution fusion | flops 19170048 | bytes 1376544 | tf_op jit(solution)/shard_map/ejr,ejd->rd/dot_general | solution.py:105
  (25 shorter events, 0.2 us)
Async XLA Ops:
  0.0 6.6 %copy-start = (bf16[16,64,1024]{2,1,0:T(8,128)(2,1)S(1)}, bf16[16,64,1024]{2,1,0:T(8,128)(2,1)}, u32[]{:S(2)}) copy-start(bf16[16,64,1024]{2,1,0:T(8,128)(2,1)} %param.15) | copy-start | bytes 6291460
  3.2 3.4 %copy-start.2 = (bf16[16,1024]{1,0:T(8,128)(2,1)S(1)}, bf16[16,1024]{1,0:T(8,128)(2,1)}, u32[]{:S(2)}) copy-start(bf16[16,1024]{1,0:T(8,128)(2,1)} %param.17) | copy-start | bytes 98308
  6.6 1.1 %copy-start.1 = (bf16[16,6144]{1,0:T(8,128)(2,1)S(1)}, bf16[16,6144]{1,0:T(8,128)(2,1)}, u32[]{:S(2)}) copy-start(bf16[16,6144]{1,0:T(8,128)(2,1)} %param.12) | copy-start | bytes 589828
  7.5 0.7 copy-start.3
  8.9 48.0 %slice-start = ((s8[9437184]{0:T(1024)(128)(4,1)}), s8[4194304]{0:T(1024)(128)(4,1)S(1)}, s32[]{:S(2)}) async-start(s8[9437184]{0:T(1024)(128)(4,1)} %bitcast.73), calls=%async_computation.2 | async-start | bytes 8388608
  51.6 5.3 %slice-start.1 = ((s8[9437184]{0:T(1024)(128)(4,1)}), s8[4194304]{0:T(1024)(128)(4,1)S(1)}, s32[]{:S(2)}) async-start(s8[9437184]{0:T(1024)(128)(4,1)} %bitcast.73), calls=%async_computation.3 | async-start | bytes 8388608
  51.6 5.3 %slice-start.2 = ((s8[9437184]{0:T(1024)(128)(4,1)}), s8[1048576]{0:T(1024)(128)(4,1)S(1)}, s32[]{:S(2)}) async-start(s8[9437184]{0:T(1024)(128)(4,1)} %bitcast.73), calls=%async_computation.4 | async-start | bytes 2097152
  51.6 6.8 %slice-start.3 = ((s8[9437184]{0:T(1024)(128)(4,1)}), s8[4194304]{0:T(1024)(128)(4,1)S(1)}, s32[]{:S(2)}) async-start(s8[9437184]{0:T(1024)(128)(4,1)} %bitcast.75), calls=%async_computation.5 | async-start | bytes 8388608
  51.6 7.7 %slice-start.4 = ((s8[9437184]{0:T(1024)(128)(4,1)}), s8[4194304]{0:T(1024)(128)(4,1)S(1)}, s32[]{:S(2)}) async-start(s8[9437184]{0:T(1024)(128)(4,1)} %bitcast.75), calls=%async_computation.6 | async-start | bytes 8388608
  56.9 2.8 %slice-start.5 = ((s8[9437184]{0:T(1024)(128)(4,1)}), s8[1048576]{0:T(1024)(128)(4,1)S(1)}, s32[]{:S(2)}) async-start(s8[9437184]{0:T(1024)(128)(4,1)} %bitcast.75), calls=%async_computation.7 | async-start | bytes 2097152
  62.3 5.2 %copy-start.4 = (f32[16,4]{0,1:T(4,128)S(1)}, f32[16,4]{0,1:T(4,128)}, u32[]{:S(2)}) copy-start(f32[16,4]{0,1:T(4,128)} %param.20) | copy-start | bytes 772
  62.3 41.5 %all-to-all-start.1 = ((bf16[16,8,6144]{2,1,0:T(8,128)(2,1)}), bf16[16,8,6144]{2,1,0:T(8,128)(2,1)}, u32[]{:S(2)}, u32[]{:S(2)}) async-start(bf16[16,8,6144]{2,1,0:T(8,128)(2,1)} %fusion.6), calls=%async_computation.1 | async-start | bytes 3145728 | tf_op jit(solution)/shard_map/all_to_all | solution.py:94
where the time goes:
time: 107 us
  blocking collectives  42.7 us (40%)
  waiting for transfers between devices  36.2 us (34%)
  matrix products  15 us (14%)
  starting transfers between devices  5.18 us (5%)
  other arithmetic  3.71 us (3%)
  local copies, waits for them, and re-layouts  3.69 us (3%)
    all_to_all x1, blocking collectives, body(): lax.all_to_all(fanned, ('attn', 'expert'), split_axis=0, concat_axis=0, t...  42.7 us
    all_to_all x1, waiting for transfers between devices, body(): lax.all_to_all(partial_value.reshape(peer_count * experts_here, cap_slots...  36.2 us
    dot_general x1, matrix products, body(): gate_act = jnp.dot(flat_rows, w_gate[0], preferred_element_type=jnp.float32)  5.28 us
    all_to_all x1, starting transfers between devices, body(): lax.all_to_all(partial_value.reshape(peer_count * experts_here, cap_slots...  5.18 us
    dot_general x1, matrix products, body(): jnp.einsum('rgjd,rpgd->rgjp', query_heads, key_cache, preferred_element_t...  2.87 us
    dot_general x1, matrix products, body(): result = jnp.dot(hidden_act, w_down[0], preferred_element_type=jnp.float32)  2.67 us
  transfers between devices with their start and end apart: 1, of which 1 were waited for; matrix products, arithmetic and copies ran while one was open for 0% of the time, Pallas kernels for 0%

commit v1 on v0

--- a/solution.py
+++ b/solution.py
@@ -6,6 +6,12 @@
 from jax.sharding import PartitionSpec as P
 
 HEAD = 128
+
+
+def ring_of(count):
+    if count == 8:
+        return [0, 2, 4, 6, 7, 5, 3, 1]
+    return list(range(count))
 
 
 def body(
@@ -66,12 +72,14 @@
     variance = jnp.mean(centered * centered, -1, keepdims=True)
     normed = (centered * lax.rsqrt(variance + 1e-05)).astype(jnp.bfloat16)
     mix_weights = gate_probs / jnp.sum(gate_probs, -1, keepdims=True)
-    experts_here = lax.axis_size("expert")
-    labels = jnp.arange(experts_here, dtype=jnp.int32)
+
+    here = lax.axis_index("expert")
+    labels = jnp.stack([here, 1 - here]).astype(jnp.int32)
     matches = expert_ids[None, :, :] == labels[:, None, None]
     coefficient = jnp.sum(jnp.where(matches, mix_weights[None], 0.0), -1)
     chosen = jnp.any(matches, -1)
-    slot_rank = jnp.cumsum(chosen.astype(jnp.int32), 1) - 1
+    earlier = jnp.arange(row_count)[:, None] > jnp.arange(row_count)[None, :]
+    slot_rank = jnp.sum(jnp.where(earlier[None], chosen[:, None, :], False).astype(jnp.int32), -1)
     cap_slots = row_count // 2
     selector = (
         slot_rank[:, None, :] == jnp.arange(cap_slots, dtype=jnp.int32)[None, :, None]
@@ -79,28 +87,77 @@
     outgoing = jnp.einsum(
         "ejr,rd->ejd", selector.astype(jnp.bfloat16), normed, preferred_element_type=jnp.float32
     ).astype(jnp.bfloat16)
-    peer_count = lax.axis_size("attn")
-    fanned = jnp.broadcast_to(outgoing[None], (peer_count,) + outgoing.shape).reshape(
-        peer_count * experts_here, cap_slots, feat_width
+
+    count = lax.axis_size("attn")
+    ring = ring_of(count)
+    right = [(ring[i], ring[(i + 1) % count]) for i in range(count)]
+    left = [(b, a) for a, b in right]
+    swap = [(0, 1), (1, 0)]
+
+    def go_right(block):
+        return lax.ppermute(block, "attn", right)
+
+    def go_left(block):
+        return lax.ppermute(block, "attn", left)
+
+    half = count // 2
+    own = outgoing[0]
+    theirs = lax.ppermute(outgoing[1], "expert", swap)
+    own_r, own_l, theirs_r, theirs_l = [own], [own], [theirs], [theirs]
+    for step in range(1, half + 1):
+        own_r.append(go_right(own_r[-1]))
+        theirs_l.append(go_left(theirs_l[-1]))
+        if step < half:
+            own_l.append(go_left(own_l[-1]))
+            theirs_r.append(go_right(theirs_r[-1]))
+
+    def experts(rows):
+        gate_act = jnp.dot(rows, w_gate[0], preferred_element_type=jnp.float32)
+        upward = jnp.dot(rows, w_up[0], preferred_element_type=jnp.float32)
+        hidden_act = (jax.nn.silu(gate_act) * upward).astype(jnp.bfloat16)
+        return jnp.dot(hidden_act, w_down[0], preferred_element_type=jnp.float32)
+
+    blocks = [own, theirs]
+    for step in range(1, half):
+        blocks += [own_r[step], own_l[step], theirs_r[step], theirs_l[step]]
+    blocks += [own_r[half], theirs_l[half]]
+    share = experts(jnp.concatenate(blocks)).reshape(len(blocks), cap_slots, feat_width)
+    own_share = {0: share[0], half: share[-2]}
+    theirs_share = {0: share[1], -half: share[-1]}
+    for step in range(1, half):
+        at = 4 * step - 2
+        own_share[-step], own_share[step] = share[at], share[at + 1]
+        theirs_share[-step], theirs_share[step] = share[at + 2], share[at + 3]
+
+    def narrow(block):
+        return block.astype(jnp.bfloat16)
+
+    own_from_l = narrow(own_share[half])
+    theirs_from_r = narrow(theirs_share[-half])
+    own_from_r = narrow(own_share[1 - half])
+    theirs_from_l = narrow(theirs_share[half - 1])
+    for step in range(half - 1, 0, -1):
+        own_from_l = narrow(go_right(own_from_l).astype(jnp.float32) + own_share[step])
+        theirs_from_r = narrow(go_left(theirs_from_r).astype(jnp.float32) + theirs_share[-step])
+        if step > 1:
+            own_from_r = narrow(
+                go_left(own_from_r).astype(jnp.float32) + own_share[1 - step]
+            )
+            theirs_from_l = narrow(
+                go_right(theirs_from_l).astype(jnp.float32) + theirs_share[step - 1]
+            )
+    own_total = (
+        own_share[0]
+        + go_right(own_from_l).astype(jnp.float32)
+        + go_left(own_from_r).astype(jnp.float32)
     )
-    arrived = lax.all_to_all(fanned, ("attn", "expert"), split_axis=0, concat_axis=0, tiled=True)
-    piece_rows = arrived.reshape(peer_count, experts_here, cap_slots, feat_width)
-    flat_rows = piece_rows.reshape(-1, feat_width)
-    gate_act = jnp.dot(flat_rows, w_gate[0], preferred_element_type=jnp.float32)
-    upward = jnp.dot(flat_rows, w_up[0], preferred_element_type=jnp.float32)
-    hidden_act = (jax.nn.silu(gate_act) * upward).astype(jnp.bfloat16)
-    result = jnp.dot(hidden_act, w_down[0], preferred_element_type=jnp.float32)
-    partial_value = result.reshape(piece_rows.shape[:-1] + (feat_width,))
-    arrived_back = lax.all_to_all(
-        partial_value.reshape(peer_count * experts_here, cap_slots, feat_width).astype(
-            jnp.bfloat16
-        ),
-        ("attn", "expert"),
-        split_axis=0,
-        concat_axis=0,
-        tiled=True,
-    ).astype(jnp.float32)
-    returned = jnp.sum(arrived_back.reshape(peer_count, experts_here, cap_slots, feat_width), 0)
+    theirs_total = (
+        theirs_share[0]
+        + go_left(theirs_from_r).astype(jnp.float32)
+        + go_right(theirs_from_l).astype(jnp.float32)
+    )
+    back = lax.ppermute(narrow(theirs_total), "expert", swap).astype(jnp.float32)
+    returned = jnp.stack([own_total, back])
     weighted = selector.astype(jnp.float32) * coefficient[:, None, :]
     expert_sum = jnp.einsum("ejr,ejd->rd", weighted, returned, precision=lax.Precision.HIGHEST)
     return residual + expert_sum

time: 107 us -> 95.8 us (0.90)
  the two profiles are of different devices: /device:TPU:13 before, /device:TPU:0 now
where the time goes in v1:
time: 95.8 us; the launch traced here: 95.3 us
  starting transfers between devices  29.8 us (31%)
  waiting for transfers between devices  29.7 us (31%)
  matrix products  23.2 us (24%)
  other arithmetic  7.76 us (8%)
  local copies, waits for them, and re-layouts  4.52 us (5%)
    ppermute x14, starting transfers between devices, go_right(): return lax.ppermute(block, 'attn', right)  26 us
    ppermute x14, waiting for transfers between devices, go_left(): return lax.ppermute(block, 'attn', left)  15.8 us
    dot_general x1, matrix products, experts(): return jnp.dot(hidden_act, w_down[0], preferred_element_type=jnp.float32)  12.5 us
    ppermute x14, waiting for transfers between devices, go_right(): return lax.ppermute(block, 'attn', right)  11.4 us
    dot_general x1, matrix products, experts(): upward = jnp.dot(rows, w_up[0], preferred_element_type=jnp.float32)  5.11 us
    convert_element_type x4, other arithmetic, narrow(): return block.astype(jnp.bfloat16)  4.4 us
    ppermute x14, starting transfers between devices, go_left(): return lax.ppermute(block, 'attn', left)  3.75 us
    dot_general x1, matrix products, body(): jnp.einsum('rgjd,rpgd->rgjp', query_heads, key_cache, preferred_element_t...  2.87 us
  transfers between devices with their start and end apart: 30, of which 16 were waited for; matrix products, arithmetic and copies ran while one was open for 2% of the time, Pallas kernels for 0%

profile of v1, /device:TPU:0, one launch (start us, length us, event | category | flops | bytes accessed | tf_op | source)
XLA Modules:
  0.0 95.3 jit_solution(71937507768703940)
XLA Ops:
  0.9 1.2 %reshape.101 = bf16[16,8,6,128]{3,2,1,0:T(8,128)(2,1)S(1)} reshape(bf16[16,6144]{1,0:T(8,128)(2,1)} %param.13) | data formatting | bytes 393216 | tf_op jit(solution)/shard_map/reshape | solution.py:38
  3.2 2.9 %fusion.72 = (f32[16,8,6]{2,1,0:T(8,128)S(1)}, f32[16,8,6,64]{3,2,1,0:T(8,128)S(1)}) fusion(bf16[16,8,6,128]{3,2,1,0:T(8,128)(2,1)S(1)} %reshape.101, pred[16,64]{1,0:T(8,128)(4,1)S(1)} %iota_compare_fusion.2, bf16[16,64,1024]{2,1,0:T(8,128)(2,1)} %param.14), kind=kOutput, calls=%fused_computation.112 | convolution fusion | flops 12729600 | bytes 2494464 | tf_op jit(solution)/shard_map/rgjd,rpgd->rgjp/dot_general | solution.py:42
  8.7 3.1 %collective-permute-start.1 = (bf16[8,6144]{1,0:T(8,128)(2,1)S(1)}, bf16[8,6144]{1,0:T(8,128)(2,1)S(1)}, u32[]{:S(2)}, u32[]{:S(2)}) collective-permute-start(bf16[8,6144]{1,0:T(8,128)(2,1)S(1)} %get-tuple-element.19), channel_id=1, source_target_pairs={{0,4},{4,8},{8,12},{12,14},{14,10},{10,6},{6,2},{2,0},{1,5},{5,9},... | collective-permute-start | bytes 294920 | tf_op jit(solution)/shard_map/ppermute | solution.py:98
  11.8 1.3 %collective-permute-done = bf16[8,6144]{1,0:T(8,128)(2,1)S(1)} collective-permute-done((bf16[8,6144]{1,0:T(8,128)(2,1)S(1)}, bf16[8,6144]{1,0:T(8,128)(2,1)S(1)}, u32[]{:S(2)}, u32[]{:S(2)}) %collective-permute-start) | collective-permute-done | bytes 98336 | tf_op jit(solution)/shard_map/ppermute | solution.py:105
  13.1 2.0 %collective-permute-start.3 = (bf16[8,6144]{1,0:T(8,128)(2,1)S(1)}, bf16[8,6144]{1,0:T(8,128)(2,1)S(1)}, u32[]{:S(2)}, u32[]{:S(2)}) collective-permute-start(bf16[8,6144]{1,0:T(8,128)(2,1)S(1)} %collective-permute-done), channel_id=1, source_target_pairs={{0,4},{4,8},{8,12},{12,14},{14,10},{10,6},{6,2},{2,0},{1,5},{5,9},... | collective-permute-start | bytes 294920 | tf_op jit(solution)/shard_map/ppermute | solution.py:98
  15.1 2.1 %collective-permute-start.5 = (bf16[8,6144]{1,0:T(8,128)(2,1)S(1)}, bf16[8,6144]{1,0:T(8,128)(2,1)S(1)}, u32[]{:S(2)}, u32[]{:S(2)}) collective-permute-start(bf16[8,6144]{1,0:T(8,128)(2,1)S(1)} %collective-permute-done.1), channel_id=1, source_target_pairs={{0,4},{4,8},{8,12},{12,14},{14,10},{10,6},{6,2},{2,0},{1,5},{5,9},... | collective-permute-start | bytes 294920 | tf_op jit(solution)/shard_map/ppermute | solution.py:98
  17.3 1.4 %collective-permute-done.3 = bf16[8,6144]{1,0:T(8,128)(2,1)S(1)} collective-permute-done((bf16[8,6144]{1,0:T(8,128)(2,1)S(1)}, bf16[8,6144]{1,0:T(8,128)(2,1)S(1)}, u32[]{:S(2)}, u32[]{:S(2)}) %collective-permute-start.3) | collective-permute-done | bytes 98336 | tf_op jit(solution)/shard_map/ppermute | solution.py:98
  18.7 1.9 %collective-permute-start.7 = (bf16[8,6144]{1,0:T(8,128)(2,1)S(1)}, bf16[8,6144]{1,0:T(8,128)(2,1)S(1)}, u32[]{:S(2)}, u32[]{:S(2)}) collective-permute-start(bf16[8,6144]{1,0:T(8,128)(2,1)S(1)} %collective-permute-done.3), channel_id=1, source_target_pairs={{0,4},{4,8},{8,12},{12,14},{14,10},{10,6},{6,2},{2,0},{1,5},{5,9},... | collective-permute-start | bytes 294920 | tf_op jit(solution)/shard_map/ppermute | solution.py:98
  20.8 2.0 %collective-permute-start.9 = (bf16[8,6144]{1,0:T(8,128)(2,1)S(1)}, bf16[8,6144]{1,0:T(8,128)(2,1)S(1)}, u32[]{:S(2)}, u32[]{:S(2)}) collective-permute-start(bf16[8,6144]{1,0:T(8,128)(2,1)S(1)} %collective-permute-done.5), channel_id=1, source_target_pairs={{0,4},{4,8},{8,12},{12,14},{14,10},{10,6},{6,2},{2,0},{1,5},{5,9},... | collective-permute-start | bytes 294920 | tf_op jit(solution)/shard_map/ppermute | solution.py:98
  23.0 1.2 %collective-permute-done.7 = bf16[8,6144]{1,0:T(8,128)(2,1)S(1)} collective-permute-done((bf16[8,6144]{1,0:T(8,128)(2,1)S(1)}, bf16[8,6144]{1,0:T(8,128)(2,1)S(1)}, u32[]{:S(2)}, u32[]{:S(2)}) %collective-permute-start.7) | collective-permute-done | bytes 98336 | tf_op jit(solution)/shard_map/ppermute | solution.py:98
  24.2 2.0 %collective-permute-start.11 = (bf16[8,6144]{1,0:T(8,128)(2,1)S(1)}, bf16[8,6144]{1,0:T(8,128)(2,1)S(1)}, u32[]{:S(2)}, u32[]{:S(2)}) collective-permute-start(bf16[8,6144]{1,0:T(8,128)(2,1)S(1)} %collective-permute-done.7), channel_id=1, source_target_pairs={{0,4},{4,8},{8,12},{12,14},{14,10},{10,6},{6,2},{2,0},{1,5},{5,9},... | collective-permute-start | bytes 294920 | tf_op jit(solution)/shard_map/ppermute | solution.py:98
  26.5 1.9 %collective-permute-start.13 = (bf16[8,6144]{1,0:T(8,128)(2,1)S(1)}, bf16[8,6144]{1,0:T(8,128)(2,1)S(1)}, u32[]{:S(2)}, u32[]{:S(2)}) collective-permute-start(bf16[8,6144]{1,0:T(8,128)(2,1)S(1)} %collective-permute-done.9), channel_id=1, source_target_pairs={{0,4},{4,8},{8,12},{12,14},{14,10},{10,6},{6,2},{2,0},{1,5},{5,9},... | collective-permute-start | bytes 294920 | tf_op jit(solution)/shard_map/ppermute | solution.py:98
  28.4 3.2 %collective-permute-done.12 = bf16[8,6144]{1,0:T(8,128)(2,1)S(1)} collective-permute-done((bf16[8,6144]{1,0:T(8,128)(2,1)S(1)}, bf16[8,6144]{1,0:T(8,128)(2,1)S(1)}, u32[]{:S(2)}, u32[]{:S(2)}) %collective-permute-start.12) | collective-permute-done | bytes 98336 | tf_op jit(solution)/shard_map/ppermute | solution.py:101
  31.6 4.6 %collective-permute-done.14 = bf16[8,6144]{1,0:T(8,128)(2,1)S(1)} collective-permute-done((bf16[8,6144]{1,0:T(8,128)(2,1)S(1)}, bf16[8,6144]{1,0:T(8,128)(2,1)S(1)}, u32[]{:S(2)}, u32[]{:S(2)}) %collective-permute-start.14) | collective-permute-done | bytes 98336 | tf_op jit(solution)/shard_map/ppermute | solution.py:101
  37.4 5.1 %fusion.2 = f32[128,768]{1,0:T(8,128)S(1)} fusion(bf16[128,6144]{1,0:T(8,128)(2,1)S(1)} %constant_dynamic-update-slice_fusion, bf16[1,6144,768]{2,1,0:T(8,128)(2,1)} %param.22), kind=kOutput, calls=%fused_computation.2 | convolution fusion | flops 1207959552 | bytes 11403264 | tf_op jit(solution)/shard_map/dot_general | solution.py:116
  42.5 12.5 %fusion.73 = (bf16[128,6144]{1,0:T(8,128)(2,1)}, f32[128,6144]{1,0:T(8,128)}) fusion(bf16[1,768,6144]{2,1,0:T(8,128)(2,1)} %param.23, f32[128,768]{1,0:T(8,128)S(1)} %fusion.2, bf16[128,6144]{1,0:T(8,128)(2,1)} %copy-done.1, bf16[1,6144,768]{2,1,0:T(8,128)(2,1)} %param.21), kind=kOutput, calls=%fused_computation.113 | convolution fusion | flops 2417295360 | bytes 25559040 | tf_op jit(solution)/shard_map/dot_general | solution.py:118
  56.1 1.6 %collective-permute-start.15 = (bf16[8,6144]{1,0:T(8,128)(2,1)S(1)}, bf16[8,6144]{1,0:T(8,128)(2,1)S(1)}, u32[]{:S(2)}, u32[]{:S(2)}) collective-permute-start(bf16[8,6144]{1,0:T(8,128)(2,1)S(1)} %get-tuple-element.15), channel_id=1, source_target_pairs={{0,4},{4,8},{8,12},{12,14},{14,10},{10,6},{6,2},{2,0},{1,5},{5,9},... | collective-permute-start | bytes 294920 | tf_op jit(solution)/shard_map/ppermute | solution.py:98
  58.4 3.2 %collective-permute-done.15 = bf16[8,6144]{1,0:T(8,128)(2,1)S(1)} collective-permute-done((bf16[8,6144]{1,0:T(8,128)(2,1)S(1)}, bf16[8,6144]{1,0:T(8,128)(2,1)S(1)}, u32[]{:S(2)}, u32[]{:S(2)}) %collective-permute-start.15) | collective-permute-done | bytes 98336 | tf_op jit(solution)/shard_map/ppermute | solution.py:98
  62.6 1.6 %collective-permute-start.16 = (bf16[8,6144]{1,0:T(8,128)(2,1)S(1)}, bf16[8,6144]{1,0:T(8,128)(2,1)S(1)}, u32[]{:S(2)}, u32[]{:S(2)}) collective-permute-start(bf16[8,6144]{1,0:T(8,128)(2,1)S(1)} %fusion.47), channel_id=1, source_target_pairs={{0,4},{4,8},{8,12},{12,14},{14,10},{10,6},{6,2},{2,0},{1,5},{5,9},... | collective-permute-start | bytes 294920 | tf_op jit(solution)/shard_map/ppermute | solution.py:98
  64.2 1.5 %collective-permute-start.26 = (bf16[8,6144]{1,0:T(8,128)(2,1)S(1)}, bf16[8,6144]{1,0:T(8,128)(2,1)S(1)}, u32[]{:S(2)}, u32[]{:S(2)}) collective-permute-start(bf16[8,6144]{1,0:T(8,128)(2,1)S(1)} %get-tuple-element.16), channel_id=1, source_target_pairs={{0,4},{4,8},{8,12},{12,14},{14,10},{10,6},{6,2},{2,0},{1,5},{5,9},... | collective-permute-start | bytes 294920 | tf_op jit(solution)/shard_map/ppermute | solution.py:98
  65.8 1.5 %collective-permute-done.16 = bf16[8,6144]{1,0:T(8,128)(2,1)S(1)} collective-permute-done((bf16[8,6144]{1,0:T(8,128)(2,1)S(1)}, bf16[8,6144]{1,0:T(8,128)(2,1)S(1)}, u32[]{:S(2)}, u32[]{:S(2)}) %collective-permute-start.16) | collective-permute-done | bytes 98336 | tf_op jit(solution)/shard_map/ppermute | solution.py:98
  68.5 1.6 %collective-permute-start.17 = (bf16[8,6144]{1,0:T(8,128)(2,1)S(1)}, bf16[8,6144]{1,0:T(8,128)(2,1)S(1)}, u32[]{:S(2)}, u32[]{:S(2)}) collective-permute-start(bf16[8,6144]{1,0:T(8,128)(2,1)S(1)} %get-tuple-element.12), channel_id=1, source_target_pairs={{0,4},{4,8},{8,12},{12,14},{14,10},{10,6},{6,2},{2,0},{1,5},{5,9},... | collective-permute-start | bytes 294920 | tf_op jit(solution)/shard_map/ppermute | solution.py:98
  70.9 3.1 %collective-permute-done.17 = bf16[8,6144]{1,0:T(8,128)(2,1)S(1)} collective-permute-done((bf16[8,6144]{1,0:T(8,128)(2,1)S(1)}, bf16[8,6144]{1,0:T(8,128)(2,1)S(1)}, u32[]{:S(2)}, u32[]{:S(2)}) %collective-permute-start.17) | collective-permute-done | bytes 98336 | tf_op jit(solution)/shard_map/ppermute | solution.py:98
  74.0 1.8 %collective-permute-done.20 = bf16[8,6144]{1,0:T(8,128)(2,1)S(1)} collective-permute-done((bf16[8,6144]{1,0:T(8,128)(2,1)S(1)}, bf16[8,6144]{1,0:T(8,128)(2,1)S(1)}, u32[]{:S(2)}, u32[]{:S(2)}) %collective-permute-start.20) | collective-permute-done | bytes 98336 | tf_op jit(solution)/shard_map/ppermute | solution.py:101
  76.8 1.3 %fusion.45 = (bf16[8,6144]{1,0:T(8,128)(2,1)S(1)}, bf16[8,6144]{1,0:T(8,128)(2,1)S(1)}, bf16[8,6144]{1,0:T(8,128)(2,1)S(1)}, bf16[8,6144]{1,0:T(8,128)(2,1)S(1)}) fusion(f32[128,6144]{1,0:T(8,128)} %get-tuple-element.26, bf16[8,6144]{1,0:T(8,128)(2,1)S(1)} %collective-permute-done.17, bf16[8,6144]{1,0:T(8,128)(2,1)S(1)} %collective-permute-done.26, ...), kind=kLoop, calls=%fused_computation.51 | loop fusion | flops 589824 | bytes 1572864 | tf_op jit(solution)/shard_map/convert_element_type | solution.py:133
  78.1 1.6 %collective-permute-start.18 = (bf16[8,6144]{1,0:T(8,128)(2,1)S(1)}, bf16[8,6144]{1,0:T(8,128)(2,1)S(1)}, u32[]{:S(2)}, u32[]{:S(2)}) collective-permute-start(bf16[8,6144]{1,0:T(8,128)(2,1)S(1)} %get-tuple-element.8), channel_id=1, source_target_pairs={{0,4},{4,8},{8,12},{12,14},{14,10},{10,6},{6,2},{2,0},{1,5},{5,9},... | collective-permute-start | bytes 294920 | tf_op jit(solution)/shard_map/ppermute | solution.py:98
  80.6 1.6 %collective-permute-start.27 = (bf16[8,6144]{1,0:T(8,128)(2,1)S(1)}, bf16[8,6144]{1,0:T(8,128)(2,1)S(1)}, u32[]{:S(2)}, u32[]{:S(2)}) collective-permute-start(bf16[8,6144]{1,0:T(8,128)(2,1)S(1)} %get-tuple-element.9), channel_id=1, source_target_pairs={{0,4},{4,8},{8,12},{12,14},{14,10},{10,6},{6,2},{2,0},{1,5},{5,9},... | collective-permute-start | bytes 294920 | tf_op jit(solution)/shard_map/ppermute | solution.py:98
  82.8 1.5 %collective-permute-done.21 = bf16[8,6144]{1,0:T(8,128)(2,1)S(1)} collective-permute-done((bf16[8,6144]{1,0:T(8,128)(2,1)S(1)}, bf16[8,6144]{1,0:T(8,128)(2,1)S(1)}, u32[]{:S(2)}, u32[]{:S(2)}) %collective-permute-start.21) | collective-permute-done | bytes 98336 | tf_op jit(solution)/shard_map/ppermute | solution.py:101
  87.1 1.5 %collective-permute-start.28 = (bf16[8,6144]{1,0:T(8,128)(2,1)S(1)}, bf16[8,6144]{1,0:T(8,128)(2,1)S(1)}, u32[]{:S(2)}, u32[]{:S(2)}) collective-permute-start(bf16[8,6144]{1,0:T(8,128)(2,1)S(1)} %get-tuple-element.6), channel_id=1, source_target_pairs={{0,4},{4,8},{8,12},{12,14},{14,10},{10,6},{6,2},{2,0},{1,5},{5,9},... | collective-permute-start | bytes 294920 | tf_op jit(solution)/shard_map/ppermute | solution.py:98
  88.6 2.6 %collective-permute-done.25 = bf16[8,6144]{1,0:T(8,128)(2,1)S(1)} collective-permute-done((bf16[8,6144]{1,0:T(8,128)(2,1)S(1)}, bf16[8,6144]{1,0:T(8,128)(2,1)S(1)}, u32[]{:S(2)}, u32[]{:S(2)}) %collective-permute-start.25) | collective-permute-done | bytes 98336 | tf_op jit(solution)/shard_map/ppermute | solution.py:101
  92.8 1.2 %collective-permute-done.29 = bf16[8,6144]{1,0:T(8,128)(2,1)S(1)} collective-permute-done((bf16[8,6144]{1,0:T(8,128)(2,1)S(1)}, bf16[8,6144]{1,0:T(8,128)(2,1)S(1)}, u32[]{:S(2)}, u32[]{:S(2)}) %collective-permute-start.29) | collective-permute-done | bytes 98336 | tf_op jit(solution)/shard_map/ppermute | solution.py:159
  94.1 1.3 %fusion.6 = f32[16,6144]{1,0:T(8,128)} fusion(f32[1,8,6144]{2,1,0:T(8,128)S(1)} %bitcast_convert_fusion, f32[1,8,6144]{2,1,0:T(8,128)S(1)} %get-tuple-element.5, f32[16,6144]{1,0:T(8,128)S(1)} %reshape.105, bf16[16,6144]{1,0:T(8,128)(2,1)S(1)} %copy-done.2, f32[2,16]{1,0:T(2,128)S(1)} %fusion.60, s32[2,16]{1,0:T(2,128)S(1)} %convert_reduce_fusion, ...), kind=kOutput, calls=%fused_computation.7 | convolution fusion | flops 19268352 | bytes 1376544 | tf_op jit(solution)/shard_map/ejr,ejd->rd/dot_general | solution.py:162
  (91 shorter events, 18.3 us)
Async XLA Ops:
  0.0 6.6 %copy-start = (bf16[16,64,1024]{2,1,0:T(8,128)(2,1)S(1)}, bf16[16,64,1024]{2,1,0:T(8,128)(2,1)}, u32[]{:S(2)}) copy-start(bf16[16,64,1024]{2,1,0:T(8,128)(2,1)} %param.15) | copy-start | bytes 6291460
  8.7 6.4 %collective-permute-start.1 = (bf16[8,6144]{1,0:T(8,128)(2,1)S(1)}, bf16[8,6144]{1,0:T(8,128)(2,1)S(1)}, u32[]{:S(2)}, u32[]{:S(2)}) collective-permute-start(bf16[8,6144]{1,0:T(8,128)(2,1)S(1)} %get-tuple-element.19), channel_id=1, source_target_pairs={{0,4},{4,8},{8,12},{12,14},{14,10},{10,6},{6,2},{2,0},{1,5},{5,9},... | collective-permute-start | bytes 294920 | tf_op jit(solution)/shard_map/ppermute | solution.py:98
  11.8 5.4 %collective-permute-start.2 = (bf16[8,6144]{1,0:T(8,128)(2,1)S(1)}, bf16[8,6144]{1,0:T(8,128)(2,1)S(1)}, u32[]{:S(2)}, u32[]{:S(2)}) collective-permute-start(bf16[8,6144]{1,0:T(8,128)(2,1)S(1)} %get-tuple-element.19), channel_id=1, source_target_pairs={{4,0},{8,4},{12,8},{14,12},{10,14},{6,10},{2,6},{0,2},{5,1},{9,5},... | collective-permute-start | bytes 294920 | tf_op jit(solution)/shard_map/ppermute | solution.py:101
  11.8 1.3 %collective-permute-start = (bf16[8,6144]{1,0:T(8,128)(2,1)S(1)}, bf16[8,6144]{1,0:T(8,128)(2,1)S(1)}, u32[]{:S(2)}, u32[]{:S(2)}) collective-permute-start(bf16[8,6144]{1,0:T(8,128)(2,1)S(1)} %get-tuple-element.20), channel_id=1, source_target_pairs={{0,1},{1,0},{2,3},{3,2},{4,5},{5,4},{6,7},{7,6},{8,9},{9,8},{10,11... | collective-permute-start | bytes 294920 | tf_op jit(solution)/shard_map/ppermute | solution.py:105
  13.1 5.6 %collective-permute-start.3 = (bf16[8,6144]{1,0:T(8,128)(2,1)S(1)}, bf16[8,6144]{1,0:T(8,128)(2,1)S(1)}, u32[]{:S(2)}, u32[]{:S(2)}) collective-permute-start(bf16[8,6144]{1,0:T(8,128)(2,1)S(1)} %collective-permute-done), channel_id=1, source_target_pairs={{0,4},{4,8},{8,12},{12,14},{14,10},{10,6},{6,2},{2,0},{1,5},{5,9},... | collective-permute-start | bytes 294920 | tf_op jit(solution)/shard_map/ppermute | solution.py:98
  15.1 5.5 %collective-permute-start.4 = (bf16[8,6144]{1,0:T(8,128)(2,1)S(1)}, bf16[8,6144]{1,0:T(8,128)(2,1)S(1)}, u32[]{:S(2)}, u32[]{:S(2)}) collective-permute-start(bf16[8,6144]{1,0:T(8,128)(2,1)S(1)} %collective-permute-done), channel_id=1, source_target_pairs={{4,0},{8,4},{12,8},{14,12},{10,14},{6,10},{2,6},{0,2},{5,1},{9,5},... | collective-permute-start | bytes 294920 | tf_op jit(solution)/shard_map/ppermute | solution.py:101
  15.1 5.6 %collective-permute-start.5 = (bf16[8,6144]{1,0:T(8,128)(2,1)S(1)}, bf16[8,6144]{1,0:T(8,128)(2,1)S(1)}, u32[]{:S(2)}, u32[]{:S(2)}) collective-permute-start(bf16[8,6144]{1,0:T(8,128)(2,1)S(1)} %collective-permute-done.1), channel_id=1, source_target_pairs={{0,4},{4,8},{8,12},{12,14},{14,10},{10,6},{6,2},{2,0},{1,5},{5,9},... | collective-permute-start | bytes 294920 | tf_op jit(solution)/shard_map/ppermute | solution.py:98
  17.2 5.5 %collective-permute-start.6 = (bf16[8,6144]{1,0:T(8,128)(2,1)S(1)}, bf16[8,6144]{1,0:T(8,128)(2,1)S(1)}, u32[]{:S(2)}, u32[]{:S(2)}) collective-permute-start(bf16[8,6144]{1,0:T(8,128)(2,1)S(1)} %collective-permute-done.2), channel_id=1, source_target_pairs={{4,0},{8,4},{12,8},{14,12},{10,14},{6,10},{2,6},{0,2},{5,1},{9,5},... | collective-permute-start | bytes 294920 | tf_op jit(solution)/shard_map/ppermute | solution.py:101
  18.7 5.5 %collective-permute-start.7 = (bf16[8,6144]{1,0:T(8,128)(2,1)S(1)}, bf16[8,6144]{1,0:T(8,128)(2,1)S(1)}, u32[]{:S(2)}, u32[]{:S(2)}) collective-permute-start(bf16[8,6144]{1,0:T(8,128)(2,1)S(1)} %collective-permute-done.3), channel_id=1, source_target_pairs={{0,4},{4,8},{8,12},{12,14},{14,10},{10,6},{6,2},{2,0},{1,5},{5,9},... | collective-permute-start | bytes 294920 | tf_op jit(solution)/shard_map/ppermute | solution.py:98
  20.6 5.6 %collective-permute-start.8 = (bf16[8,6144]{1,0:T(8,128)(2,1)S(1)}, bf16[8,6144]{1,0:T(8,128)(2,1)S(1)}, u32[]{:S(2)}, u32[]{:S(2)}) collective-permute-start(bf16[8,6144]{1,0:T(8,128)(2,1)S(1)} %collective-permute-done.4), channel_id=1, source_target_pairs={{4,0},{8,4},{12,8},{14,12},{10,14},{6,10},{2,6},{0,2},{5,1},{9,5},... | collective-permute-start | bytes 294920 | tf_op jit(solution)/shard_map/ppermute | solution.py:101
  20.8 5.7 %collective-permute-start.9 = (bf16[8,6144]{1,0:T(8,128)(2,1)S(1)}, bf16[8,6144]{1,0:T(8,128)(2,1)S(1)}, u32[]{:S(2)}, u32[]{:S(2)}) collective-permute-start(bf16[8,6144]{1,0:T(8,128)(2,1)S(1)} %collective-permute-done.5), channel_id=1, source_target_pairs={{0,4},{4,8},{8,12},{12,14},{14,10},{10,6},{6,2},{2,0},{1,5},{5,9},... | collective-permute-start | bytes 294920 | tf_op jit(solution)/shard_map/ppermute | solution.py:98
  22.8 5.6 %collective-permute-start.10 = (bf16[8,6144]{1,0:T(8,128)(2,1)S(1)}, bf16[8,6144]{1,0:T(8,128)(2,1)S(1)}, u32[]{:S(2)}, u32[]{:S(2)}) collective-permute-start(bf16[8,6144]{1,0:T(8,128)(2,1)S(1)} %collective-permute-done.6), channel_id=1, source_target_pairs={{4,0},{8,4},{12,8},{14,12},{10,14},{6,10},{2,6},{0,2},{5,1},{9,5},... | collective-permute-start | bytes 294920 | tf_op jit(solution)/shard_map/ppermute | solution.py:101
  24.2 7.4 %collective-permute-start.11 = (bf16[8,6144]{1,0:T(8,128)(2,1)S(1)}, bf16[8,6144]{1,0:T(8,128)(2,1)S(1)}, u32[]{:S(2)}, u32[]{:S(2)}) collective-permute-start(bf16[8,6144]{1,0:T(8,128)(2,1)S(1)} %collective-permute-done.7), channel_id=1, source_target_pairs={{0,4},{4,8},{8,12},{12,14},{14,10},{10,6},{6,2},{2,0},{1,5},{5,9},... | collective-permute-start | bytes 294920 | tf_op jit(solution)/shard_map/ppermute | solution.py:98
  26.2 5.4 %collective-permute-start.12 = (bf16[8,6144]{1,0:T(8,128)(2,1)S(1)}, bf16[8,6144]{1,0:T(8,128)(2,1)S(1)}, u32[]{:S(2)}, u32[]{:S(2)}) collective-permute-start(bf16[8,6144]{1,0:T(8,128)(2,1)S(1)} %collective-permute-done.8), channel_id=1, source_target_pairs={{4,0},{8,4},{12,8},{14,12},{10,14},{6,10},{2,6},{0,2},{5,1},{9,5},... | collective-permute-start | bytes 294920 | tf_op jit(solution)/shard_map/ppermute | solution.py:101
  26.5 5.2 %collective-permute-start.13 = (bf16[8,6144]{1,0:T(8,128)(2,1)S(1)}, bf16[8,6144]{1,0:T(8,128)(2,1)S(1)}, u32[]{:S(2)}, u32[]{:S(2)}) collective-permute-start(bf16[8,6144]{1,0:T(8,128)(2,1)S(1)} %collective-permute-done.9), channel_id=1, source_target_pairs={{0,4},{4,8},{8,12},{12,14},{14,10},{10,6},{6,2},{2,0},{1,5},{5,9},... | collective-permute-start | bytes 294920 | tf_op jit(solution)/shard_map/ppermute | solution.py:98
  31.6 4.6 %collective-permute-start.14 = (bf16[8,6144]{1,0:T(8,128)(2,1)S(1)}, bf16[8,6144]{1,0:T(8,128)(2,1)S(1)}, u32[]{:S(2)}, u32[]{:S(2)}) collective-permute-start(bf16[8,6144]{1,0:T(8,128)(2,1)S(1)} %collective-permute-done.12), channel_id=1, source_target_pairs={{4,0},{8,4},{12,8},{14,12},{10,14},{6,10},{2,6},{0,2},{5,1},{9,5},... | collective-permute-start | bytes 294920 | tf_op jit(solution)/shard_map/ppermute | solution.py:101
  56.1 5.6 %collective-permute-start.15 = (bf16[8,6144]{1,0:T(8,128)(2,1)S(1)}, bf16[8,6144]{1,0:T(8,128)(2,1)S(1)}, u32[]{:S(2)}, u32[]{:S(2)}) collective-permute-start(bf16[8,6144]{1,0:T(8,128)(2,1)S(1)} %get-tuple-element.15), channel_id=1, source_target_pairs={{0,4},{4,8},{8,12},{12,14},{14,10},{10,6},{6,2},{2,0},{1,5},{5,9},... | collective-permute-start | bytes 294920 | tf_op jit(solution)/shard_map/ppermute | solution.py:98
  57.7 8.1 %collective-permute-start.19 = (bf16[8,6144]{1,0:T(8,128)(2,1)S(1)}, bf16[8,6144]{1,0:T(8,128)(2,1)S(1)}, u32[]{:S(2)}, u32[]{:S(2)}) collective-permute-start(bf16[8,6144]{1,0:T(8,128)(2,1)S(1)} %get-tuple-element.18), channel_id=1, source_target_pairs={{4,0},{8,4},{12,8},{14,12},{10,14},{6,10},{2,6},{0,2},{5,1},{9,5},... | collective-permute-start | bytes 294920 | tf_op jit(solution)/shard_map/ppermute | solution.py:101
  58.1 7.6 %collective-permute-start.22 = (bf16[8,6144]{1,0:T(8,128)(2,1)S(1)}, bf16[8,6144]{1,0:T(8,128)(2,1)S(1)}, u32[]{:S(2)}, u32[]{:S(2)}) collective-permute-start(bf16[8,6144]{1,0:T(8,128)(2,1)S(1)} %get-tuple-element.17), channel_id=1, source_target_pairs={{4,0},{8,4},{12,8},{14,12},{10,14},{6,10},{2,6},{0,2},{5,1},{9,5},... | collective-permute-start | bytes 294920 | tf_op jit(solution)/shard_map/ppermute | solution.py:101
  61.6 20.6 %copy-start.4 = (f32[16,4]{0,1:T(4,128)S(1)}, f32[16,4]{0,1:T(4,128)}, u32[]{:S(2)}) copy-start(f32[16,4]{0,1:T(4,128)} %param.20) | copy-start | bytes 772
  62.6 4.7 %collective-permute-start.16 = (bf16[8,6144]{1,0:T(8,128)(2,1)S(1)}, bf16[8,6144]{1,0:T(8,128)(2,1)S(1)}, u32[]{:S(2)}, u32[]{:S(2)}) collective-permute-start(bf16[8,6144]{1,0:T(8,128)(2,1)S(1)} %fusion.47), channel_id=1, source_target_pairs={{0,4},{4,8},{8,12},{12,14},{14,10},{10,6},{6,2},{2,0},{1,5},{5,9},... | collective-permute-start | bytes 294920 | tf_op jit(solution)/shard_map/ppermute | solution.py:98
  64.2 6.7 %collective-permute-start.26 = (bf16[8,6144]{1,0:T(8,128)(2,1)S(1)}, bf16[8,6144]{1,0:T(8,128)(2,1)S(1)}, u32[]{:S(2)}, u32[]{:S(2)}) collective-permute-start(bf16[8,6144]{1,0:T(8,128)(2,1)S(1)} %get-tuple-element.16), channel_id=1, source_target_pairs={{0,4},{4,8},{8,12},{12,14},{14,10},{10,6},{6,2},{2,0},{1,5},{5,9},... | collective-permute-start | bytes 294920 | tf_op jit(solution)/shard_map/ppermute | solution.py:98
  68.5 5.5 %collective-permute-start.17 = (bf16[8,6144]{1,0:T(8,128)(2,1)S(1)}, bf16[8,6144]{1,0:T(8,128)(2,1)S(1)}, u32[]{:S(2)}, u32[]{:S(2)}) collective-permute-start(bf16[8,6144]{1,0:T(8,128)(2,1)S(1)} %get-tuple-element.12), channel_id=1, source_target_pairs={{0,4},{4,8},{8,12},{12,14},{14,10},{10,6},{6,2},{2,0},{1,5},{5,9},... | collective-permute-start | bytes 294920 | tf_op jit(solution)/shard_map/ppermute | solution.py:98
  70.1 5.7 %collective-permute-start.20 = (bf16[8,6144]{1,0:T(8,128)(2,1)S(1)}, bf16[8,6144]{1,0:T(8,128)(2,1)S(1)}, u32[]{:S(2)}, u32[]{:S(2)}) collective-permute-start(bf16[8,6144]{1,0:T(8,128)(2,1)S(1)} %get-tuple-element.14), channel_id=1, source_target_pairs={{4,0},{8,4},{12,8},{14,12},{10,14},{6,10},{2,6},{0,2},{5,1},{9,5},... | collective-permute-start | bytes 294920 | tf_op jit(solution)/shard_map/ppermute | solution.py:101
  70.5 6.3 %collective-permute-start.23 = (bf16[8,6144]{1,0:T(8,128)(2,1)S(1)}, bf16[8,6144]{1,0:T(8,128)(2,1)S(1)}, u32[]{:S(2)}, u32[]{:S(2)}) collective-permute-start(bf16[8,6144]{1,0:T(8,128)(2,1)S(1)} %get-tuple-element.13), channel_id=1, source_target_pairs={{4,0},{8,4},{12,8},{14,12},{10,14},{6,10},{2,6},{0,2},{5,1},{9,5},... | collective-permute-start | bytes 294920 | tf_op jit(solution)/shard_map/ppermute | solution.py:101
  78.1 4.7 %collective-permute-start.18 = (bf16[8,6144]{1,0:T(8,128)(2,1)S(1)}, bf16[8,6144]{1,0:T(8,128)(2,1)S(1)}, u32[]{:S(2)}, u32[]{:S(2)}) collective-permute-start(bf16[8,6144]{1,0:T(8,128)(2,1)S(1)} %get-tuple-element.8), channel_id=1, source_target_pairs={{0,4},{4,8},{8,12},{12,14},{14,10},{10,6},{6,2},{2,0},{1,5},{5,9},... | collective-permute-start | bytes 294920 | tf_op jit(solution)/shard_map/ppermute | solution.py:98
  79.7 4.6 %collective-permute-start.21 = (bf16[8,6144]{1,0:T(8,128)(2,1)S(1)}, bf16[8,6144]{1,0:T(8,128)(2,1)S(1)}, u32[]{:S(2)}, u32[]{:S(2)}) collective-permute-start(bf16[8,6144]{1,0:T(8,128)(2,1)S(1)} %get-tuple-element.11), channel_id=1, source_target_pairs={{4,0},{8,4},{12,8},{14,12},{10,14},{6,10},{2,6},{0,2},{5,1},{9,5},... | collective-permute-start | bytes 294920 | tf_op jit(solution)/shard_map/ppermute | solution.py:101
  80.2 5.2 %collective-permute-start.24 = (bf16[8,6144]{1,0:T(8,128)(2,1)S(1)}, bf16[8,6144]{1,0:T(8,128)(2,1)S(1)}, u32[]{:S(2)}, u32[]{:S(2)}) collective-permute-start(bf16[8,6144]{1,0:T(8,128)(2,1)S(1)} %get-tuple-element.10), channel_id=1, source_target_pairs={{4,0},{8,4},{12,8},{14,12},{10,14},{6,10},{2,6},{0,2},{5,1},{9,5},... | collective-permute-start | bytes 294920 | tf_op jit(solution)/shard_map/ppermute | solution.py:101
  80.6 4.7 %collective-permute-start.27 = (bf16[8,6144]{1,0:T(8,128)(2,1)S(1)}, bf16[8,6144]{1,0:T(8,128)(2,1)S(1)}, u32[]{:S(2)}, u32[]{:S(2)}) collective-permute-start(bf16[8,6144]{1,0:T(8,128)(2,1)S(1)} %get-tuple-element.9), channel_id=1, source_target_pairs={{0,4},{4,8},{8,12},{12,14},{14,10},{10,6},{6,2},{2,0},{1,5},{5,9},... | collective-permute-start | bytes 294920 | tf_op jit(solution)/shard_map/ppermute | solution.py:98
  86.6 4.7 %collective-permute-start.25 = (bf16[8,6144]{1,0:T(8,128)(2,1)S(1)}, bf16[8,6144]{1,0:T(8,128)(2,1)S(1)}, u32[]{:S(2)}, u32[]{:S(2)}) collective-permute-start(bf16[8,6144]{1,0:T(8,128)(2,1)S(1)} %get-tuple-element.7), channel_id=1, source_target_pairs={{4,0},{8,4},{12,8},{14,12},{10,14},{6,10},{2,6},{0,2},{5,1},{9,5},... | collective-permute-start | bytes 294920 | tf_op jit(solution)/shard_map/ppermute | solution.py:101
  87.1 4.6 %collective-permute-start.28 = (bf16[8,6144]{1,0:T(8,128)(2,1)S(1)}, bf16[8,6144]{1,0:T(8,128)(2,1)S(1)}, u32[]{:S(2)}, u32[]{:S(2)}) collective-permute-start(bf16[8,6144]{1,0:T(8,128)(2,1)S(1)} %get-tuple-element.6), channel_id=1, source_target_pairs={{0,4},{4,8},{8,12},{12,14},{14,10},{10,6},{6,2},{2,0},{1,5},{5,9},... | collective-permute-start | bytes 294920 | tf_op jit(solution)/shard_map/ppermute | solution.py:98
  92.7 1.4 %collective-permute-start.29 = (bf16[8,6144]{1,0:T(8,128)(2,1)S(1)}, bf16[8,6144]{1,0:T(8,128)(2,1)S(1)}, u32[]{:S(2)}, u32[]{:S(2)}) collective-permute-start(bf16[8,6144]{1,0:T(8,128)(2,1)S(1)} %fusion.42), channel_id=1, source_target_pairs={{0,1},{1,0},{2,3},{3,2},{4,5},{5,4},{6,7},{7,6},{8,9},{9,8},{10,11... | collective-permute-start | bytes 294920 | tf_op jit(solution)/shard_map/ppermute | solution.py:159
  (4 other events, 6.3 us)

commit v2 on v1

v2 whole, which is shorter than its diff:
```python
import math

import jax
import jax.numpy as jnp
from jax import lax
from jax.experimental import pallas as pl
from jax.experimental.pallas import tpu as pltpu
from jax.sharding import PartitionSpec as P

HEAD = 128


def ring_of(count):
    if count == 8:
        return [0, 2, 4, 6, 7, 5, 3, 1]
    return list(range(count))


def experts_kernel(rows_ref, gate_ref, up_ref, down_ref, out_ref, act_ref):
    feat_width = rows_ref.shape[1]
    hidden = gate_ref.shape[1]
    step = 256

    @pl.loop(0, hidden // step)
    def _(index):
        columns = pl.ds(pl.multiple_of(index * step, step), step)
        gate_act = jnp.dot(
            rows_ref[...], gate_ref[:, columns], preferred_element_type=jnp.float32
        )
        upward = jnp.dot(rows_ref[...], up_ref[:, columns], preferred_element_type=jnp.float32)
        act_ref[:, columns] = (gate_act / (1.0 + jnp.exp(-gate_act)) * upward).astype(
            act_ref.dtype
        )

    wide = 512

    @pl.loop(0, feat_width // wide)
    def _(index):
        columns = pl.ds(pl.multiple_of(index * wide, wide), wide)
        out_ref[:, columns] = jnp.dot(
            act_ref[...], down_ref[:, columns], preferred_element_type=jnp.float32
        ).astype(out_ref.dtype)


def experts(rows, gate, up, down):
    count, feat_width = rows.shape
    hidden = gate.shape[1]
    vmem = pl.BlockSpec(memory_space=pltpu.VMEM)
    return pl.pallas_call(
        experts_kernel,
        out_shape=jax.ShapeDtypeStruct((count, feat_width), jnp.bfloat16),
        in_specs=[vmem] * 4,
        out_specs=vmem,
        scratch_shapes=[pltpu.VMEM((count, hidden), jnp.bfloat16)],
        compiler_params=pltpu.CompilerParams(vmem_limit_bytes=8 << 20),
        cost_estimate=pl.CostEstimate(
            flops=6 * count * feat_width * hidden,
            bytes_accessed=6 * feat_width * hidden,
            transcendentals=count * hidden,
        ),
    )(rows, gate, up, down)


def add_kernel(*refs):
    total = refs[0][...].astype(jnp.float32)
    for ref in refs[1:-1]:
        total = total + ref[...].astype(jnp.float32)
    refs[-1][...] = total.astype(refs[-1].dtype)


def add(*terms):
    vmem = pl.BlockSpec(memory_space=pltpu.VMEM)
    size = terms[0].size
    return pl.pallas_call(
        add_kernel,
        out_shape=jax.ShapeDtypeStruct(terms[0].shape, terms[0].dtype),
        in_specs=[vmem] * len(terms),
        out_specs=vmem,
        compiler_params=pltpu.CompilerParams(vmem_limit_bytes=1 << 20),
        cost_estimate=pl.CostEstimate(
            flops=size * len(terms), bytes_accessed=2 * size * len(terms), transcendentals=0
        ),
    )(*terms)


def front_kernel(
    here_ref,
    hidden_ref,
    query_ref,
    key_ref,
    value_ref,
    new_key_ref,
    new_value_ref,
    length_ref,
    ids_ref,
    probs_ref,
    residual_ref,
    own_ref,
    theirs_ref,
    slots_ref,
    weights_ref,
    normed_ref,
):
    rows, feat_width = hidden_ref.shape
    span = key_ref.shape[1]
    kv_width = key_ref.shape[2]
    kv_heads = kv_width // HEAD
    group = feat_width // kv_width
    scale = 1.0 / math.sqrt(HEAD)
    shape = (group * rows, rows * span)
    column = lax.broadcasted_iota(jnp.int32, shape, 1)
    request = lax.broadcasted_iota(jnp.int32, shape, 0) & (rows - 1)
    first = request * span
    limit = first + jnp.concatenate([length_ref[...]] * group, 0)
    valid = (column >= first) & (column < limit)
    total = jnp.zeros((rows, 1), jnp.float32)
    for head in range(kv_heads):
        lanes = pl.ds(head * HEAD, HEAD)
        wanted = [head * group + member for member in range(group)]
        query = jnp.concatenate([query_ref[:, q * HEAD : (q + 1) * HEAD] for q in wanted], 0)
        keys = key_ref[:, :, lanes].reshape(rows * span, HEAD)
        scores = (
            lax.dot_general(
                query, keys, (((1,), (1,)), ((), ())), preferred_element_type=jnp.float32
            )
            * scale
        )
        scores = jnp.where(valid, scores, -1e30)
        new_key = jnp.concatenate([new_key_ref[:, lanes].astype(jnp.float32)] * group, 0)
        own_score = jnp.sum(query.astype(jnp.float32) * new_key, -1, keepdims=True) * scale
        top = jnp.maximum(jnp.max(scores, -1, keepdims=True), own_score)
        powers = jnp.exp(scores - top)
        own_power = jnp.exp(own_score - top)
        inverse = 1.0 / (jnp.sum(powers, -1, keepdims=True) + own_power)
        attention = (powers * inverse).astype(jnp.bfloat16)
        own_weight = (own_power * inverse).astype(jnp.bfloat16).astype(jnp.float32)
        values = value_ref[:, :, lanes].reshape(rows * span, HEAD)
        mixed = jnp.dot(attention, values, preferred_element_type=jnp.float32)
        new_value = jnp.concatenate([new_value_ref[:, lanes].astype(jnp.float32)] * group, 0)
        mixed = mixed + own_weight * new_value
        for member, q in enumerate(wanted):
            cols = pl.ds(q * HEAD, HEAD)
            part = hidden_ref[:, cols].astype(jnp.float32) + mixed[
                member * rows : (member + 1) * rows
            ]
            residual_ref[:, cols] = part
            total = total + jnp.sum(part, -1, keepdims=True)
    centre = total * (1.0 / feat_width)
    spread = jnp.zeros((rows, 1), jnp.float32)
    wide = 1024
    for at in range(0, feat_width, wide):
        centered = residual_ref[:, at : at + wide] - centre
        spread = spread + jnp.sum(centered * centered, -1, keepdims=True)
    inverse = lax.rsqrt(spread * (1.0 / feat_width) + 1e-05)
    for at in range(0, feat_width, wide):
        centered = residual_ref[:, at : at + wide] - centre
        normed_ref[:, at : at + wide] = (centered * inverse).astype(jnp.bfloat16)

    here = here_ref[0]
    mix = probs_ref[...] / jnp.sum(probs_ref[...], -1, keepdims=True)
    below = (
        lax.broadcasted_iota(jnp.int32, (rows, rows), 0)
        > lax.broadcasted_iota(jnp.int32, (rows, rows), 1)
    ).astype(jnp.float32)
    cap = own_ref.shape[0]
    slot = lax.broadcasted_iota(jnp.int32, (rows, cap), 1).astype(jnp.float32)
    for place, label in enumerate((here, 1 - here)):
        match = ids_ref[...] == label
        weights_ref[:, place : place + 1] = jnp.sum(jnp.where(match, mix, 0.0), -1, keepdims=True)
        chosen = jnp.max(jnp.where(match, 1.0, 0.0), -1, keepdims=True)
        rank = jnp.dot(
            below, jnp.broadcast_to(chosen, (rows, cap)), preferred_element_type=jnp.float32
        )
        picks = jnp.where(rank == slot, chosen, 0.0)
        slots_ref[:, place * cap : (place + 1) * cap] = picks
        out_ref = (own_ref, theirs_ref)[place]
        out_ref[...] = lax.dot_general(
            picks.astype(jnp.bfloat16),
            normed_ref[...],
            (((0,), (0,)), ((), ())),
            preferred_element_type=jnp.float32,
        ).astype(jnp.bfloat16)


def tail_kernel(
    residual_ref, slots_ref, weights_ref, first_ref, second_ref, third_ref, back_ref, out_ref
):
    cap = back_ref.shape[0]
    own = (
        first_ref[...].astype(jnp.float32)
        + second_ref[...].astype(jnp.float32)
        + third_ref[...].astype(jnp.float32)
    ).astype(jnp.bfloat16)
    result = residual_ref[...]
    for place, block in enumerate((own, back_ref[...])):
        picks = slots_ref[:, place * cap : (place + 1) * cap].astype(jnp.bfloat16)
        result = result + weights_ref[:, place : place + 1] * jnp.dot(
            picks, block, preferred_element_type=jnp.float32
        )
    out_ref[...] = result


def body(
    hidden_in,
    queries,
    cache_keys,
    cache_values,
    new_keys,
    new_values,
    lengths,
    expert_ids,
    gate_probs,
    w_gate,
    w_up,
    w_down,
):
    row_count = hidden_in.shape[0]
    feat_width = hidden_in.shape[1]
    cap_slots = row_count // 2
    vmem = pl.BlockSpec(memory_space=pltpu.VMEM)
    here = lax.axis_index("expert").astype(jnp.int32).reshape(1)
    residual, own, theirs, slots, weights = pl.pallas_call(
        front_kernel,
        out_shape=(
            jax.ShapeDtypeStruct((row_count, feat_width), jnp.float32),
            jax.ShapeDtypeStruct((cap_slots, feat_width), jnp.bfloat16),
            jax.ShapeDtypeStruct((cap_slots, feat_width), jnp.bfloat16),
            jax.ShapeDtypeStruct((row_count, 2 * cap_slots), jnp.float32),
            jax.ShapeDtypeStruct((row_count, 2), jnp.float32),
        ),
        in_specs=[pl.BlockSpec(memory_space=pltpu.SMEM)] + [vmem] * 9,
        out_specs=(vmem,) * 5,
        scratch_shapes=[pltpu.VMEM((row_count, feat_width), jnp.bfloat16)],
        compiler_params=pltpu.CompilerParams(vmem_limit_bytes=16 << 20),
        cost_estimate=pl.CostEstimate(
            flops=10**9, bytes_accessed=40 * 10**6, transcendentals=10**6
        ),
    )(
        here,
        hidden_in,
        queries,
        cache_keys,
        cache_values,
        new_keys,
        new_values,
        lengths.reshape(row_count, 1),
        expert_ids,
        gate_probs,
    )

    count = lax.axis_size("attn")
    ring = ring_of(count)
    right = [(ring[i], ring[(i + 1) % count]) for i in range(count)]
    left = [(b, a) for a, b in right]
    swap = [(0, 1), (1, 0)]

    def go_right(block):
        return lax.ppermute(block, "attn", right)

    def go_left(block):
        return lax.ppermute(block, "attn", left)

    half = count // 2
    theirs = lax.ppermute(theirs, "expert", swap)
    own_r, own_l, theirs_r, theirs_l = [own], [own], [theirs], [theirs]
    for step in range(1, half + 1):
        own_r.append(go_right(own_r[-1]))
        theirs_l.append(go_left(theirs_l[-1]))
        if step < half:
            own_l.append(go_left(own_l[-1]))
            theirs_r.append(go_right(theirs_r[-1]))

    blocks = [own, theirs]
    for step in range(1, half):
        blocks += [own_r[step], own_l[step], theirs_r[step], theirs_l[step]]
    blocks += [own_r[half], theirs_l[half]]
    share = experts(jnp.concatenate(blocks), w_gate[0], w_up[0], w_down[0]).reshape(len(blocks), cap_slots, feat_width)
    own_share = {0: share[0], half: share[-2]}
    theirs_share = {0: share[1], -half: share[-1]}
    for step in range(1, half):
        at = 4 * step - 2
        own_share[-step], own_share[step] = share[at], share[at + 1]
        theirs_share[-step], theirs_share[step] = share[at + 2], share[at + 3]

    own_from_l = own_share[half]
    theirs_from_r = theirs_share[-half]
    own_from_r = own_share[1 - half]
    theirs_from_l = theirs_share[half - 1]
    for step in range(half - 1, 0, -1):
        own_from_l = add(go_right(own_from_l), own_share[step])
        theirs_from_r = add(go_left(theirs_from_r), theirs_share[-step])
        if step > 1:
            own_from_r = add(go_left(own_from_r), own_share[1 - step])
            theirs_from_l = add(go_right(theirs_from_l), theirs_share[step - 1])
    theirs_total = add(
        theirs_share[0], go_left(theirs_from_r), go_right(theirs_from_l)
    )
    back = lax.ppermute(theirs_total, "expert", swap)
    return pl.pallas_call(
        tail_kernel,
        out_shape=jax.ShapeDtypeStruct((row_count, feat_width), jnp.float32),
        in_specs=[vmem] * 7,
        out_specs=vmem,
        compiler_params=pltpu.CompilerParams(vmem_limit_bytes=4 << 20),
    )(
        residual,
        slots,
        weights,
        own_share[0],
        go_right(own_from_l),
        go_left(own_from_r),
        back,
    )


def solution(mesh):
    placed = (
        P(("groups", "attn", "expert"), None),
        P(("groups", "attn", "expert"), None),
        P(("groups", "attn", "expert"), None, None),
        P(("groups", "attn", "expert"), None, None),
        P(("groups", "attn", "expert"), None),
        P(("groups", "attn", "expert"), None),
        P(("groups", "attn", "expert")),
        P(("groups", "attn", "expert"), None),
        P(("groups", "attn", "expert"), None),
        P("expert", None, "attn"),
        P("expert", None, "attn"),
        P("expert", "attn", None),
    )
    return jax.shard_map(
        body,
        mesh=mesh,
        in_specs=placed,
        out_specs=P(("groups", "attn", "expert"), None),
        check_vma=False,
    )
```

time: 95.8 us -> 82.1 us (0.86)
  matrix products: 23.2 us -> 0 us
  local copies, waits for them, and re-layouts: 4.52 us -> 20.1 us
  Pallas kernels: 0 us -> 12.3 us
  waiting for transfers between devices: 29.7 us -> 18.2 us
  other arithmetic: 7.76 us -> 0 us
  starting transfers between devices: 29.8 us -> 30.8 us
    dot_general x7 -> x0, matrix products: 23.2 us -> none  [the longest x1 12.5 us: experts(): return jnp.dot(hidden_act, w_down[0], preferred_element_type=jnp.float32)]
    unnamed x28 -> x35, local copies, waits for them, and re-layouts: 1.34 us -> 19.2 us
    pallas_call x0 -> x14, Pallas kernels: none -> 12.3 us  [the longest x1 6.52 us: experts(): pl.pallas_call(experts_kernel, out_shape=jax.ShapeDtypeStruct((count, fea...]
    ppermute x14, waiting for transfers between devices: 11.4 us -> 5.11 us  [go_right(): return lax.ppermute(block, 'attn', right)]
    convert_element_type x4 -> x0, other arithmetic: 4.4 us -> none  [narrow(): return block.astype(jnp.bfloat16)]
    ppermute x14, starting transfers between devices: 3.75 us -> 7.94 us  [go_left(): return lax.ppermute(block, 'attn', left)]
    ppermute x14, waiting for transfers between devices: 15.8 us -> 11.8 us  [go_left(): return lax.ppermute(block, 'attn', left)]
    ppermute x14, starting transfers between devices: 26 us -> 22.8 us  [go_right(): return lax.ppermute(block, 'attn', right)]
  transfers between devices with their start and end apart: 30 -> 30, of which waited for: 16 -> 15; matrix products, arithmetic and copies ran while one was open for 2% -> 0% of each run, Pallas kernels for 0% -> 0%
where the time goes in v2:
time: 82.1 us; the launch traced here: 81.6 us
  starting transfers between devices  30.8 us (38%)
  local copies, waits for them, and re-layouts  20.1 us (24%)
  waiting for transfers between devices  18.2 us (22%)
  Pallas kernels  12.3 us (15%)
    ppermute x14, starting transfers between devices, go_right(): return lax.ppermute(block, 'attn', right)  22.8 us
    unnamed x35, local copies, waits for them, and re-layouts  19.2 us
    ppermute x14, waiting for transfers between devices, go_left(): return lax.ppermute(block, 'attn', left)  11.8 us
    ppermute x14, starting transfers between devices, go_left(): return lax.ppermute(block, 'attn', left)  7.94 us
    pallas_call x1, Pallas kernels, experts(): pl.pallas_call(experts_kernel, out_shape=jax.ShapeDtypeStruct((count, fea...  6.52 us
    ppermute x14, waiting for transfers between devices, go_right(): return lax.ppermute(block, 'attn', right)  5.11 us
    pallas_call x1, Pallas kernels, body(): pl.pallas_call(front_kernel, out_shape=(jax.ShapeDtypeStruct((row_count,...  4.47 us
  transfers between devices with their start and end apart: 30, of which 15 were waited for; matrix products, arithmetic and copies ran while one was open for 0% of the time, Pallas kernels for 0%

profile of v2, /device:TPU:0, one launch (start us, length us, event | category | flops | bytes accessed | tf_op | source)
XLA Modules:
  0.0 81.6 jit_solution(11185573955769024911)
XLA Ops:
  2.2 1.6 %copy-done.3 = bf16[16,64,1024]{2,1,0:T(8,128)(2,1)S(1)} copy-done((bf16[16,64,1024]{2,1,0:T(8,128)(2,1)S(1)}, bf16[16,64,1024]{2,1,0:T(8,128)(2,1)}, u32[]{:S(2)}) %copy-start.3) | copy-done | bytes 2097176
  3.8 1.6 %copy-done.4 = bf16[16,64,1024]{2,1,0:T(8,128)(2,1)S(1)} copy-done((bf16[16,64,1024]{2,1,0:T(8,128)(2,1)S(1)}, bf16[16,64,1024]{2,1,0:T(8,128)(2,1)}, u32[]{:S(2)}) %copy-start.4) | copy-done | bytes 2097176
  8.8 4.5 %shard_map.118 = (f32[16,6144]{1,0:T(8,128)S(1)}, bf16[8,6144]{1,0:T(8,128)(2,1)S(1)}, bf16[8,6144]{1,0:T(8,128)(2,1)S(1)}, f32[16,16]{1,0:T(8,128)S(1)}, f32[16,2]{1,0:T(8,128)S(1)}) custom-call(s32[1]{0:T(128)} %bitcast.here_ref, bf16[16,6144]{1,0:T(8,128)(2,1)S(1)} %copy-done.5, bf16[16,6144]{1,0:T(8,128)(2,1)S(1)} %copy-done.6, ...), custom_call_target="tpu_custom_call" | custom-call | flops 1000000000 | bytes 40000000 | tf_op jit(solution)/shard_map/pallas_call | solution.py:222
  13.3 3.1 %collective-permute-start.1 = (bf16[8,6144]{1,0:T(8,128)(2,1)S(1)}, bf16[8,6144]{1,0:T(8,128)(2,1)S(1)}, u32[]{:S(2)}, u32[]{:S(2)}) collective-permute-start(bf16[8,6144]{1,0:T(8,128)(2,1)S(1)} %get-tuple-element.13), channel_id=1, source_target_pairs={{0,4},{4,8},{8,12},{12,14},{14,10},{10,6},{6,2},{2,0},{1,5},{5,9},... | collective-permute-start | bytes 294920 | tf_op jit(solution)/shard_map/ppermute | solution.py:258
  16.4 1.3 %collective-permute-done = bf16[8,6144]{1,0:T(8,128)(2,1)S(1)} collective-permute-done((bf16[8,6144]{1,0:T(8,128)(2,1)S(1)}, bf16[8,6144]{1,0:T(8,128)(2,1)S(1)}, u32[]{:S(2)}, u32[]{:S(2)}) %collective-permute-start) | collective-permute-done | bytes 98336 | tf_op jit(solution)/shard_map/ppermute | solution.py:264
  17.7 2.0 %collective-permute-start.3 = (bf16[8,6144]{1,0:T(8,128)(2,1)S(1)}, bf16[8,6144]{1,0:T(8,128)(2,1)S(1)}, u32[]{:S(2)}, u32[]{:S(2)}) collective-permute-start(bf16[8,6144]{1,0:T(8,128)(2,1)S(1)} %collective-permute-done), channel_id=1, source_target_pairs={{0,4},{4,8},{8,12},{12,14},{14,10},{10,6},{6,2},{2,0},{1,5},{5,9},... | collective-permute-start | bytes 294920 | tf_op jit(solution)/shard_map/ppermute | solution.py:258
  19.7 2.1 %collective-permute-start.5 = (bf16[8,6144]{1,0:T(8,128)(2,1)S(1)}, bf16[8,6144]{1,0:T(8,128)(2,1)S(1)}, u32[]{:S(2)}, u32[]{:S(2)}) collective-permute-start(bf16[8,6144]{1,0:T(8,128)(2,1)S(1)} %collective-permute-done.1), channel_id=1, source_target_pairs={{0,4},{4,8},{8,12},{12,14},{14,10},{10,6},{6,2},{2,0},{1,5},{5,9},... | collective-permute-start | bytes 294920 | tf_op jit(solution)/shard_map/ppermute | solution.py:258
  21.9 1.4 %collective-permute-done.3 = bf16[8,6144]{1,0:T(8,128)(2,1)S(1)} collective-permute-done((bf16[8,6144]{1,0:T(8,128)(2,1)S(1)}, bf16[8,6144]{1,0:T(8,128)(2,1)S(1)}, u32[]{:S(2)}, u32[]{:S(2)}) %collective-permute-start.3) | collective-permute-done | bytes 98336 | tf_op jit(solution)/shard_map/ppermute | solution.py:258
  23.2 1.9 %collective-permute-start.7 = (bf16[8,6144]{1,0:T(8,128)(2,1)S(1)}, bf16[8,6144]{1,0:T(8,128)(2,1)S(1)}, u32[]{:S(2)}, u32[]{:S(2)}) collective-permute-start(bf16[8,6144]{1,0:T(8,128)(2,1)S(1)} %collective-permute-done.3), channel_id=1, source_target_pairs={{0,4},{4,8},{8,12},{12,14},{14,10},{10,6},{6,2},{2,0},{1,5},{5,9},... | collective-permute-start | bytes 294920 | tf_op jit(solution)/shard_map/ppermute | solution.py:258
  25.3 2.0 %collective-permute-start.9 = (bf16[8,6144]{1,0:T(8,128)(2,1)S(1)}, bf16[8,6144]{1,0:T(8,128)(2,1)S(1)}, u32[]{:S(2)}, u32[]{:S(2)}) collective-permute-start(bf16[8,6144]{1,0:T(8,128)(2,1)S(1)} %collective-permute-done.5), channel_id=1, source_target_pairs={{0,4},{4,8},{8,12},{12,14},{14,10},{10,6},{6,2},{2,0},{1,5},{5,9},... | collective-permute-start | bytes 294920 | tf_op jit(solution)/shard_map/ppermute | solution.py:258
  27.5 1.2 %collective-permute-done.7 = bf16[8,6144]{1,0:T(8,128)(2,1)S(1)} collective-permute-done((bf16[8,6144]{1,0:T(8,128)(2,1)S(1)}, bf16[8,6144]{1,0:T(8,128)(2,1)S(1)}, u32[]{:S(2)}, u32[]{:S(2)}) %collective-permute-start.7) | collective-permute-done | bytes 98336 | tf_op jit(solution)/shard_map/ppermute | solution.py:258
  28.8 2.0 %collective-permute-start.11 = (bf16[8,6144]{1,0:T(8,128)(2,1)S(1)}, bf16[8,6144]{1,0:T(8,128)(2,1)S(1)}, u32[]{:S(2)}, u32[]{:S(2)}) collective-permute-start(bf16[8,6144]{1,0:T(8,128)(2,1)S(1)} %collective-permute-done.7), channel_id=1, source_target_pairs={{0,4},{4,8},{8,12},{12,14},{14,10},{10,6},{6,2},{2,0},{1,5},{5,9},... | collective-permute-start | bytes 294920 | tf_op jit(solution)/shard_map/ppermute | solution.py:258
  31.0 1.9 %collective-permute-start.13 = (bf16[8,6144]{1,0:T(8,128)(2,1)S(1)}, bf16[8,6144]{1,0:T(8,128)(2,1)S(1)}, u32[]{:S(2)}, u32[]{:S(2)}) collective-permute-start(bf16[8,6144]{1,0:T(8,128)(2,1)S(1)} %collective-permute-done.9), channel_id=1, source_target_pairs={{0,4},{4,8},{8,12},{12,14},{14,10},{10,6},{6,2},{2,0},{1,5},{5,9},... | collective-permute-start | bytes 294920 | tf_op jit(solution)/shard_map/ppermute | solution.py:258
  32.9 3.2 %collective-permute-done.12 = bf16[8,6144]{1,0:T(8,128)(2,1)S(1)} collective-permute-done((bf16[8,6144]{1,0:T(8,128)(2,1)S(1)}, bf16[8,6144]{1,0:T(8,128)(2,1)S(1)}, u32[]{:S(2)}, u32[]{:S(2)}) %collective-permute-start.12) | collective-permute-done | bytes 98336 | tf_op jit(solution)/shard_map/ppermute | solution.py:261
  36.2 4.6 %collective-permute-done.14 = bf16[8,6144]{1,0:T(8,128)(2,1)S(1)} collective-permute-done((bf16[8,6144]{1,0:T(8,128)(2,1)S(1)}, bf16[8,6144]{1,0:T(8,128)(2,1)S(1)}, u32[]{:S(2)}, u32[]{:S(2)}) %collective-permute-start.14) | collective-permute-done | bytes 98336 | tf_op jit(solution)/shard_map/ppermute | solution.py:261
  40.8 3.7 %copy-done = bf16[1,6144,768]{2,1,0:T(8,128)(2,1)S(1)} copy-done((bf16[1,6144,768]{2,1,0:T(8,128)(2,1)S(1)}, bf16[1,6144,768]{2,1,0:T(8,128)(2,1)}, u32[]{:S(2)}) %copy-start) | copy-done | bytes 9437208
  44.4 3.7 %copy-done.1 = bf16[1,6144,768]{2,1,0:T(8,128)(2,1)S(1)} copy-done((bf16[1,6144,768]{2,1,0:T(8,128)(2,1)S(1)}, bf16[1,6144,768]{2,1,0:T(8,128)(2,1)}, u32[]{:S(2)}) %copy-start.1) | copy-done | bytes 9437208
  48.1 3.7 %copy-done.2 = bf16[1,768,6144]{2,1,0:T(8,128)(2,1)S(1)} copy-done((bf16[1,768,6144]{2,1,0:T(8,128)(2,1)S(1)}, bf16[1,768,6144]{2,1,0:T(8,128)(2,1)}, u32[]{:S(2)}) %copy-start.2) | copy-done | bytes 9437208
  51.8 6.5 %shard_map.119 = bf16[128,6144]{1,0:T(8,128)(2,1)S(1)} custom-call(bf16[128,6144]{1,0:T(8,128)(2,1)S(1)} %constant_dynamic-update-slice_fusion.rows_ref, bf16[6144,768]{1,0:T(8,128)(2,1)S(1)} %bitcast.5, bf16[6144,768]{1,0:T(8,128)(2,1)S(1)} %bitcast.6, bf16[768,6144]{1,0:T(8,128)(2,1)S(1)} %bitcast.7), custom_call_target="tpu_custom_call" | custom-call | flops 3623878656 | bytes 28311552 | tf_op jit(solution)/shard_map/pallas_call | solution.py:49
  58.5 2.0 %collective-permute-start.15 = (bf16[8,6144]{1,0:T(8,128)(2,1)S(1)}, bf16[8,6144]{1,0:T(8,128)(2,1)S(1)}, u32[]{:S(2)}, u32[]{:S(2)}) collective-permute-start(bf16[8,6144]{1,0:T(8,128)(2,1)S(1)} %get-tuple-element.29), channel_id=1, source_target_pairs={{0,4},{4,8},{8,12},{12,14},{14,10},{10,6},{6,2},{2,0},{1,5},{5,9},... | collective-permute-start | bytes 294920 | tf_op jit(solution)/shard_map/ppermute | solution.py:258
  60.5 1.6 %collective-permute-start.26 = (bf16[8,6144]{1,0:T(8,128)(2,1)S(1)}, bf16[8,6144]{1,0:T(8,128)(2,1)S(1)}, u32[]{:S(2)}, u32[]{:S(2)}) collective-permute-start(bf16[8,6144]{1,0:T(8,128)(2,1)S(1)} %get-tuple-element.17), channel_id=1, source_target_pairs={{0,4},{4,8},{8,12},{12,14},{14,10},{10,6},{6,2},{2,0},{1,5},{5,9},... | collective-permute-start | bytes 294920 | tf_op jit(solution)/shard_map/ppermute | solution.py:258
  62.1 1.2 %collective-permute-done.22.refs_0_ = bf16[8,6144]{1,0:T(8,128)(2,1)S(1)} collective-permute-done((bf16[8,6144]{1,0:T(8,128)(2,1)S(1)}, bf16[8,6144]{1,0:T(8,128)(2,1)S(1)}, u32[]{:S(2)}, u32[]{:S(2)}) %collective-permute-start.22) | collective-permute-done | bytes 98336 | tf_op jit(solution)/shard_map/ppermute | solution.py:261
  64.1 1.9 %collective-permute-start.19 = (bf16[8,6144]{1,0:T(8,128)(2,1)S(1)}, bf16[8,6144]{1,0:T(8,128)(2,1)S(1)}, u32[]{:S(2)}, u32[]{:S(2)}) collective-permute-start(bf16[8,6144]{1,0:T(8,128)(2,1)S(1)} %get-tuple-element.25), channel_id=1, source_target_pairs={{4,0},{8,4},{12,8},{14,12},{10,14},{6,10},{2,6},{0,2},{5,1},{9,5},... | collective-permute-start | bytes 294920 | tf_op jit(solution)/shard_map/ppermute | solution.py:261
  66.3 1.3 %collective-permute-start.27 = (bf16[8,6144]{1,0:T(8,128)(2,1)S(1)}, bf16[8,6144]{1,0:T(8,128)(2,1)S(1)}, u32[]{:S(2)}, u32[]{:S(2)}) collective-permute-start(bf16[8,6144]{1,0:T(8,128)(2,1)S(1)} %shard_map.128), channel_id=1, source_target_pairs={{0,4},{4,8},{8,12},{12,14},{14,10},{10,6},{6,2},{2,0},{1,5},{5,9},... | collective-permute-start | bytes 294920 | tf_op jit(solution)/shard_map/ppermute | solution.py:258
  69.2 1.6 %collective-permute-start.20 = (bf16[8,6144]{1,0:T(8,128)(2,1)S(1)}, bf16[8,6144]{1,0:T(8,128)(2,1)S(1)}, u32[]{:S(2)}, u32[]{:S(2)}) collective-permute-start(bf16[8,6144]{1,0:T(8,128)(2,1)S(1)} %shard_map.123), channel_id=1, source_target_pairs={{4,0},{8,4},{12,8},{14,12},{10,14},{6,10},{2,6},{0,2},{5,1},{9,5},... | collective-permute-start | bytes 294920 | tf_op jit(solution)/shard_map/ppermute | solution.py:261
  72.5 1.2 %collective-permute-start.28 = (bf16[8,6144]{1,0:T(8,128)(2,1)S(1)}, bf16[8,6144]{1,0:T(8,128)(2,1)S(1)}, u32[]{:S(2)}, u32[]{:S(2)}) collective-permute-start(bf16[8,6144]{1,0:T(8,128)(2,1)S(1)} %shard_map.129), channel_id=1, source_target_pairs={{0,4},{4,8},{8,12},{12,14},{14,10},{10,6},{6,2},{2,0},{1,5},{5,9},... | collective-permute-start | bytes 294920 | tf_op jit(solution)/shard_map/ppermute | solution.py:258
  74.7 1.2 %collective-permute-start.21 = (bf16[8,6144]{1,0:T(8,128)(2,1)S(1)}, bf16[8,6144]{1,0:T(8,128)(2,1)S(1)}, u32[]{:S(2)}, u32[]{:S(2)}) collective-permute-start(bf16[8,6144]{1,0:T(8,128)(2,1)S(1)} %shard_map.124), channel_id=1, source_target_pairs={{4,0},{8,4},{12,8},{14,12},{10,14},{6,10},{2,6},{0,2},{5,1},{9,5},... | collective-permute-start | bytes 294920 | tf_op jit(solution)/shard_map/ppermute | solution.py:261
  75.9 1.0 %collective-permute-start.18 = (bf16[8,6144]{1,0:T(8,128)(2,1)S(1)}, bf16[8,6144]{1,0:T(8,128)(2,1)S(1)}, u32[]{:S(2)}, u32[]{:S(2)}) collective-permute-start(bf16[8,6144]{1,0:T(8,128)(2,1)S(1)} %shard_map.122), channel_id=1, source_target_pairs={{0,4},{4,8},{8,12},{12,14},{14,10},{10,6},{6,2},{2,0},{1,5},{5,9},... | collective-permute-start | bytes 294920 | tf_op jit(solution)/shard_map/ppermute | solution.py:258
  77.2 1.2 %collective-permute-done.25.refs_1_ = bf16[8,6144]{1,0:T(8,128)(2,1)S(1)} collective-permute-done((bf16[8,6144]{1,0:T(8,128)(2,1)S(1)}, bf16[8,6144]{1,0:T(8,128)(2,1)S(1)}, u32[]{:S(2)}, u32[]{:S(2)}) %collective-permute-start.25) | collective-permute-done | bytes 98336 | tf_op jit(solution)/shard_map/ppermute | solution.py:261
  78.6 0.9 %collective-permute-done.21.third_ref = bf16[8,6144]{1,0:T(8,128)(2,1)S(1)} collective-permute-done((bf16[8,6144]{1,0:T(8,128)(2,1)S(1)}, bf16[8,6144]{1,0:T(8,128)(2,1)S(1)}, u32[]{:S(2)}, u32[]{:S(2)}) %collective-permute-start.21) | collective-permute-done | bytes 98336 | tf_op jit(solution)/shard_map/ppermute | solution.py:261
  79.5 1.1 %collective-permute-done.18.second_ref = bf16[8,6144]{1,0:T(8,128)(2,1)S(1)} collective-permute-done((bf16[8,6144]{1,0:T(8,128)(2,1)S(1)}, bf16[8,6144]{1,0:T(8,128)(2,1)S(1)}, u32[]{:S(2)}, u32[]{:S(2)}) %collective-permute-start.18) | collective-permute-done | bytes 98336 | tf_op jit(solution)/shard_map/ppermute | solution.py:258
  80.6 1.0 %shard_map.131 = f32[16,6144]{1,0:T(8,128)} custom-call(f32[16,6144]{1,0:T(8,128)S(1)} %get-tuple-element.10.residual_ref, f32[16,16]{1,0:T(8,128)S(1)} %get-tuple-element.11.slots_ref, f32[16,2]{1,0:T(8,128)S(1)} %get-tuple-element.12.weights_ref, bf16[8,6144]{1,0:T(8,128)(2,1)S(1)} %get-tuple-element.30.first_ref, ...), custom_call_target="tpu_custom_call" | custom-call | tf_op jit(solution)/shard_map/pallas_call | solution.py:299
  (80 shorter events, 12.4 us)
Async XLA Ops:
  13.3 6.4 %collective-permute-start.1 = (bf16[8,6144]{1,0:T(8,128)(2,1)S(1)}, bf16[8,6144]{1,0:T(8,128)(2,1)S(1)}, u32[]{:S(2)}, u32[]{:S(2)}) collective-permute-start(bf16[8,6144]{1,0:T(8,128)(2,1)S(1)} %get-tuple-element.13), channel_id=1, source_target_pairs={{0,4},{4,8},{8,12},{12,14},{14,10},{10,6},{6,2},{2,0},{1,5},{5,9},... | collective-permute-start | bytes 294920 | tf_op jit(solution)/shard_map/ppermute | solution.py:258
  16.3 5.4 %collective-permute-start.2 = (bf16[8,6144]{1,0:T(8,128)(2,1)S(1)}, bf16[8,6144]{1,0:T(8,128)(2,1)S(1)}, u32[]{:S(2)}, u32[]{:S(2)}) collective-permute-start(bf16[8,6144]{1,0:T(8,128)(2,1)S(1)} %get-tuple-element.13), channel_id=1, source_target_pairs={{4,0},{8,4},{12,8},{14,12},{10,14},{6,10},{2,6},{0,2},{5,1},{9,5},... | collective-permute-start | bytes 294920 | tf_op jit(solution)/shard_map/ppermute | solution.py:261
  16.4 1.3 %collective-permute-start = (bf16[8,6144]{1,0:T(8,128)(2,1)S(1)}, bf16[8,6144]{1,0:T(8,128)(2,1)S(1)}, u32[]{:S(2)}, u32[]{:S(2)}) collective-permute-start(bf16[8,6144]{1,0:T(8,128)(2,1)S(1)} %get-tuple-element.14), channel_id=1, source_target_pairs={{0,1},{1,0},{2,3},{3,2},{4,5},{5,4},{6,7},{7,6},{8,9},{9,8},{10,11... | collective-permute-start | bytes 294920 | tf_op jit(solution)/shard_map/ppermute | solution.py:264
  17.7 5.6 %collective-permute-start.3 = (bf16[8,6144]{1,0:T(8,128)(2,1)S(1)}, bf16[8,6144]{1,0:T(8,128)(2,1)S(1)}, u32[]{:S(2)}, u32[]{:S(2)}) collective-permute-start(bf16[8,6144]{1,0:T(8,128)(2,1)S(1)} %collective-permute-done), channel_id=1, source_target_pairs={{0,4},{4,8},{8,12},{12,14},{14,10},{10,6},{6,2},{2,0},{1,5},{5,9},... | collective-permute-start | bytes 294920 | tf_op jit(solution)/shard_map/ppermute | solution.py:258
  19.7 5.5 %collective-permute-start.4 = (bf16[8,6144]{1,0:T(8,128)(2,1)S(1)}, bf16[8,6144]{1,0:T(8,128)(2,1)S(1)}, u32[]{:S(2)}, u32[]{:S(2)}) collective-permute-start(bf16[8,6144]{1,0:T(8,128)(2,1)S(1)} %collective-permute-done), channel_id=1, source_target_pairs={{4,0},{8,4},{12,8},{14,12},{10,14},{6,10},{2,6},{0,2},{5,1},{9,5},... | collective-permute-start | bytes 294920 | tf_op jit(solution)/shard_map/ppermute | solution.py:261
  19.7 5.6 %collective-permute-start.5 = (bf16[8,6144]{1,0:T(8,128)(2,1)S(1)}, bf16[8,6144]{1,0:T(8,128)(2,1)S(1)}, u32[]{:S(2)}, u32[]{:S(2)}) collective-permute-start(bf16[8,6144]{1,0:T(8,128)(2,1)S(1)} %collective-permute-done.1), channel_id=1, source_target_pairs={{0,4},{4,8},{8,12},{12,14},{14,10},{10,6},{6,2},{2,0},{1,5},{5,9},... | collective-permute-start | bytes 294920 | tf_op jit(solution)/shard_map/ppermute | solution.py:258
  21.8 5.5 %collective-permute-start.6 = (bf16[8,6144]{1,0:T(8,128)(2,1)S(1)}, bf16[8,6144]{1,0:T(8,128)(2,1)S(1)}, u32[]{:S(2)}, u32[]{:S(2)}) collective-permute-start(bf16[8,6144]{1,0:T(8,128)(2,1)S(1)} %collective-permute-done.2), channel_id=1, source_target_pairs={{4,0},{8,4},{12,8},{14,12},{10,14},{6,10},{2,6},{0,2},{5,1},{9,5},... | collective-permute-start | bytes 294920 | tf_op jit(solution)/shard_map/ppermute | solution.py:261
  23.2 5.5 %collective-permute-start.7 = (bf16[8,6144]{1,0:T(8,128)(2,1)S(1)}, bf16[8,6144]{1,0:T(8,128)(2,1)S(1)}, u32[]{:S(2)}, u32[]{:S(2)}) collective-permute-start(bf16[8,6144]{1,0:T(8,128)(2,1)S(1)} %collective-permute-done.3), channel_id=1, source_target_pairs={{0,4},{4,8},{8,12},{12,14},{14,10},{10,6},{6,2},{2,0},{1,5},{5,9},... | collective-permute-start | bytes 294920 | tf_op jit(solution)/shard_map/ppermute | solution.py:258
  25.2 5.6 %collective-permute-start.8 = (bf16[8,6144]{1,0:T(8,128)(2,1)S(1)}, bf16[8,6144]{1,0:T(8,128)(2,1)S(1)}, u32[]{:S(2)}, u32[]{:S(2)}) collective-permute-start(bf16[8,6144]{1,0:T(8,128)(2,1)S(1)} %collective-permute-done.4), channel_id=1, source_target_pairs={{4,0},{8,4},{12,8},{14,12},{10,14},{6,10},{2,6},{0,2},{5,1},{9,5},... | collective-permute-start | bytes 294920 | tf_op jit(solution)/shard_map/ppermute | solution.py:261
  25.3 5.7 %collective-permute-start.9 = (bf16[8,6144]{1,0:T(8,128)(2,1)S(1)}, bf16[8,6144]{1,0:T(8,128)(2,1)S(1)}, u32[]{:S(2)}, u32[]{:S(2)}) collective-permute-start(bf16[8,6144]{1,0:T(8,128)(2,1)S(1)} %collective-permute-done.5), channel_id=1, source_target_pairs={{0,4},{4,8},{8,12},{12,14},{14,10},{10,6},{6,2},{2,0},{1,5},{5,9},... | collective-permute-start | bytes 294920 | tf_op jit(solution)/shard_map/ppermute | solution.py:258
  27.3 5.6 %collective-permute-start.10 = (bf16[8,6144]{1,0:T(8,128)(2,1)S(1)}, bf16[8,6144]{1,0:T(8,128)(2,1)S(1)}, u32[]{:S(2)}, u32[]{:S(2)}) collective-permute-start(bf16[8,6144]{1,0:T(8,128)(2,1)S(1)} %collective-permute-done.6), channel_id=1, source_target_pairs={{4,0},{8,4},{12,8},{14,12},{10,14},{6,10},{2,6},{0,2},{5,1},{9,5},... | collective-permute-start | bytes 294920 | tf_op jit(solution)/shard_map/ppermute | solution.py:261
  28.8 7.4 %collective-permute-start.11 = (bf16[8,6144]{1,0:T(8,128)(2,1)S(1)}, bf16[8,6144]{1,0:T(8,128)(2,1)S(1)}, u32[]{:S(2)}, u32[]{:S(2)}) collective-permute-start(bf16[8,6144]{1,0:T(8,128)(2,1)S(1)} %collective-permute-done.7), channel_id=1, source_target_pairs={{0,4},{4,8},{8,12},{12,14},{14,10},{10,6},{6,2},{2,0},{1,5},{5,9},... | collective-permute-start | bytes 294920 | tf_op jit(solution)/shard_map/ppermute | solution.py:258
  30.7 5.4 %collective-permute-start.12 = (bf16[8,6144]{1,0:T(8,128)(2,1)S(1)}, bf16[8,6144]{1,0:T(8,128)(2,1)S(1)}, u32[]{:S(2)}, u32[]{:S(2)}) collective-permute-start(bf16[8,6144]{1,0:T(8,128)(2,1)S(1)} %collective-permute-done.8), channel_id=1, source_target_pairs={{4,0},{8,4},{12,8},{14,12},{10,14},{6,10},{2,6},{0,2},{5,1},{9,5},... | collective-permute-start | bytes 294920 | tf_op jit(solution)/shard_map/ppermute | solution.py:261
  31.0 5.2 %collective-permute-start.13 = (bf16[8,6144]{1,0:T(8,128)(2,1)S(1)}, bf16[8,6144]{1,0:T(8,128)(2,1)S(1)}, u32[]{:S(2)}, u32[]{:S(2)}) collective-permute-start(bf16[8,6144]{1,0:T(8,128)(2,1)S(1)} %collective-permute-done.9), channel_id=1, source_target_pairs={{0,4},{4,8},{8,12},{12,14},{14,10},{10,6},{6,2},{2,0},{1,5},{5,9},... | collective-permute-start | bytes 294920 | tf_op jit(solution)/shard_map/ppermute | solution.py:258
  36.1 4.6 %collective-permute-start.14 = (bf16[8,6144]{1,0:T(8,128)(2,1)S(1)}, bf16[8,6144]{1,0:T(8,128)(2,1)S(1)}, u32[]{:S(2)}, u32[]{:S(2)}) collective-permute-start(bf16[8,6144]{1,0:T(8,128)(2,1)S(1)} %collective-permute-done.12), channel_id=1, source_target_pairs={{4,0},{8,4},{12,8},{14,12},{10,14},{6,10},{2,6},{0,2},{5,1},{9,5},... | collective-permute-start | bytes 294920 | tf_op jit(solution)/shard_map/ppermute | solution.py:261
  40.8 3.7 %copy-start = (bf16[1,6144,768]{2,1,0:T(8,128)(2,1)S(1)}, bf16[1,6144,768]{2,1,0:T(8,128)(2,1)}, u32[]{:S(2)}) copy-start(bf16[1,6144,768]{2,1,0:T(8,128)(2,1)} %param.21) | copy-start | bytes 28311556
  44.4 3.7 %copy-start.1 = (bf16[1,6144,768]{2,1,0:T(8,128)(2,1)S(1)}, bf16[1,6144,768]{2,1,0:T(8,128)(2,1)}, u32[]{:S(2)}) copy-start(bf16[1,6144,768]{2,1,0:T(8,128)(2,1)} %param.22) | copy-start | bytes 28311556
  58.5 4.9 %collective-permute-start.22 = (bf16[8,6144]{1,0:T(8,128)(2,1)S(1)}, bf16[8,6144]{1,0:T(8,128)(2,1)S(1)}, u32[]{:S(2)}, u32[]{:S(2)}) collective-permute-start(bf16[8,6144]{1,0:T(8,128)(2,1)S(1)} %get-tuple-element.21), channel_id=1, source_target_pairs={{4,0},{8,4},{12,8},{14,12},{10,14},{6,10},{2,6},{0,2},{5,1},{9,5},... | collective-permute-start | bytes 294920 | tf_op jit(solution)/shard_map/ppermute | solution.py:261
  58.5 7.5 %collective-permute-start.15 = (bf16[8,6144]{1,0:T(8,128)(2,1)S(1)}, bf16[8,6144]{1,0:T(8,128)(2,1)S(1)}, u32[]{:S(2)}, u32[]{:S(2)}) collective-permute-start(bf16[8,6144]{1,0:T(8,128)(2,1)S(1)} %get-tuple-element.29), channel_id=1, source_target_pairs={{0,4},{4,8},{8,12},{12,14},{14,10},{10,6},{6,2},{2,0},{1,5},{5,9},... | collective-permute-start | bytes 294920 | tf_op jit(solution)/shard_map/ppermute | solution.py:258
  60.5 5.7 %collective-permute-start.26 = (bf16[8,6144]{1,0:T(8,128)(2,1)S(1)}, bf16[8,6144]{1,0:T(8,128)(2,1)S(1)}, u32[]{:S(2)}, u32[]{:S(2)}) collective-permute-start(bf16[8,6144]{1,0:T(8,128)(2,1)S(1)} %get-tuple-element.17), channel_id=1, source_target_pairs={{0,4},{4,8},{8,12},{12,14},{14,10},{10,6},{6,2},{2,0},{1,5},{5,9},... | collective-permute-start | bytes 294920 | tf_op jit(solution)/shard_map/ppermute | solution.py:258
  63.4 4.7 %collective-permute-start.23 = (bf16[8,6144]{1,0:T(8,128)(2,1)S(1)}, bf16[8,6144]{1,0:T(8,128)(2,1)S(1)}, u32[]{:S(2)}, u32[]{:S(2)}) collective-permute-start(bf16[8,6144]{1,0:T(8,128)(2,1)S(1)} %shard_map.125), channel_id=1, source_target_pairs={{4,0},{8,4},{12,8},{14,12},{10,14},{6,10},{2,6},{0,2},{5,1},{9,5},... | collective-permute-start | bytes 294920 | tf_op jit(solution)/shard_map/ppermute | solution.py:261
  64.1 5.1 %collective-permute-start.19 = (bf16[8,6144]{1,0:T(8,128)(2,1)S(1)}, bf16[8,6144]{1,0:T(8,128)(2,1)S(1)}, u32[]{:S(2)}, u32[]{:S(2)}) collective-permute-start(bf16[8,6144]{1,0:T(8,128)(2,1)S(1)} %get-tuple-element.25), channel_id=1, source_target_pairs={{4,0},{8,4},{12,8},{14,12},{10,14},{6,10},{2,6},{0,2},{5,1},{9,5},... | collective-permute-start | bytes 294920 | tf_op jit(solution)/shard_map/ppermute | solution.py:261
  66.1 4.9 %collective-permute-start.16 = (bf16[8,6144]{1,0:T(8,128)(2,1)S(1)}, bf16[8,6144]{1,0:T(8,128)(2,1)S(1)}, u32[]{:S(2)}, u32[]{:S(2)}) collective-permute-start(bf16[8,6144]{1,0:T(8,128)(2,1)S(1)} %shard_map.120), channel_id=1, source_target_pairs={{0,4},{4,8},{8,12},{12,14},{14,10},{10,6},{6,2},{2,0},{1,5},{5,9},... | collective-permute-start | bytes 294920 | tf_op jit(solution)/shard_map/ppermute | solution.py:258
  66.3 6.2 %collective-permute-start.27 = (bf16[8,6144]{1,0:T(8,128)(2,1)S(1)}, bf16[8,6144]{1,0:T(8,128)(2,1)S(1)}, u32[]{:S(2)}, u32[]{:S(2)}) collective-permute-start(bf16[8,6144]{1,0:T(8,128)(2,1)S(1)} %shard_map.128), channel_id=1, source_target_pairs={{0,4},{4,8},{8,12},{12,14},{14,10},{10,6},{6,2},{2,0},{1,5},{5,9},... | collective-permute-start | bytes 294920 | tf_op jit(solution)/shard_map/ppermute | solution.py:258
  68.1 5.7 %collective-permute-start.24 = (bf16[8,6144]{1,0:T(8,128)(2,1)S(1)}, bf16[8,6144]{1,0:T(8,128)(2,1)S(1)}, u32[]{:S(2)}, u32[]{:S(2)}) collective-permute-start(bf16[8,6144]{1,0:T(8,128)(2,1)S(1)} %shard_map.126), channel_id=1, source_target_pairs={{4,0},{8,4},{12,8},{14,12},{10,14},{6,10},{2,6},{0,2},{5,1},{9,5},... | collective-permute-start | bytes 294920 | tf_op jit(solution)/shard_map/ppermute | solution.py:261
  69.2 5.5 %collective-permute-start.20 = (bf16[8,6144]{1,0:T(8,128)(2,1)S(1)}, bf16[8,6144]{1,0:T(8,128)(2,1)S(1)}, u32[]{:S(2)}, u32[]{:S(2)}) collective-permute-start(bf16[8,6144]{1,0:T(8,128)(2,1)S(1)} %shard_map.123), channel_id=1, source_target_pairs={{4,0},{8,4},{12,8},{14,12},{10,14},{6,10},{2,6},{0,2},{5,1},{9,5},... | collective-permute-start | bytes 294920 | tf_op jit(solution)/shard_map/ppermute | solution.py:261
  71.0 4.9 %collective-permute-start.17 = (bf16[8,6144]{1,0:T(8,128)(2,1)S(1)}, bf16[8,6144]{1,0:T(8,128)(2,1)S(1)}, u32[]{:S(2)}, u32[]{:S(2)}) collective-permute-start(bf16[8,6144]{1,0:T(8,128)(2,1)S(1)} %shard_map.121), channel_id=1, source_target_pairs={{0,4},{4,8},{8,12},{12,14},{14,10},{10,6},{6,2},{2,0},{1,5},{5,9},... | collective-permute-start | bytes 294920 | tf_op jit(solution)/shard_map/ppermute | solution.py:258
  72.5 4.7 %collective-permute-start.28 = (bf16[8,6144]{1,0:T(8,128)(2,1)S(1)}, bf16[8,6144]{1,0:T(8,128)(2,1)S(1)}, u32[]{:S(2)}, u32[]{:S(2)}) collective-permute-start(bf16[8,6144]{1,0:T(8,128)(2,1)S(1)} %shard_map.129), channel_id=1, source_target_pairs={{0,4},{4,8},{8,12},{12,14},{14,10},{10,6},{6,2},{2,0},{1,5},{5,9},... | collective-permute-start | bytes 294920 | tf_op jit(solution)/shard_map/ppermute | solution.py:258
  73.8 4.7 %collective-permute-start.25 = (bf16[8,6144]{1,0:T(8,128)(2,1)S(1)}, bf16[8,6144]{1,0:T(8,128)(2,1)S(1)}, u32[]{:S(2)}, u32[]{:S(2)}) collective-permute-start(bf16[8,6144]{1,0:T(8,128)(2,1)S(1)} %shard_map.127), channel_id=1, source_target_pairs={{4,0},{8,4},{12,8},{14,12},{10,14},{6,10},{2,6},{0,2},{5,1},{9,5},... | collective-permute-start | bytes 294920 | tf_op jit(solution)/shard_map/ppermute | solution.py:261
  74.7 4.8 %collective-permute-start.21 = (bf16[8,6144]{1,0:T(8,128)(2,1)S(1)}, bf16[8,6144]{1,0:T(8,128)(2,1)S(1)}, u32[]{:S(2)}, u32[]{:S(2)}) collective-permute-start(bf16[8,6144]{1,0:T(8,128)(2,1)S(1)} %shard_map.124), channel_id=1, source_target_pairs={{4,0},{8,4},{12,8},{14,12},{10,14},{6,10},{2,6},{0,2},{5,1},{9,5},... | collective-permute-start | bytes 294920 | tf_op jit(solution)/shard_map/ppermute | solution.py:261
  75.9 4.7 %collective-permute-start.18 = (bf16[8,6144]{1,0:T(8,128)(2,1)S(1)}, bf16[8,6144]{1,0:T(8,128)(2,1)S(1)}, u32[]{:S(2)}, u32[]{:S(2)}) collective-permute-start(bf16[8,6144]{1,0:T(8,128)(2,1)S(1)} %shard_map.122), channel_id=1, source_target_pairs={{0,4},{4,8},{8,12},{12,14},{14,10},{10,6},{6,2},{2,0},{1,5},{5,9},... | collective-permute-start | bytes 294920 | tf_op jit(solution)/shard_map/ppermute | solution.py:258
  78.5 2.1 %collective-permute-start.29 = (bf16[8,6144]{1,0:T(8,128)(2,1)S(1)}, bf16[8,6144]{1,0:T(8,128)(2,1)S(1)}, u32[]{:S(2)}, u32[]{:S(2)}) collective-permute-start(bf16[8,6144]{1,0:T(8,128)(2,1)S(1)} %shard_map.130), channel_id=1, source_target_pairs={{0,1},{1,0},{2,3},{3,2},{4,5},{5,4},{6,7},{7,6},{8,9},{9,8},{10,11... | collective-permute-start | bytes 294920 | tf_op jit(solution)/shard_map/ppermute | solution.py:298
  (7 other events, 10.2 us)

commit v3 on v2

--- a/solution.py
+++ b/solution.py
@@ -16,29 +16,48 @@
     return list(range(count))
 
 
+def load_kernel(after_ref, source_ref, held_ref, sem):
+    copy = pltpu.make_async_copy(source_ref, held_ref, sem)
+    copy.start()
+    copy.wait()
+
+
+def in_hbm(array):
+    return pltpu.with_memory_space_constraint(array, pltpu.HBM)
+
+
+def load(weights, after, room):
+    return pl.pallas_call(
+        load_kernel,
+        out_shape=pltpu.VMEM(weights.shape, weights.dtype),
+        in_specs=[pl.BlockSpec(memory_space=pl.ANY), pl.BlockSpec(memory_space=pltpu.HBM)],
+        out_specs=pl.BlockSpec(memory_space=pltpu.VMEM),
+        scratch_shapes=[pltpu.SemaphoreType.DMA],
+        compiler_params=pltpu.CompilerParams(vmem_limit_bytes=room),
+        cost_estimate=pl.CostEstimate(
+            flops=0, bytes_accessed=2 * weights.size, transcendentals=0
+        ),
+    )(after, in_hbm(weights))
+
+
 def experts_kernel(rows_ref, gate_ref, up_ref, down_ref, out_ref, act_ref):
     feat_width = rows_ref.shape[1]
     hidden = gate_ref.shape[1]
-    step = 256
-
-    @pl.loop(0, hidden // step)
-    def _(index):
-        columns = pl.ds(pl.multiple_of(index * step, step), step)
+    step = math.gcd(hidden, 256)
+    for at in range(0, hidden, step):
         gate_act = jnp.dot(
-            rows_ref[...], gate_ref[:, columns], preferred_element_type=jnp.float32
-        )
-        upward = jnp.dot(rows_ref[...], up_ref[:, columns], preferred_element_type=jnp.float32)
-        act_ref[:, columns] = (gate_act / (1.0 + jnp.exp(-gate_act)) * upward).astype(
+            rows_ref[...], gate_ref[:, at : at + step], preferred_element_type=jnp.float32
+        )
+        upward = jnp.dot(
+            rows_ref[...], up_ref[:, at : at + step], preferred_element_type=jnp.float32
+        )
+        act_ref[:, at : at + step] = (gate_act / (1.0 + jnp.exp(-gate_act)) * upward).astype(
             act_ref.dtype
         )
-
     wide = 512
-
-    @pl.loop(0, feat_width // wide)
-    def _(index):
-        columns = pl.ds(pl.multiple_of(index * wide, wide), wide)
-        out_ref[:, columns] = jnp.dot(
-            act_ref[...], down_ref[:, columns], preferred_element_type=jnp.float32
+    for at in range(0, feat_width, wide):
+        out_ref[:, at : at + wide] = jnp.dot(
+            act_ref[...], down_ref[:, at : at + wide], preferred_element_type=jnp.float32
         ).astype(out_ref.dtype)
 
 
@@ -52,7 +71,7 @@
         in_specs=[vmem] * 4,
         out_specs=vmem,
         scratch_shapes=[pltpu.VMEM((count, hidden), jnp.bfloat16)],
-        compiler_params=pltpu.CompilerParams(vmem_limit_bytes=8 << 20),
+        compiler_params=pltpu.CompilerParams(vmem_limit_bytes=8<<20),
         cost_estimate=pl.CostEstimate(
             flops=6 * count * feat_width * hidden,
             bytes_accessed=6 * feat_width * hidden,
@@ -83,8 +102,30 @@
     )(*terms)
 
 
+def column_of(row):
+    shape = (row.shape[1], row.shape[1])
+    same = lax.broadcasted_iota(jnp.int32, shape, 0) == lax.broadcasted_iota(jnp.int32, shape, 1)
+    return jnp.sum(jnp.where(same, row, 0.0), -1, keepdims=True)
+
+
 def front_kernel(
     here_ref,
+    hidden_hbm,
+    query_hbm,
+    key_hbm,
+    value_hbm,
+    new_key_hbm,
+    new_value_hbm,
+    length_hbm,
+    ids_hbm,
+    probs_hbm,
+    gate_hbm,
+    residual_ref,
+    own_ref,
+    theirs_ref,
+    slots_ref,
+    weights_ref,
+    gate_ref,
     hidden_ref,
     query_ref,
     key_ref,
@@ -94,13 +135,34 @@
     length_ref,
     ids_ref,
     probs_ref,
-    residual_ref,
-    own_ref,
-    theirs_ref,
-    slots_ref,
-    weights_ref,
     normed_ref,
+    sems,
 ):
+    half = key_ref.shape[2] // 2
+    low, high = pl.ds(0, half), pl.ds(half, half)
+    pairs = [
+        (length_hbm, length_ref),
+        (query_hbm, query_ref),
+        (key_hbm.at[:, :, low], key_ref.at[:, :, low]),
+        (new_key_hbm, new_key_ref),
+        (value_hbm.at[:, :, low], value_ref.at[:, :, low]),
+        (new_value_hbm, new_value_ref),
+        (hidden_hbm, hidden_ref),
+        (key_hbm.at[:, :, high], key_ref.at[:, :, high]),
+        (value_hbm.at[:, :, high], value_ref.at[:, :, high]),
+        (ids_hbm, ids_ref),
+        (probs_hbm, probs_ref),
+        (gate_hbm, gate_ref),
+    ]
+    copies = [
+        pltpu.make_async_copy(source, target, sems.at[at])
+        for at, (source, target) in enumerate(pairs)
+    ]
+    for copy in copies[:-1]:
+        copy.start()
+    for copy in copies[:4]:
+        copy.wait()
+    copies[-1].start()
     rows, feat_width = hidden_ref.shape
     span = key_ref.shape[1]
     kv_width = key_ref.shape[2]
@@ -111,10 +173,14 @@
     column = lax.broadcasted_iota(jnp.int32, shape, 1)
     request = lax.broadcasted_iota(jnp.int32, shape, 0) & (rows - 1)
     first = request * span
-    limit = first + jnp.concatenate([length_ref[...]] * group, 0)
+    lengths = column_of(length_ref[...].astype(jnp.float32)).astype(jnp.int32)
+    limit = first + jnp.concatenate([lengths] * group, 0)
     valid = (column >= first) & (column < limit)
     total = jnp.zeros((rows, 1), jnp.float32)
     for head in range(kv_heads):
+        if head * 2 == kv_heads:
+            copies[7].wait()
+            copies[8].wait()
         lanes = pl.ds(head * HEAD, HEAD)
         wanted = [head * group + member for member in range(group)]
         query = jnp.concatenate([query_ref[:, q * HEAD : (q + 1) * HEAD] for q in wanted], 0)
@@ -134,6 +200,9 @@
         inverse = 1.0 / (jnp.sum(powers, -1, keepdims=True) + own_power)
         attention = (powers * inverse).astype(jnp.bfloat16)
         own_weight = (own_power * inverse).astype(jnp.bfloat16).astype(jnp.float32)
+        if head == 0:
+            for copy in copies[4:7]:
+                copy.wait()
         values = value_ref[:, :, lanes].reshape(rows * span, HEAD)
         mixed = jnp.dot(attention, values, preferred_element_type=jnp.float32)
         new_value = jnp.concatenate([new_value_ref[:, lanes].astype(jnp.float32)] * group, 0)
@@ -156,30 +225,32 @@
         centered = residual_ref[:, at : at + wide] - centre
         normed_ref[:, at : at + wide] = (centered * inverse).astype(jnp.bfloat16)
 
+    copies[9].wait()
+    copies[10].wait()
     here = here_ref[0]
-    mix = probs_ref[...] / jnp.sum(probs_ref[...], -1, keepdims=True)
-    below = (
+    mix = probs_ref[...] / jnp.sum(probs_ref[...], 0, keepdims=True)
+    above = (
         lax.broadcasted_iota(jnp.int32, (rows, rows), 0)
-        > lax.broadcasted_iota(jnp.int32, (rows, rows), 1)
+        < lax.broadcasted_iota(jnp.int32, (rows, rows), 1)
     ).astype(jnp.float32)
     cap = own_ref.shape[0]
-    slot = lax.broadcasted_iota(jnp.int32, (rows, cap), 1).astype(jnp.float32)
+    slot = lax.broadcasted_iota(jnp.int32, (cap, rows), 0).astype(jnp.float32)
     for place, label in enumerate((here, 1 - here)):
         match = ids_ref[...] == label
-        weights_ref[:, place : place + 1] = jnp.sum(jnp.where(match, mix, 0.0), -1, keepdims=True)
-        chosen = jnp.max(jnp.where(match, 1.0, 0.0), -1, keepdims=True)
+        weights_ref[:, place : place + 1] = column_of(
+            jnp.sum(jnp.where(match, mix, 0.0), 0, keepdims=True)
+        )
+        chosen = jnp.max(jnp.where(match, 1.0, 0.0), 0, keepdims=True)
         rank = jnp.dot(
-            below, jnp.broadcast_to(chosen, (rows, cap)), preferred_element_type=jnp.float32
+            jnp.broadcast_to(chosen, (cap, rows)), above, preferred_element_type=jnp.float32
         )
         picks = jnp.where(rank == slot, chosen, 0.0)
-        slots_ref[:, place * cap : (place + 1) * cap] = picks
+        slots_ref[place * cap : (place + 1) * cap, :] = picks
         out_ref = (own_ref, theirs_ref)[place]
-        out_ref[...] = lax.dot_general(
-            picks.astype(jnp.bfloat16),
-            normed_ref[...],
-            (((0,), (0,)), ((), ())),
-            preferred_element_type=jnp.float32,
+        out_ref[...] = jnp.dot(
+            picks.astype(jnp.bfloat16), normed_ref[...], preferred_element_type=jnp.float32
         ).astype(jnp.bfloat16)
+    copies[-1].wait()
 
 
 def tail_kernel(
@@ -193,9 +264,9 @@
     ).astype(jnp.bfloat16)
     result = residual_ref[...]
     for place, block in enumerate((own, back_ref[...])):
-        picks = slots_ref[:, place * cap : (place + 1) * cap].astype(jnp.bfloat16)
-        result = result + weights_ref[:, place : place + 1] * jnp.dot(
-            picks, block, preferred_element_type=jnp.float32
+        picks = slots_ref[place * cap : (place + 1) * cap, :].astype(jnp.bfloat16)
+        result = result + weights_ref[:, place : place + 1] * lax.dot_general(
+            picks, block, (((0,), (0,)), ((), ())), preferred_element_type=jnp.float32
         )
     out_ref[...] = result
 
@@ -219,39 +290,48 @@
     cap_slots = row_count // 2
     vmem = pl.BlockSpec(memory_space=pltpu.VMEM)
     here = lax.axis_index("expert").astype(jnp.int32).reshape(1)
-    residual, own, theirs, slots, weights = pl.pallas_call(
-        front_kernel,
-        out_shape=(
-            jax.ShapeDtypeStruct((row_count, feat_width), jnp.float32),
-            jax.ShapeDtypeStruct((cap_slots, feat_width), jnp.bfloat16),
-            jax.ShapeDtypeStruct((cap_slots, feat_width), jnp.bfloat16),
-            jax.ShapeDtypeStruct((row_count, 2 * cap_slots), jnp.float32),
-            jax.ShapeDtypeStruct((row_count, 2), jnp.float32),
-        ),
-        in_specs=[pl.BlockSpec(memory_space=pltpu.SMEM)] + [vmem] * 9,
-        out_specs=(vmem,) * 5,
-        scratch_shapes=[pltpu.VMEM((row_count, feat_width), jnp.bfloat16)],
-        compiler_params=pltpu.CompilerParams(vmem_limit_bytes=16 << 20),
-        cost_estimate=pl.CostEstimate(
-            flops=10**9, bytes_accessed=40 * 10**6, transcendentals=10**6
-        ),
-    )(
-        here,
+    arrays = (
         hidden_in,
         queries,
         cache_keys,
         cache_values,
         new_keys,
         new_values,
-        lengths.reshape(row_count, 1),
-        expert_ids,
-        gate_probs,
-    )
+        lengths.reshape(1, row_count),
+        expert_ids.T,
+        gate_probs.T,
+        w_gate[0],
+    )
+    residual, own, theirs, slots, weights, gate = pl.pallas_call(
+        front_kernel,
+        out_shape=(
+            jax.ShapeDtypeStruct((row_count, feat_width), jnp.float32),
+            jax.ShapeDtypeStruct((cap_slots, feat_width), jnp.bfloat16),
+            jax.ShapeDtypeStruct((cap_slots, feat_width), jnp.bfloat16),
+            jax.ShapeDtypeStruct((2 * cap_slots, row_count), jnp.float32),
+            jax.ShapeDtypeStruct((row_count, 2), jnp.float32),
+            pltpu.VMEM(w_gate.shape[1:], w_gate.dtype),
+        ),
+        in_specs=[pl.BlockSpec(memory_space=pltpu.SMEM)]
+        + [pl.BlockSpec(memory_space=pltpu.HBM)] * len(arrays),
+        out_specs=(vmem,) * 6,
+        scratch_shapes=[pltpu.VMEM(array.shape, array.dtype) for array in arrays[:-1]]
+        + [
+            pltpu.VMEM((row_count, feat_width), jnp.bfloat16),
+            pltpu.SemaphoreType.DMA((len(arrays) + 2,)),
+        ],
+        compiler_params=pltpu.CompilerParams(vmem_limit_bytes=16<<20),
+        cost_estimate=pl.CostEstimate(
+            flops=10**9, bytes_accessed=40 * 10**6, transcendentals=10**6
+        ),
+    )(here, *[in_hbm(array) for array in arrays])
 
     count = lax.axis_size("attn")
     ring = ring_of(count)
     right = [(ring[i], ring[(i + 1) % count]) for i in range(count)]
     left = [(b, a) for a, b in right]
+    right_two = [(ring[i], ring[(i + 2) % count]) for i in range(count)]
+    left_two = [(b, a) for a, b in right_two]
     swap = [(0, 1), (1, 0)]
 
     def go_right(block):
@@ -263,18 +343,21 @@
     half = count // 2
     theirs = lax.ppermute(theirs, "expert", swap)
     own_r, own_l, theirs_r, theirs_l = [own], [own], [theirs], [theirs]
-    for step in range(1, half + 1):
+    for step in range(1, half):
         own_r.append(go_right(own_r[-1]))
+        own_l.append(go_left(own_l[-1]))
         theirs_l.append(go_left(theirs_l[-1]))
-        if step < half:
-            own_l.append(go_left(own_l[-1]))
-            theirs_r.append(go_right(theirs_r[-1]))
-
+        theirs_r.append(go_right(theirs_r[-1]))
+    own_r.append(lax.ppermute(own_r[half - 2], "attn", right_two))
+    theirs_l.append(lax.ppermute(theirs_l[half - 2], "attn", left_two))
+
+    up = load(w_up[0], own_l[half - 1], 1<<20)
+    down = load(w_down[0], theirs_r[half - 1], 1<<20)
     blocks = [own, theirs]
     for step in range(1, half):
         blocks += [own_r[step], own_l[step], theirs_r[step], theirs_l[step]]
     blocks += [own_r[half], theirs_l[half]]
-    share = experts(jnp.concatenate(blocks), w_gate[0], w_up[0], w_down[0]).reshape(len(blocks), cap_slots, feat_width)
+    share = experts(jnp.concatenate(blocks), gate, up, down).reshape(len(blocks), cap_slots, feat_width)
     own_share = {0: share[0], half: share[-2]}
     theirs_share = {0: share[1], -half: share[-1]}
     for step in range(1, half):
@@ -282,16 +365,24 @@
         own_share[-step], own_share[step] = share[at], share[at + 1]
         theirs_share[-step], theirs_share[step] = share[at + 2], share[at + 3]
 
-    own_from_l = own_share[half]
-    theirs_from_r = theirs_share[-half]
+    own_from_l = add(
+        lax.ppermute(own_share[half], "attn", right_two),
+        go_right(own_share[half - 1]),
+        own_share[half - 2],
+    )
+    theirs_from_r = add(
+        lax.ppermute(theirs_share[-half], "attn", left_two),
+        go_left(theirs_share[1 - half]),
+        theirs_share[2 - half],
+    )
     own_from_r = own_share[1 - half]
     theirs_from_l = theirs_share[half - 1]
-    for step in range(half - 1, 0, -1):
-        own_from_l = add(go_right(own_from_l), own_share[step])
-        theirs_from_r = add(go_left(theirs_from_r), theirs_share[-step])
-        if step > 1:
-            own_from_r = add(go_left(own_from_r), own_share[1 - step])
-            theirs_from_l = add(go_right(theirs_from_l), theirs_share[step - 1])
+    for step in range(half - 2, 0, -1):
+        own_from_r = add(go_left(own_from_r), own_share[-step])
+        theirs_from_l = add(go_right(theirs_from_l), theirs_share[step])
+        if step < half - 2:
+            own_from_l = add(go_right(own_from_l), own_share[step])
+            theirs_from_r = add(go_left(theirs_from_r), theirs_share[-step])
     theirs_total = add(
         theirs_share[0], go_left(theirs_from_r), go_right(theirs_from_l)
     )

time: 82.1 us -> 68.4 us (0.83)
  local copies, waits for them, and re-layouts: 20.1 us -> 0.25 us
  Pallas kernels: 12.3 us -> 19.1 us
  waiting for transfers between devices: 18.2 us -> 17.3 us
    unnamed x35 -> x15, local copies, waits for them, and re-layouts: 19.2 us -> 0.12 us
    ppermute x14 -> x12, starting transfers between devices: 22.8 us -> 12.1 us  [go_right(): return lax.ppermute(block, 'attn', right)]
    pallas_call x0 -> x2, Pallas kernels: none -> 7.38 us  [load(): pl.pallas_call(load_kernel, out_shape=pltpu.VMEM(weights.shape, weights.d...]
    ppermute x0 -> x4, starting transfers between devices: none -> 5.89 us  [the longest x1 2.2 us: body(): lax.ppermute(theirs_share[-half], 'attn', left_two)]
    ppermute x14 -> x12, starting transfers between devices: 7.94 us -> 13.4 us  [go_left(): return lax.ppermute(block, 'attn', left)]
    ppermute x14 -> x12, waiting for transfers between devices: 11.8 us -> 7.67 us  [go_left(): return lax.ppermute(block, 'attn', left)]
    pallas_call x1, Pallas kernels: 6.52 us -> 4.05 us  [experts(): pl.pallas_call(experts_kernel, out_shape=jax.ShapeDtypeStruct((count, fea...]
    ppermute x0 -> x4, waiting for transfers between devices: none -> 2.14 us  [the longest x1 1.93 us: body(): lax.ppermute(theirs_share[-half], 'attn', left_two)]
  transfers between devices with their start and end apart: 30 -> 30, of which waited for: 15 -> 14; matrix products, arithmetic and copies ran while one was open for 0% -> 0% of each run, Pallas kernels for 0% -> 11%
where the time goes in v3:
time: 68.4 us; the launch traced here: 68.2 us
  starting transfers between devices  31.4 us (46%)
  Pallas kernels  19.1 us (28%)
  waiting for transfers between devices  17.3 us (25%)
    ppermute x12, starting transfers between devices, go_left(): return lax.ppermute(block, 'attn', left)  13.4 us
    ppermute x12, starting transfers between devices, go_right(): return lax.ppermute(block, 'attn', right)  12.1 us
    ppermute x12, waiting for transfers between devices, go_left(): return lax.ppermute(block, 'attn', left)  7.67 us
    pallas_call x2, Pallas kernels, load(): pl.pallas_call(load_kernel, out_shape=pltpu.VMEM(weights.shape, weights.d...  7.38 us
    pallas_call x1, Pallas kernels, body(): pl.pallas_call(front_kernel, out_shape=(jax.ShapeDtypeStruct((row_count,...  6.3 us
    ppermute x12, waiting for transfers between devices, go_right(): return lax.ppermute(block, 'attn', right)  6.15 us
    pallas_call x1, Pallas kernels, experts(): pl.pallas_call(experts_kernel, out_shape=jax.ShapeDtypeStruct((count, fea...  4.05 us
    ppermute x1, starting transfers between devices, body(): lax.ppermute(theirs_share[-half], 'attn', left_two)  2.2 us
  transfers between devices with their start and end apart: 30, of which 14 were waited for; matrix products, arithmetic and copies ran while one was open for 0% of the time, Pallas kernels for 11%

profile of v3, /device:TPU:0, one launch (start us, length us, event | category | flops | bytes accessed | tf_op | source)
XLA Modules:
  0.0 68.2 jit_solution(12979267839456384605)
XLA Ops:
  0.0 6.3 %shard_map.118 = (f32[16,6144]{1,0:T(8,128)S(1)}, bf16[8,6144]{1,0:T(8,128)(2,1)S(1)}, bf16[8,6144]{1,0:T(8,128)(2,1)S(1)}, f32[16,16]{1,0:T(8,128)S(1)}, f32[16...) custom-call(s32[1]{0:T(128)} %bitcast.here_ref, bf16[16,6144]{1,0:T(8,128)(2,1)} %hidden_hbm.1, bf16[16,6144]{1,0:T(8,128)(2,1)} %query_hbm.1, ...), custom_call_target="tpu_custom_call" | custom-call | flops 1000000000 | bytes 40000000 | tf_op jit(solution)/shard_map/pallas_call | solution.py:305
  6.3 3.0 %collective-permute-start.2 = (bf16[8,6144]{1,0:T(8,128)(2,1)S(1)}, bf16[8,6144]{1,0:T(8,128)(2,1)S(1)}, u32[]{:S(2)}, u32[]{:S(2)}) collective-permute-start(bf16[8,6144]{1,0:T(8,128)(2,1)S(1)} %get-tuple-element.14), channel_id=1, source_target_pairs={{4,0},{8,4},{12,8},{14,12},{10,14},{6,10},{2,6},{0,2},{5,1},{9,5},... | collective-permute-start | bytes 294920 | tf_op jit(solution)/shard_map/ppermute | solution.py:341
  9.5 1.3 %collective-permute-done = bf16[8,6144]{1,0:T(8,128)(2,1)S(1)} collective-permute-done((bf16[8,6144]{1,0:T(8,128)(2,1)S(1)}, bf16[8,6144]{1,0:T(8,128)(2,1)S(1)}, u32[]{:S(2)}, u32[]{:S(2)}) %collective-permute-start) | collective-permute-done | bytes 98336 | tf_op jit(solution)/shard_map/ppermute | solution.py:344
  10.7 1.9 %collective-permute-start.4 = (bf16[8,6144]{1,0:T(8,128)(2,1)S(1)}, bf16[8,6144]{1,0:T(8,128)(2,1)S(1)}, u32[]{:S(2)}, u32[]{:S(2)}) collective-permute-start(bf16[8,6144]{1,0:T(8,128)(2,1)S(1)} %collective-permute-done), channel_id=1, source_target_pairs={{4,0},{8,4},{12,8},{14,12},{10,14},{6,10},{2,6},{0,2},{5,1},{9,5},... | collective-permute-start | bytes 294920 | tf_op jit(solution)/shard_map/ppermute | solution.py:341
  12.8 1.9 %collective-permute-start.6 = (bf16[8,6144]{1,0:T(8,128)(2,1)S(1)}, bf16[8,6144]{1,0:T(8,128)(2,1)S(1)}, u32[]{:S(2)}, u32[]{:S(2)}) collective-permute-start(bf16[8,6144]{1,0:T(8,128)(2,1)S(1)} %collective-permute-done.2), channel_id=1, source_target_pairs={{4,0},{8,4},{12,8},{14,12},{10,14},{6,10},{2,6},{0,2},{5,1},{9,5},... | collective-permute-start | bytes 294920 | tf_op jit(solution)/shard_map/ppermute | solution.py:341
  14.8 4.5 %collective-permute-done.5 = bf16[8,6144]{1,0:T(8,128)(2,1)S(1)} collective-permute-done((bf16[8,6144]{1,0:T(8,128)(2,1)S(1)}, bf16[8,6144]{1,0:T(8,128)(2,1)S(1)}, u32[]{:S(2)}, u32[]{:S(2)}) %collective-permute-start.5) | collective-permute-done | bytes 98336 | tf_op jit(solution)/shard_map/ppermute | solution.py:338
  19.4 1.5 %collective-permute-start.13 = (bf16[8,6144]{1,0:T(8,128)(2,1)S(1)}, bf16[8,6144]{1,0:T(8,128)(2,1)S(1)}, u32[]{:S(2)}, u32[]{:S(2)}) collective-permute-start(bf16[8,6144]{1,0:T(8,128)(2,1)S(1)} %collective-permute-done.5), channel_id=1, source_target_pairs={{0,8},{4,12},{8,14},{12,10},{14,6},{10,2},{6,0},{2,4},{1,9},{5,13}... | collective-permute-start | bytes 294920 | tf_op jit(solution)/shard_map/ppermute | solution.py:351
  20.9 1.6 %collective-permute-start.9 = (bf16[8,6144]{1,0:T(8,128)(2,1)S(1)}, bf16[8,6144]{1,0:T(8,128)(2,1)S(1)}, u32[]{:S(2)}, u32[]{:S(2)}) collective-permute-start(bf16[8,6144]{1,0:T(8,128)(2,1)S(1)} %collective-permute-done.5), channel_id=1, source_target_pairs={{0,4},{4,8},{8,12},{12,14},{14,10},{10,6},{6,2},{2,0},{1,5},{5,9},... | collective-permute-start | bytes 294920 | tf_op jit(solution)/shard_map/ppermute | solution.py:338
  22.9 1.6 %collective-permute-start.7 = (bf16[8,6144]{1,0:T(8,128)(2,1)S(1)}, bf16[8,6144]{1,0:T(8,128)(2,1)S(1)}, u32[]{:S(2)}, u32[]{:S(2)}) collective-permute-start(bf16[8,6144]{1,0:T(8,128)(2,1)S(1)} %collective-permute-done.3), channel_id=1, source_target_pairs={{0,4},{4,8},{8,12},{12,14},{14,10},{10,6},{6,2},{2,0},{1,5},{5,9},... | collective-permute-start | bytes 294920 | tf_op jit(solution)/shard_map/ppermute | solution.py:338
  25.0 2.1 %collective-permute-done.8 = bf16[8,6144]{1,0:T(8,128)(2,1)S(1)} collective-permute-done((bf16[8,6144]{1,0:T(8,128)(2,1)S(1)}, bf16[8,6144]{1,0:T(8,128)(2,1)S(1)}, u32[]{:S(2)}, u32[]{:S(2)}) %collective-permute-start.8) | collective-permute-done | bytes 98336 | tf_op jit(solution)/shard_map/ppermute | solution.py:341
  27.2 0.9 %collective-permute-start.14 = (bf16[8,6144]{1,0:T(8,128)(2,1)S(1)}, bf16[8,6144]{1,0:T(8,128)(2,1)S(1)}, u32[]{:S(2)}, u32[]{:S(2)}) collective-permute-start(bf16[8,6144]{1,0:T(8,128)(2,1)S(1)} %collective-permute-done.8), channel_id=1, source_target_pairs={{8,0},{12,4},{14,8},{10,12},{6,14},{2,10},{0,6},{4,2},{9,1},{13,5}... | collective-permute-start | bytes 294920 | tf_op jit(solution)/shard_map/ppermute | solution.py:352
  28.3 2.7 %collective-permute-start.12 = (bf16[8,6144]{1,0:T(8,128)(2,1)S(1)}, bf16[8,6144]{1,0:T(8,128)(2,1)S(1)}, u32[]{:S(2)}, u32[]{:S(2)}) collective-permute-start(bf16[8,6144]{1,0:T(8,128)(2,1)S(1)} %collective-permute-done.8), channel_id=1, source_target_pairs={{4,0},{8,4},{12,8},{14,12},{10,14},{6,10},{2,6},{0,2},{5,1},{9,5},... | collective-permute-start | bytes 294920 | tf_op jit(solution)/shard_map/ppermute | solution.py:341
  31.1 3.7 %shard_map.119.up_ref = bf16[6144,768]{1,0:T(8,128)(2,1)S(1)} custom-call(bf16[8,6144]{1,0:T(8,128)(2,1)S(1)} %collective-permute-done.10.after_ref, bf16[6144,768]{1,0:T(8,128)(2,1)} %bitcast.8), custom_call_target="tpu_custom_call" | custom-call | bytes 9437184 | tf_op jit(solution)/shard_map/pallas_call | solution.py:30
  34.8 0.9 %collective-permute-done.11.after_ref = bf16[8,6144]{1,0:T(8,128)(2,1)S(1)} collective-permute-done((bf16[8,6144]{1,0:T(8,128)(2,1)S(1)}, bf16[8,6144]{1,0:T(8,128)(2,1)S(1)}, u32[]{:S(2)}, u32[]{:S(2)}) %collective-permute-start.11) | collective-permute-done | bytes 98336 | tf_op jit(solution)/shard_map/ppermute | solution.py:338
  35.7 3.7 %shard_map.120.down_ref = bf16[768,6144]{1,0:T(8,128)(2,1)S(1)} custom-call(bf16[8,6144]{1,0:T(8,128)(2,1)S(1)} %collective-permute-done.11.after_ref, bf16[768,6144]{1,0:T(8,128)(2,1)} %bitcast.9), custom_call_target="tpu_custom_call" | custom-call | bytes 9437184 | tf_op jit(solution)/shard_map/pallas_call | solution.py:30
  39.4 4.1 %shard_map.121 = bf16[128,6144]{1,0:T(8,128)(2,1)S(1)} custom-call(bf16[128,6144]{1,0:T(8,128)(2,1)S(1)} %constant_dynamic-update-slice_fusion.rows_ref, bf16[6144,768]{1,0:T(8,128)(2,1)S(1)} %get-tuple-element.16.gate_ref, bf16[6144,768]{1,0:T(8,128)(2,1)S(1)} %shard_map.119.up_ref, bf16[768,6144]{1,0:T(8,128)(2,1)S(1)} %shard_map.120.down_ref), custom_call_target="tpu_custom_call" | custom-call | flops 3623878656 | bytes 28311552 | tf_op jit(solution)/shard_map/pallas_call | solution.py:68
  43.6 1.0 %collective-permute-start.26 = (bf16[8,6144]{1,0:T(8,128)(2,1)S(1)}, bf16[8,6144]{1,0:T(8,128)(2,1)S(1)}, u32[]{:S(2)}, u32[]{:S(2)}) collective-permute-start(bf16[8,6144]{1,0:T(8,128)(2,1)S(1)} %get-tuple-element.19), channel_id=1, source_target_pairs={{0,4},{4,8},{8,12},{12,14},{14,10},{10,6},{6,2},{2,0},{1,5},{5,9},... | collective-permute-start | bytes 294920 | tf_op jit(solution)/shard_map/ppermute | solution.py:338
  44.6 1.1 %collective-permute-start.23 = (bf16[8,6144]{1,0:T(8,128)(2,1)S(1)}, bf16[8,6144]{1,0:T(8,128)(2,1)S(1)}, u32[]{:S(2)}, u32[]{:S(2)}) collective-permute-start(bf16[8,6144]{1,0:T(8,128)(2,1)S(1)} %get-tuple-element.22), channel_id=1, source_target_pairs={{4,0},{8,4},{12,8},{14,12},{10,14},{6,10},{2,6},{0,2},{5,1},{9,5},... | collective-permute-start | bytes 294920 | tf_op jit(solution)/shard_map/ppermute | solution.py:341
  45.7 2.2 %collective-permute-start.22 = (bf16[8,6144]{1,0:T(8,128)(2,1)S(1)}, bf16[8,6144]{1,0:T(8,128)(2,1)S(1)}, u32[]{:S(2)}, u32[]{:S(2)}) collective-permute-start(bf16[8,6144]{1,0:T(8,128)(2,1)S(1)} %get-tuple-element.23), channel_id=1, source_target_pairs={{8,0},{12,4},{14,8},{10,12},{6,14},{2,10},{0,6},{4,2},{9,1},{13,5}... | collective-permute-start | bytes 294920 | tf_op jit(solution)/shard_map/ppermute | solution.py:374
  47.9 1.1 %collective-permute-start.19 = (bf16[8,6144]{1,0:T(8,128)(2,1)S(1)}, bf16[8,6144]{1,0:T(8,128)(2,1)S(1)}, u32[]{:S(2)}, u32[]{:S(2)}) collective-permute-start(bf16[8,6144]{1,0:T(8,128)(2,1)S(1)} %get-tuple-element.27), channel_id=1, source_target_pairs={{4,0},{8,4},{12,8},{14,12},{10,14},{6,10},{2,6},{0,2},{5,1},{9,5},... | collective-permute-start | bytes 294920 | tf_op jit(solution)/shard_map/ppermute | solution.py:341
  49.0 0.9 %collective-permute-start.16 = (bf16[8,6144]{1,0:T(8,128)(2,1)S(1)}, bf16[8,6144]{1,0:T(8,128)(2,1)S(1)}, u32[]{:S(2)}, u32[]{:S(2)}) collective-permute-start(bf16[8,6144]{1,0:T(8,128)(2,1)S(1)} %get-tuple-element.30), channel_id=1, source_target_pairs={{0,4},{4,8},{8,12},{12,14},{14,10},{10,6},{6,2},{2,0},{1,5},{5,9},... | collective-permute-start | bytes 294920 | tf_op jit(solution)/shard_map/ppermute | solution.py:338
  49.9 1.2 %collective-permute-start.15 = (bf16[8,6144]{1,0:T(8,128)(2,1)S(1)}, bf16[8,6144]{1,0:T(8,128)(2,1)S(1)}, u32[]{:S(2)}, u32[]{:S(2)}) collective-permute-start(bf16[8,6144]{1,0:T(8,128)(2,1)S(1)} %get-tuple-element.31), channel_id=1, source_target_pairs={{0,8},{4,12},{8,14},{12,10},{14,6},{10,2},{6,0},{2,4},{1,9},{5,13}... | collective-permute-start | bytes 294920 | tf_op jit(solution)/shard_map/ppermute | solution.py:369
  51.2 1.3 %collective-permute-start.27 = (bf16[8,6144]{1,0:T(8,128)(2,1)S(1)}, bf16[8,6144]{1,0:T(8,128)(2,1)S(1)}, u32[]{:S(2)}, u32[]{:S(2)}) collective-permute-start(bf16[8,6144]{1,0:T(8,128)(2,1)S(1)} %shard_map.128), channel_id=1, source_target_pairs={{0,4},{4,8},{8,12},{12,14},{14,10},{10,6},{6,2},{2,0},{1,5},{5,9},... | collective-permute-start | bytes 294920 | tf_op jit(solution)/shard_map/ppermute | solution.py:338
  52.5 1.9 %collective-permute-done.22.refs_0_ = bf16[8,6144]{1,0:T(8,128)(2,1)S(1)} collective-permute-done((bf16[8,6144]{1,0:T(8,128)(2,1)S(1)}, bf16[8,6144]{1,0:T(8,128)(2,1)S(1)}, u32[]{:S(2)}, u32[]{:S(2)}) %collective-permute-start.22) | collective-permute-done | bytes 98336 | tf_op jit(solution)/shard_map/ppermute | solution.py:374
  54.5 0.8 %collective-permute-done.19.refs_0_ = bf16[8,6144]{1,0:T(8,128)(2,1)S(1)} collective-permute-done((bf16[8,6144]{1,0:T(8,128)(2,1)S(1)}, bf16[8,6144]{1,0:T(8,128)(2,1)S(1)}, u32[]{:S(2)}, u32[]{:S(2)}) %collective-permute-start.19) | collective-permute-done | bytes 98336 | tf_op jit(solution)/shard_map/ppermute | solution.py:341
  55.9 2.5 %collective-permute-start.17 = (bf16[8,6144]{1,0:T(8,128)(2,1)S(1)}, bf16[8,6144]{1,0:T(8,128)(2,1)S(1)}, u32[]{:S(2)}, u32[]{:S(2)}) collective-permute-start(bf16[8,6144]{1,0:T(8,128)(2,1)S(1)} %shard_map.122), channel_id=1, source_target_pairs={{0,4},{4,8},{8,12},{12,14},{14,10},{10,6},{6,2},{2,0},{1,5},{5,9},... | collective-permute-start | bytes 294920 | tf_op jit(solution)/shard_map/ppermute | solution.py:338
  58.4 1.0 %collective-permute-start.28 = (bf16[8,6144]{1,0:T(8,128)(2,1)S(1)}, bf16[8,6144]{1,0:T(8,128)(2,1)S(1)}, u32[]{:S(2)}, u32[]{:S(2)}) collective-permute-start(bf16[8,6144]{1,0:T(8,128)(2,1)S(1)} %shard_map.129), channel_id=1, source_target_pairs={{0,4},{4,8},{8,12},{12,14},{14,10},{10,6},{6,2},{2,0},{1,5},{5,9},... | collective-permute-start | bytes 294920 | tf_op jit(solution)/shard_map/ppermute | solution.py:338
  59.4 0.7 %collective-permute-done.24.refs_0_ = bf16[8,6144]{1,0:T(8,128)(2,1)S(1)} collective-permute-done((bf16[8,6144]{1,0:T(8,128)(2,1)S(1)}, bf16[8,6144]{1,0:T(8,128)(2,1)S(1)}, u32[]{:S(2)}, u32[]{:S(2)}) %collective-permute-start.24) | collective-permute-done | bytes 98336 | tf_op jit(solution)/shard_map/ppermute | solution.py:341
  60.6 1.6 %collective-permute-done.20.refs_0_ = bf16[8,6144]{1,0:T(8,128)(2,1)S(1)} collective-permute-done((bf16[8,6144]{1,0:T(8,128)(2,1)S(1)}, bf16[8,6144]{1,0:T(8,128)(2,1)S(1)}, u32[]{:S(2)}, u32[]{:S(2)}) %collective-permute-start.20) | collective-permute-done | bytes 98336 | tf_op jit(solution)/shard_map/ppermute | solution.py:341
  62.5 1.8 %collective-permute-start.18 = (bf16[8,6144]{1,0:T(8,128)(2,1)S(1)}, bf16[8,6144]{1,0:T(8,128)(2,1)S(1)}, u32[]{:S(2)}, u32[]{:S(2)}) collective-permute-start(bf16[8,6144]{1,0:T(8,128)(2,1)S(1)} %shard_map.123), channel_id=1, source_target_pairs={{0,4},{4,8},{8,12},{12,14},{14,10},{10,6},{6,2},{2,0},{1,5},{5,9},... | collective-permute-start | bytes 294920 | tf_op jit(solution)/shard_map/ppermute | solution.py:338
  65.0 1.9 %collective-permute-done.21.third_ref = bf16[8,6144]{1,0:T(8,128)(2,1)S(1)} collective-permute-done((bf16[8,6144]{1,0:T(8,128)(2,1)S(1)}, bf16[8,6144]{1,0:T(8,128)(2,1)S(1)}, u32[]{:S(2)}, u32[]{:S(2)}) %collective-permute-start.21) | collective-permute-done | bytes 98336 | tf_op jit(solution)/shard_map/ppermute | solution.py:341
  67.2 1.0 %shard_map.131 = f32[16,6144]{1,0:T(8,128)} custom-call(f32[16,6144]{1,0:T(8,128)S(1)} %get-tuple-element.11.residual_ref, f32[16,16]{1,0:T(8,128)S(1)} %get-tuple-element.12.slots_ref, f32[16,2]{1,0:T(8,128)S(1)} %get-tuple-element.13.weights_ref, bf16[8,6144]{1,0:T(8,128)(2,1)S(1)} %get-tuple-element.32.first_ref, ...), custom_call_target="tpu_custom_call" | custom-call | tf_op jit(solution)/shard_map/pallas_call | solution.py:390
  (59 shorter events, 4.2 us)
Async XLA Ops:
  6.3 6.5 %collective-permute-start.2 = (bf16[8,6144]{1,0:T(8,128)(2,1)S(1)}, bf16[8,6144]{1,0:T(8,128)(2,1)S(1)}, u32[]{:S(2)}, u32[]{:S(2)}) collective-permute-start(bf16[8,6144]{1,0:T(8,128)(2,1)S(1)} %get-tuple-element.14), channel_id=1, source_target_pairs={{4,0},{8,4},{12,8},{14,12},{10,14},{6,10},{2,6},{0,2},{5,1},{9,5},... | collective-permute-start | bytes 294920 | tf_op jit(solution)/shard_map/ppermute | solution.py:341
  9.3 5.4 %collective-permute-start.1 = (bf16[8,6144]{1,0:T(8,128)(2,1)S(1)}, bf16[8,6144]{1,0:T(8,128)(2,1)S(1)}, u32[]{:S(2)}, u32[]{:S(2)}) collective-permute-start(bf16[8,6144]{1,0:T(8,128)(2,1)S(1)} %get-tuple-element.14), channel_id=1, source_target_pairs={{0,4},{4,8},{8,12},{12,14},{14,10},{10,6},{6,2},{2,0},{1,5},{5,9},... | collective-permute-start | bytes 294920 | tf_op jit(solution)/shard_map/ppermute | solution.py:338
  9.4 1.3 %collective-permute-start = (bf16[8,6144]{1,0:T(8,128)(2,1)S(1)}, bf16[8,6144]{1,0:T(8,128)(2,1)S(1)}, u32[]{:S(2)}, u32[]{:S(2)}) collective-permute-start(bf16[8,6144]{1,0:T(8,128)(2,1)S(1)} %get-tuple-element.15), channel_id=1, source_target_pairs={{0,1},{1,0},{2,3},{3,2},{4,5},{5,4},{6,7},{7,6},{8,9},{9,8},{10,11... | collective-permute-start | bytes 294920 | tf_op jit(solution)/shard_map/ppermute | solution.py:344
  10.7 11.7 %collective-permute-start.4 = (bf16[8,6144]{1,0:T(8,128)(2,1)S(1)}, bf16[8,6144]{1,0:T(8,128)(2,1)S(1)}, u32[]{:S(2)}, u32[]{:S(2)}) collective-permute-start(bf16[8,6144]{1,0:T(8,128)(2,1)S(1)} %collective-permute-done), channel_id=1, source_target_pairs={{4,0},{8,4},{12,8},{14,12},{10,14},{6,10},{2,6},{0,2},{5,1},{9,5},... | collective-permute-start | bytes 294920 | tf_op jit(solution)/shard_map/ppermute | solution.py:341
  12.7 10.3 %collective-permute-start.3 = (bf16[8,6144]{1,0:T(8,128)(2,1)S(1)}, bf16[8,6144]{1,0:T(8,128)(2,1)S(1)}, u32[]{:S(2)}, u32[]{:S(2)}) collective-permute-start(bf16[8,6144]{1,0:T(8,128)(2,1)S(1)} %collective-permute-done), channel_id=1, source_target_pairs={{0,4},{4,8},{8,12},{12,14},{14,10},{10,6},{6,2},{2,0},{1,5},{5,9},... | collective-permute-start | bytes 294920 | tf_op jit(solution)/shard_map/ppermute | solution.py:338
  12.8 11.7 %collective-permute-start.6 = (bf16[8,6144]{1,0:T(8,128)(2,1)S(1)}, bf16[8,6144]{1,0:T(8,128)(2,1)S(1)}, u32[]{:S(2)}, u32[]{:S(2)}) collective-permute-start(bf16[8,6144]{1,0:T(8,128)(2,1)S(1)} %collective-permute-done.2), channel_id=1, source_target_pairs={{4,0},{8,4},{12,8},{14,12},{10,14},{6,10},{2,6},{0,2},{5,1},{9,5},... | collective-permute-start | bytes 294920 | tf_op jit(solution)/shard_map/ppermute | solution.py:341
  14.7 4.7 %collective-permute-start.5 = (bf16[8,6144]{1,0:T(8,128)(2,1)S(1)}, bf16[8,6144]{1,0:T(8,128)(2,1)S(1)}, u32[]{:S(2)}, u32[]{:S(2)}) collective-permute-start(bf16[8,6144]{1,0:T(8,128)(2,1)S(1)} %collective-permute-done.1), channel_id=1, source_target_pairs={{0,4},{4,8},{8,12},{12,14},{14,10},{10,6},{6,2},{2,0},{1,5},{5,9},... | collective-permute-start | bytes 294920 | tf_op jit(solution)/shard_map/ppermute | solution.py:338
  19.4 16.3 %collective-permute-start.13 = (bf16[8,6144]{1,0:T(8,128)(2,1)S(1)}, bf16[8,6144]{1,0:T(8,128)(2,1)S(1)}, u32[]{:S(2)}, u32[]{:S(2)}) collective-permute-start(bf16[8,6144]{1,0:T(8,128)(2,1)S(1)} %collective-permute-done.5), channel_id=1, source_target_pairs={{0,8},{4,12},{8,14},{12,10},{14,6},{10,2},{6,0},{2,4},{1,9},{5,13}... | collective-permute-start | bytes 294920 | tf_op jit(solution)/shard_map/ppermute | solution.py:351
  20.9 10.1 %collective-permute-start.9 = (bf16[8,6144]{1,0:T(8,128)(2,1)S(1)}, bf16[8,6144]{1,0:T(8,128)(2,1)S(1)}, u32[]{:S(2)}, u32[]{:S(2)}) collective-permute-start(bf16[8,6144]{1,0:T(8,128)(2,1)S(1)} %collective-permute-done.5), channel_id=1, source_target_pairs={{0,4},{4,8},{8,12},{12,14},{14,10},{10,6},{6,2},{2,0},{1,5},{5,9},... | collective-permute-start | bytes 294920 | tf_op jit(solution)/shard_map/ppermute | solution.py:338
  22.5 4.7 %collective-permute-start.8 = (bf16[8,6144]{1,0:T(8,128)(2,1)S(1)}, bf16[8,6144]{1,0:T(8,128)(2,1)S(1)}, u32[]{:S(2)}, u32[]{:S(2)}) collective-permute-start(bf16[8,6144]{1,0:T(8,128)(2,1)S(1)} %collective-permute-done.4), channel_id=1, source_target_pairs={{4,0},{8,4},{12,8},{14,12},{10,14},{6,10},{2,6},{0,2},{5,1},{9,5},... | collective-permute-start | bytes 294920 | tf_op jit(solution)/shard_map/ppermute | solution.py:341
  22.9 5.3 %collective-permute-start.7 = (bf16[8,6144]{1,0:T(8,128)(2,1)S(1)}, bf16[8,6144]{1,0:T(8,128)(2,1)S(1)}, u32[]{:S(2)}, u32[]{:S(2)}) collective-permute-start(bf16[8,6144]{1,0:T(8,128)(2,1)S(1)} %collective-permute-done.3), channel_id=1, source_target_pairs={{0,4},{4,8},{8,12},{12,14},{14,10},{10,6},{6,2},{2,0},{1,5},{5,9},... | collective-permute-start | bytes 294920 | tf_op jit(solution)/shard_map/ppermute | solution.py:338
  24.5 6.5 %collective-permute-start.10 = (bf16[8,6144]{1,0:T(8,128)(2,1)S(1)}, bf16[8,6144]{1,0:T(8,128)(2,1)S(1)}, u32[]{:S(2)}, u32[]{:S(2)}) collective-permute-start(bf16[8,6144]{1,0:T(8,128)(2,1)S(1)} %collective-permute-done.6), channel_id=1, source_target_pairs={{4,0},{8,4},{12,8},{14,12},{10,14},{6,10},{2,6},{0,2},{5,1},{9,5},... | collective-permute-start | bytes 294920 | tf_op jit(solution)/shard_map/ppermute | solution.py:341
  27.2 12.2 %collective-permute-start.14 = (bf16[8,6144]{1,0:T(8,128)(2,1)S(1)}, bf16[8,6144]{1,0:T(8,128)(2,1)S(1)}, u32[]{:S(2)}, u32[]{:S(2)}) collective-permute-start(bf16[8,6144]{1,0:T(8,128)(2,1)S(1)} %collective-permute-done.8), channel_id=1, source_target_pairs={{8,0},{12,4},{14,8},{10,12},{6,14},{2,10},{0,6},{4,2},{9,1},{13,5}... | collective-permute-start | bytes 294920 | tf_op jit(solution)/shard_map/ppermute | solution.py:352
  28.3 7.4 %collective-permute-start.12 = (bf16[8,6144]{1,0:T(8,128)(2,1)S(1)}, bf16[8,6144]{1,0:T(8,128)(2,1)S(1)}, u32[]{:S(2)}, u32[]{:S(2)}) collective-permute-start(bf16[8,6144]{1,0:T(8,128)(2,1)S(1)} %collective-permute-done.8), channel_id=1, source_target_pairs={{4,0},{8,4},{12,8},{14,12},{10,14},{6,10},{2,6},{0,2},{5,1},{9,5},... | collective-permute-start | bytes 294920 | tf_op jit(solution)/shard_map/ppermute | solution.py:341
  31.0 4.7 %collective-permute-start.11 = (bf16[8,6144]{1,0:T(8,128)(2,1)S(1)}, bf16[8,6144]{1,0:T(8,128)(2,1)S(1)}, u32[]{:S(2)}, u32[]{:S(2)}) collective-permute-start(bf16[8,6144]{1,0:T(8,128)(2,1)S(1)} %collective-permute-done.7), channel_id=1, source_target_pairs={{0,4},{4,8},{8,12},{12,14},{14,10},{10,6},{6,2},{2,0},{1,5},{5,9},... | collective-permute-start | bytes 294920 | tf_op jit(solution)/shard_map/ppermute | solution.py:338
  43.6 6.3 %collective-permute-start.26 = (bf16[8,6144]{1,0:T(8,128)(2,1)S(1)}, bf16[8,6144]{1,0:T(8,128)(2,1)S(1)}, u32[]{:S(2)}, u32[]{:S(2)}) collective-permute-start(bf16[8,6144]{1,0:T(8,128)(2,1)S(1)} %get-tuple-element.19), channel_id=1, source_target_pairs={{0,4},{4,8},{8,12},{12,14},{14,10},{10,6},{6,2},{2,0},{1,5},{5,9},... | collective-permute-start | bytes 294920 | tf_op jit(solution)/shard_map/ppermute | solution.py:338
  44.6 6.6 %collective-permute-start.23 = (bf16[8,6144]{1,0:T(8,128)(2,1)S(1)}, bf16[8,6144]{1,0:T(8,128)(2,1)S(1)}, u32[]{:S(2)}, u32[]{:S(2)}) collective-permute-start(bf16[8,6144]{1,0:T(8,128)(2,1)S(1)} %get-tuple-element.22), channel_id=1, source_target_pairs={{4,0},{8,4},{12,8},{14,12},{10,14},{6,10},{2,6},{0,2},{5,1},{9,5},... | collective-permute-start | bytes 294920 | tf_op jit(solution)/shard_map/ppermute | solution.py:341
  45.7 8.7 %collective-permute-start.22 = (bf16[8,6144]{1,0:T(8,128)(2,1)S(1)}, bf16[8,6144]{1,0:T(8,128)(2,1)S(1)}, u32[]{:S(2)}, u32[]{:S(2)}) collective-permute-start(bf16[8,6144]{1,0:T(8,128)(2,1)S(1)} %get-tuple-element.23), channel_id=1, source_target_pairs={{8,0},{12,4},{14,8},{10,12},{6,14},{2,10},{0,6},{4,2},{9,1},{13,5}... | collective-permute-start | bytes 294920 | tf_op jit(solution)/shard_map/ppermute | solution.py:374
  47.9 7.4 %collective-permute-start.19 = (bf16[8,6144]{1,0:T(8,128)(2,1)S(1)}, bf16[8,6144]{1,0:T(8,128)(2,1)S(1)}, u32[]{:S(2)}, u32[]{:S(2)}) collective-permute-start(bf16[8,6144]{1,0:T(8,128)(2,1)S(1)} %get-tuple-element.27), channel_id=1, source_target_pairs={{4,0},{8,4},{12,8},{14,12},{10,14},{6,10},{2,6},{0,2},{5,1},{9,5},... | collective-permute-start | bytes 294920 | tf_op jit(solution)/shard_map/ppermute | solution.py:341
  49.0 6.6 %collective-permute-start.16 = (bf16[8,6144]{1,0:T(8,128)(2,1)S(1)}, bf16[8,6144]{1,0:T(8,128)(2,1)S(1)}, u32[]{:S(2)}, u32[]{:S(2)}) collective-permute-start(bf16[8,6144]{1,0:T(8,128)(2,1)S(1)} %get-tuple-element.30), channel_id=1, source_target_pairs={{0,4},{4,8},{8,12},{12,14},{14,10},{10,6},{6,2},{2,0},{1,5},{5,9},... | collective-permute-start | bytes 294920 | tf_op jit(solution)/shard_map/ppermute | solution.py:338
  49.9 5.9 %collective-permute-start.15 = (bf16[8,6144]{1,0:T(8,128)(2,1)S(1)}, bf16[8,6144]{1,0:T(8,128)(2,1)S(1)}, u32[]{:S(2)}, u32[]{:S(2)}) collective-permute-start(bf16[8,6144]{1,0:T(8,128)(2,1)S(1)} %get-tuple-element.31), channel_id=1, source_target_pairs={{0,8},{4,12},{8,14},{12,10},{14,6},{10,2},{6,0},{2,4},{1,9},{5,13}... | collective-permute-start | bytes 294920 | tf_op jit(solution)/shard_map/ppermute | solution.py:369
  51.2 7.2 %collective-permute-start.27 = (bf16[8,6144]{1,0:T(8,128)(2,1)S(1)}, bf16[8,6144]{1,0:T(8,128)(2,1)S(1)}, u32[]{:S(2)}, u32[]{:S(2)}) collective-permute-start(bf16[8,6144]{1,0:T(8,128)(2,1)S(1)} %shard_map.128), channel_id=1, source_target_pairs={{0,4},{4,8},{8,12},{12,14},{14,10},{10,6},{6,2},{2,0},{1,5},{5,9},... | collective-permute-start | bytes 294920 | tf_op jit(solution)/shard_map/ppermute | solution.py:338
  54.4 5.7 %collective-permute-start.24 = (bf16[8,6144]{1,0:T(8,128)(2,1)S(1)}, bf16[8,6144]{1,0:T(8,128)(2,1)S(1)}, u32[]{:S(2)}, u32[]{:S(2)}) collective-permute-start(bf16[8,6144]{1,0:T(8,128)(2,1)S(1)} %shard_map.126), channel_id=1, source_target_pairs={{4,0},{8,4},{12,8},{14,12},{10,14},{6,10},{2,6},{0,2},{5,1},{9,5},... | collective-permute-start | bytes 294920 | tf_op jit(solution)/shard_map/ppermute | solution.py:341
  55.4 6.8 %collective-permute-start.20 = (bf16[8,6144]{1,0:T(8,128)(2,1)S(1)}, bf16[8,6144]{1,0:T(8,128)(2,1)S(1)}, u32[]{:S(2)}, u32[]{:S(2)}) collective-permute-start(bf16[8,6144]{1,0:T(8,128)(2,1)S(1)} %shard_map.124), channel_id=1, source_target_pairs={{4,0},{8,4},{12,8},{14,12},{10,14},{6,10},{2,6},{0,2},{5,1},{9,5},... | collective-permute-start | bytes 294920 | tf_op jit(solution)/shard_map/ppermute | solution.py:341
  55.9 6.6 %collective-permute-start.17 = (bf16[8,6144]{1,0:T(8,128)(2,1)S(1)}, bf16[8,6144]{1,0:T(8,128)(2,1)S(1)}, u32[]{:S(2)}, u32[]{:S(2)}) collective-permute-start(bf16[8,6144]{1,0:T(8,128)(2,1)S(1)} %shard_map.122), channel_id=1, source_target_pairs={{0,4},{4,8},{8,12},{12,14},{14,10},{10,6},{6,2},{2,0},{1,5},{5,9},... | collective-permute-start | bytes 294920 | tf_op jit(solution)/shard_map/ppermute | solution.py:338
  58.4 5.9 %collective-permute-start.28 = (bf16[8,6144]{1,0:T(8,128)(2,1)S(1)}, bf16[8,6144]{1,0:T(8,128)(2,1)S(1)}, u32[]{:S(2)}, u32[]{:S(2)}) collective-permute-start(bf16[8,6144]{1,0:T(8,128)(2,1)S(1)} %shard_map.129), channel_id=1, source_target_pairs={{0,4},{4,8},{8,12},{12,14},{14,10},{10,6},{6,2},{2,0},{1,5},{5,9},... | collective-permute-start | bytes 294920 | tf_op jit(solution)/shard_map/ppermute | solution.py:338
  60.2 4.7 %collective-permute-start.25 = (bf16[8,6144]{1,0:T(8,128)(2,1)S(1)}, bf16[8,6144]{1,0:T(8,128)(2,1)S(1)}, u32[]{:S(2)}, u32[]{:S(2)}) collective-permute-start(bf16[8,6144]{1,0:T(8,128)(2,1)S(1)} %shard_map.127), channel_id=1, source_target_pairs={{4,0},{8,4},{12,8},{14,12},{10,14},{6,10},{2,6},{0,2},{5,1},{9,5},... | collective-permute-start | bytes 294920 | tf_op jit(solution)/shard_map/ppermute | solution.py:341
  62.2 4.7 %collective-permute-start.21 = (bf16[8,6144]{1,0:T(8,128)(2,1)S(1)}, bf16[8,6144]{1,0:T(8,128)(2,1)S(1)}, u32[]{:S(2)}, u32[]{:S(2)}) collective-permute-start(bf16[8,6144]{1,0:T(8,128)(2,1)S(1)} %shard_map.125), channel_id=1, source_target_pairs={{4,0},{8,4},{12,8},{14,12},{10,14},{6,10},{2,6},{0,2},{5,1},{9,5},... | collective-permute-start | bytes 294920 | tf_op jit(solution)/shard_map/ppermute | solution.py:341
  62.5 4.7 %collective-permute-start.18 = (bf16[8,6144]{1,0:T(8,128)(2,1)S(1)}, bf16[8,6144]{1,0:T(8,128)(2,1)S(1)}, u32[]{:S(2)}, u32[]{:S(2)}) collective-permute-start(bf16[8,6144]{1,0:T(8,128)(2,1)S(1)} %shard_map.123), channel_id=1, source_target_pairs={{0,4},{4,8},{8,12},{12,14},{14,10},{10,6},{6,2},{2,0},{1,5},{5,9},... | collective-permute-start | bytes 294920 | tf_op jit(solution)/shard_map/ppermute | solution.py:338
  64.9 2.3 %collective-permute-start.29 = (bf16[8,6144]{1,0:T(8,128)(2,1)S(1)}, bf16[8,6144]{1,0:T(8,128)(2,1)S(1)}, u32[]{:S(2)}, u32[]{:S(2)}) collective-permute-start(bf16[8,6144]{1,0:T(8,128)(2,1)S(1)} %shard_map.130), channel_id=1, source_target_pairs={{0,1},{1,0},{2,3},{3,2},{4,5},{5,4},{6,7},{7,6},{8,9},{9,8},{10,11... | collective-permute-start | bytes 294920 | tf_op jit(solution)/shard_map/ppermute | solution.py:389

commit v4 on v3

--- a/solution.py
+++ b/solution.py
@@ -16,68 +16,39 @@
     return list(range(count))
 
 
-def load_kernel(after_ref, source_ref, held_ref, sem):
-    copy = pltpu.make_async_copy(source_ref, held_ref, sem)
-    copy.start()
-    copy.wait()
-
-
 def in_hbm(array):
     return pltpu.with_memory_space_constraint(array, pltpu.HBM)
 
 
-def load(weights, after, room):
-    return pl.pallas_call(
-        load_kernel,
-        out_shape=pltpu.VMEM(weights.shape, weights.dtype),
-        in_specs=[pl.BlockSpec(memory_space=pl.ANY), pl.BlockSpec(memory_space=pltpu.HBM)],
-        out_specs=pl.BlockSpec(memory_space=pltpu.VMEM),
-        scratch_shapes=[pltpu.SemaphoreType.DMA],
-        compiler_params=pltpu.CompilerParams(vmem_limit_bytes=room),
-        cost_estimate=pl.CostEstimate(
-            flops=0, bytes_accessed=2 * weights.size, transcendentals=0
-        ),
-    )(after, in_hbm(weights))
-
-
-def experts_kernel(rows_ref, gate_ref, up_ref, down_ref, out_ref, act_ref):
-    feat_width = rows_ref.shape[1]
+def experts_kernel(rows_ref, gate_ref, upward_ref, act_ref):
     hidden = gate_ref.shape[1]
     step = math.gcd(hidden, 256)
     for at in range(0, hidden, step):
+        columns = slice(at, at + step)
         gate_act = jnp.dot(
-            rows_ref[...], gate_ref[:, at : at + step], preferred_element_type=jnp.float32
-        )
-        upward = jnp.dot(
-            rows_ref[...], up_ref[:, at : at + step], preferred_element_type=jnp.float32
-        )
-        act_ref[:, at : at + step] = (gate_act / (1.0 + jnp.exp(-gate_act)) * upward).astype(
-            act_ref.dtype
-        )
-    wide = 512
-    for at in range(0, feat_width, wide):
-        out_ref[:, at : at + wide] = jnp.dot(
-            act_ref[...], down_ref[:, at : at + wide], preferred_element_type=jnp.float32
-        ).astype(out_ref.dtype)
-
-
-def experts(rows, gate, up, down):
+            rows_ref[...], gate_ref[:, columns], preferred_element_type=jnp.float32
+        )
+        act_ref[:, columns] = (
+            gate_act / (1.0 + jnp.exp(-gate_act)) * upward_ref[:, columns]
+        ).astype(act_ref.dtype)
+
+
+def activate(rows, gate, upward):
     count, feat_width = rows.shape
     hidden = gate.shape[1]
     vmem = pl.BlockSpec(memory_space=pltpu.VMEM)
     return pl.pallas_call(
         experts_kernel,
-        out_shape=jax.ShapeDtypeStruct((count, feat_width), jnp.bfloat16),
-        in_specs=[vmem] * 4,
+        out_shape=jax.ShapeDtypeStruct((count, hidden), jnp.bfloat16),
+        in_specs=[vmem] * 3,
         out_specs=vmem,
-        scratch_shapes=[pltpu.VMEM((count, hidden), jnp.bfloat16)],
-        compiler_params=pltpu.CompilerParams(vmem_limit_bytes=8<<20),
+        compiler_params=pltpu.CompilerParams(vmem_limit_bytes=8 << 20),
         cost_estimate=pl.CostEstimate(
-            flops=6 * count * feat_width * hidden,
-            bytes_accessed=6 * feat_width * hidden,
+            flops=2 * count * feat_width * hidden,
+            bytes_accessed=2 * feat_width * hidden,
             transcendentals=count * hidden,
         ),
-    )(rows, gate, up, down)
+    )(rows, gate, upward)
 
 
 def add_kernel(*refs):
@@ -343,21 +314,23 @@
     half = count // 2
     theirs = lax.ppermute(theirs, "expert", swap)
     own_r, own_l, theirs_r, theirs_l = [own], [own], [theirs], [theirs]
-    for step in range(1, half):
+    for step in range(1, half + 1):
         own_r.append(go_right(own_r[-1]))
-        own_l.append(go_left(own_l[-1]))
-        theirs_l.append(go_left(theirs_l[-1]))
-        theirs_r.append(go_right(theirs_r[-1]))
-    own_r.append(lax.ppermute(own_r[half - 2], "attn", right_two))
+        if step < half:
+            own_l.append(go_left(own_l[-1]))
+            theirs_r.append(go_right(theirs_r[-1]))
+            theirs_l.append(go_left(theirs_l[-1]))
     theirs_l.append(lax.ppermute(theirs_l[half - 2], "attn", left_two))
 
-    up = load(w_up[0], own_l[half - 1], 1<<20)
-    down = load(w_down[0], theirs_r[half - 1], 1<<20)
     blocks = [own, theirs]
     for step in range(1, half):
         blocks += [own_r[step], own_l[step], theirs_r[step], theirs_l[step]]
     blocks += [own_r[half], theirs_l[half]]
-    share = experts(jnp.concatenate(blocks), gate, up, down).reshape(len(blocks), cap_slots, feat_width)
+    rows = jnp.concatenate(blocks)
+    upward = jnp.dot(rows, w_up[0], preferred_element_type=jnp.float32)
+    active = activate(rows, gate, upward)
+    share = jnp.dot(active, w_down[0], preferred_element_type=jnp.float32)
+    share = share.astype(jnp.bfloat16).reshape(len(blocks), cap_slots, feat_width)
     own_share = {0: share[0], half: share[-2]}
     theirs_share = {0: share[1], -half: share[-1]}
     for step in range(1, half):
@@ -365,24 +338,16 @@
         own_share[-step], own_share[step] = share[at], share[at + 1]
         theirs_share[-step], theirs_share[step] = share[at + 2], share[at + 3]
 
-    own_from_l = add(
-        lax.ppermute(own_share[half], "attn", right_two),
-        go_right(own_share[half - 1]),
-        own_share[half - 2],
-    )
-    theirs_from_r = add(
-        lax.ppermute(theirs_share[-half], "attn", left_two),
-        go_left(theirs_share[1 - half]),
-        theirs_share[2 - half],
-    )
+    own_from_l = own_share[half]
+    theirs_from_r = theirs_share[-half]
     own_from_r = own_share[1 - half]
     theirs_from_l = theirs_share[half - 1]
-    for step in range(half - 2, 0, -1):
-        own_from_r = add(go_left(own_from_r), own_share[-step])
-        theirs_from_l = add(go_right(theirs_from_l), theirs_share[step])
-        if step < half - 2:
-            own_from_l = add(go_right(own_from_l), own_share[step])
-            theirs_from_r = add(go_left(theirs_from_r), theirs_share[-step])
+    for step in range(half - 1, 0, -1):
+        own_from_l = add(go_right(own_from_l), own_share[step])
+        theirs_from_r = add(go_left(theirs_from_r), theirs_share[-step])
+        if step > 1:
+            own_from_r = add(go_left(own_from_r), own_share[1 - step])
+            theirs_from_l = add(go_right(theirs_from_l), theirs_share[step - 1])
     theirs_total = add(
         theirs_share[0], go_left(theirs_from_r), go_right(theirs_from_l)
     )

time: 68.4 us -> 62 us (0.906)
  Pallas kernels: 19.1 us -> 9.21 us
  matrix products: 0 us -> 2.87 us
  local copies, waits for them, and re-layouts: 0.25 us -> 1.27 us
    pallas_call x3 -> x1, Pallas kernels: 11.4 us -> 1.44 us  [activate(): pl.pallas_call(experts_kernel, out_shape=jax.ShapeDtypeStruct((count, hid...]
    ppermute x12 -> x14, starting transfers between devices: 12.1 us -> 17 us  [go_right(): return lax.ppermute(block, 'attn', right)]
    ppermute x3 -> x0, starting transfers between devices: 4.95 us -> none  [the longest x1 2.2 us: body(): lax.ppermute(theirs_share[-half], 'attn', left_two)]
    dot_general x0 -> x2, matrix products: none -> 2.87 us  [the longest x1 1.48 us: body(): upward = jnp.dot(rows, w_up[0], preferred_element_type=jnp.float32)]
    ppermute x12 -> x13, starting transfers between devices: 13.4 us -> 11 us  [go_left(): return lax.ppermute(block, 'attn', left)]
    ppermute x3 -> x0, waiting for transfers between devices: 2.14 us -> none  [the longest x1 1.93 us: body(): lax.ppermute(theirs_share[-half], 'attn', left_two)]
    ppermute x12 -> x14, waiting for transfers between devices: 6.15 us -> 8.19 us  [go_right(): return lax.ppermute(block, 'attn', right)]
    ppermute x1, starting transfers between devices: 0.94 us -> 2.79 us  [body(): theirs_l.append(lax.ppermute(theirs_l[half - 2], 'attn', left_two))]
  transfers between devices with their start and end apart: 30 -> 30, of which waited for: 14 -> 13; matrix products, arithmetic and copies ran while one was open for 0% -> 0% of each run, Pallas kernels for 11% -> 0%
where the time goes in v4:
time: 62 us; the launch traced here: 61.8 us
  starting transfers between devices  30.9 us (50%)
  waiting for transfers between devices  17.3 us (28%)
  Pallas kernels  9.21 us (15%)
  matrix products  2.87 us (5%)
  local copies, waits for them, and re-layouts  1.27 us (2%)
    ppermute x14, starting transfers between devices, go_right(): return lax.ppermute(block, 'attn', right)  17 us
    ppermute x13, starting transfers between devices, go_left(): return lax.ppermute(block, 'attn', left)  11 us
    ppermute x14, waiting for transfers between devices, go_right(): return lax.ppermute(block, 'attn', right)  8.19 us
    ppermute x13, waiting for transfers between devices, go_left(): return lax.ppermute(block, 'attn', left)  7.86 us
    pallas_call x1, Pallas kernels, body(): pl.pallas_call(front_kernel, out_shape=(jax.ShapeDtypeStruct((row_count,...  6.43 us
    ppermute x1, starting transfers between devices, body(): theirs_l.append(lax.ppermute(theirs_l[half - 2], 'attn', left_two))  2.79 us
    dot_general x1, matrix products, body(): upward = jnp.dot(rows, w_up[0], preferred_element_type=jnp.float32)  1.48 us
    pallas_call x1, Pallas kernels, activate(): pl.pallas_call(experts_kernel, out_shape=jax.ShapeDtypeStruct((count, hid...  1.44 us
  transfers between devices with their start and end apart: 30, of which 13 were waited for; matrix products, arithmetic and copies ran while one was open for 0% of the time, Pallas kernels for 0%

profile of v4, /device:TPU:0, one launch (start us, length us, event | category | flops | bytes accessed | tf_op | source)
XLA Modules:
  0.0 61.8 jit_solution(11849740544510002019)
XLA Ops:
  0.0 6.4 %shard_map.118 = (f32[16,6144]{1,0:T(8,128)S(1)}, bf16[8,6144]{1,0:T(8,128)(2,1)S(1)}, bf16[8,6144]{1,0:T(8,128)(2,1)S(1)}, f32[16,16]{1,0:T(8,128)S(1)}, f32[16...) custom-call(s32[1]{0:T(128)} %bitcast.here_ref, bf16[16,6144]{1,0:T(8,128)(2,1)} %hidden_hbm.1, bf16[16,6144]{1,0:T(8,128)(2,1)} %query_hbm.1, ...), custom_call_target="tpu_custom_call" | custom-call | flops 1000000000 | bytes 40000000 | tf_op jit(solution)/shard_map/pallas_call | solution.py:276
  6.4 3.1 %collective-permute-start.1 = (bf16[8,6144]{1,0:T(8,128)(2,1)S(1)}, bf16[8,6144]{1,0:T(8,128)(2,1)S(1)}, u32[]{:S(2)}, u32[]{:S(2)}) collective-permute-start(bf16[8,6144]{1,0:T(8,128)(2,1)S(1)} %get-tuple-element.14), channel_id=1, source_target_pairs={{0,4},{4,8},{8,12},{12,14},{14,10},{10,6},{6,2},{2,0},{1,5},{5,9},... | collective-permute-start | bytes 294920 | tf_op jit(solution)/shard_map/ppermute | solution.py:309
  9.5 1.3 %collective-permute-done = bf16[8,6144]{1,0:T(8,128)(2,1)S(1)} collective-permute-done((bf16[8,6144]{1,0:T(8,128)(2,1)S(1)}, bf16[8,6144]{1,0:T(8,128)(2,1)S(1)}, u32[]{:S(2)}, u32[]{:S(2)}) %collective-permute-start) | collective-permute-done | bytes 98336 | tf_op jit(solution)/shard_map/ppermute | solution.py:315
  10.8 2.0 %collective-permute-start.3 = (bf16[8,6144]{1,0:T(8,128)(2,1)S(1)}, bf16[8,6144]{1,0:T(8,128)(2,1)S(1)}, u32[]{:S(2)}, u32[]{:S(2)}) collective-permute-start(bf16[8,6144]{1,0:T(8,128)(2,1)S(1)} %collective-permute-done), channel_id=1, source_target_pairs={{0,4},{4,8},{8,12},{12,14},{14,10},{10,6},{6,2},{2,0},{1,5},{5,9},... | collective-permute-start | bytes 294920 | tf_op jit(solution)/shard_map/ppermute | solution.py:309
  12.9 2.1 %collective-permute-start.5 = (bf16[8,6144]{1,0:T(8,128)(2,1)S(1)}, bf16[8,6144]{1,0:T(8,128)(2,1)S(1)}, u32[]{:S(2)}, u32[]{:S(2)}) collective-permute-start(bf16[8,6144]{1,0:T(8,128)(2,1)S(1)} %collective-permute-done.1), channel_id=1, source_target_pairs={{0,4},{4,8},{8,12},{12,14},{14,10},{10,6},{6,2},{2,0},{1,5},{5,9},... | collective-permute-start | bytes 294920 | tf_op jit(solution)/shard_map/ppermute | solution.py:309
  15.0 1.4 %collective-permute-done.3 = bf16[8,6144]{1,0:T(8,128)(2,1)S(1)} collective-permute-done((bf16[8,6144]{1,0:T(8,128)(2,1)S(1)}, bf16[8,6144]{1,0:T(8,128)(2,1)S(1)}, u32[]{:S(2)}, u32[]{:S(2)}) %collective-permute-start.3) | collective-permute-done | bytes 98336 | tf_op jit(solution)/shard_map/ppermute | solution.py:309
  16.4 1.9 %collective-permute-start.7 = (bf16[8,6144]{1,0:T(8,128)(2,1)S(1)}, bf16[8,6144]{1,0:T(8,128)(2,1)S(1)}, u32[]{:S(2)}, u32[]{:S(2)}) collective-permute-start(bf16[8,6144]{1,0:T(8,128)(2,1)S(1)} %collective-permute-done.3), channel_id=1, source_target_pairs={{0,4},{4,8},{8,12},{12,14},{14,10},{10,6},{6,2},{2,0},{1,5},{5,9},... | collective-permute-start | bytes 294920 | tf_op jit(solution)/shard_map/ppermute | solution.py:309
  18.5 1.9 %collective-permute-start.9 = (bf16[8,6144]{1,0:T(8,128)(2,1)S(1)}, bf16[8,6144]{1,0:T(8,128)(2,1)S(1)}, u32[]{:S(2)}, u32[]{:S(2)}) collective-permute-start(bf16[8,6144]{1,0:T(8,128)(2,1)S(1)} %collective-permute-done.5), channel_id=1, source_target_pairs={{0,4},{4,8},{8,12},{12,14},{14,10},{10,6},{6,2},{2,0},{1,5},{5,9},... | collective-permute-start | bytes 294920 | tf_op jit(solution)/shard_map/ppermute | solution.py:309
  20.7 3.0 %collective-permute-done.8 = bf16[8,6144]{1,0:T(8,128)(2,1)S(1)} collective-permute-done((bf16[8,6144]{1,0:T(8,128)(2,1)S(1)}, bf16[8,6144]{1,0:T(8,128)(2,1)S(1)}, u32[]{:S(2)}, u32[]{:S(2)}) %collective-permute-start.8) | collective-permute-done | bytes 98336 | tf_op jit(solution)/shard_map/ppermute | solution.py:312
  24.2 2.8 %collective-permute-start.14 = (bf16[8,6144]{1,0:T(8,128)(2,1)S(1)}, bf16[8,6144]{1,0:T(8,128)(2,1)S(1)}, u32[]{:S(2)}, u32[]{:S(2)}) collective-permute-start(bf16[8,6144]{1,0:T(8,128)(2,1)S(1)} %collective-permute-done.8), channel_id=1, source_target_pairs={{8,0},{12,4},{14,8},{10,12},{6,14},{2,10},{0,6},{4,2},{9,1},{13,5}... | collective-permute-start | bytes 294920 | tf_op jit(solution)/shard_map/ppermute | solution.py:323
  27.8 3.8 %collective-permute-done.11 = bf16[8,6144]{1,0:T(8,128)(2,1)S(1)} collective-permute-done((bf16[8,6144]{1,0:T(8,128)(2,1)S(1)}, bf16[8,6144]{1,0:T(8,128)(2,1)S(1)}, u32[]{:S(2)}, u32[]{:S(2)}) %collective-permute-start.11) | collective-permute-done | bytes 98336 | tf_op jit(solution)/shard_map/ppermute | solution.py:309
  31.6 1.0 %collective-permute-done.13 = bf16[8,6144]{1,0:T(8,128)(2,1)S(1)} collective-permute-done((bf16[8,6144]{1,0:T(8,128)(2,1)S(1)}, bf16[8,6144]{1,0:T(8,128)(2,1)S(1)}, u32[]{:S(2)}, u32[]{:S(2)}) %collective-permute-start.13) | collective-permute-done | bytes 98336 | tf_op jit(solution)/shard_map/ppermute | solution.py:309
  32.7 1.5 %fusion.2.upward_ref = f32[128,768]{1,0:T(8,128)S(1)} fusion(bf16[128,6144]{1,0:T(8,128)(2,1)S(1)} %constant_dynamic-update-slice_fusion.rows_ref, bf16[1,6144,768]{2,1,0:T(8,128)(2,1)S(1)} %bitcast.16), kind=kOutput, calls=%fused_computation.2 | convolution fusion | flops 1207959552 | bytes 11403264 | tf_op jit(solution)/shard_map/dot_general | solution.py:330
  34.2 1.4 %shard_map.119 = bf16[128,768]{1,0:T(8,128)(2,1)S(1)} custom-call(bf16[128,6144]{1,0:T(8,128)(2,1)S(1)} %constant_dynamic-update-slice_fusion.rows_ref, bf16[6144,768]{1,0:T(8,128)(2,1)S(1)} %get-tuple-element.16.gate_ref, f32[128,768]{1,0:T(8,128)S(1)} %fusion.2.upward_ref), custom_call_target="tpu_custom_call" | custom-call | flops 1207959552 | bytes 9437184 | tf_op jit(solution)/shard_map/pallas_call | solution.py:40
  35.7 1.0 %slice-done.5 = s8[4194304]{0:T(1024)(128)(4,1)S(1)} async-done(((s8[9437184]{0:T(1024)(128)(4,1)}), s8[4194304]{0:T(1024)(128)(4,1)S(1)}, s32[]{:S(2)}) %slice-start.5) | async-done | bytes 4194328
  36.7 1.4 %fusion.4 = bf16[128,6144]{1,0:T(8,128)(2,1)S(1)} fusion(bf16[128,768]{1,0:T(8,128)(2,1)S(1)} %shard_map.119, bf16[1,768,6144]{2,1,0:T(8,128)(2,1)S(1)} %bitcast.18), kind=kOutput, calls=%fused_computation.4 | convolution fusion | flops 1208745984 | bytes 11206656 | tf_op jit(solution)/shard_map/dot_general | solution.py:332
  38.2 1.6 %collective-permute-start.22 = (bf16[8,6144]{1,0:T(8,128)(2,1)S(1)}, bf16[8,6144]{1,0:T(8,128)(2,1)S(1)}, u32[]{:S(2)}, u32[]{:S(2)}) collective-permute-start(bf16[8,6144]{1,0:T(8,128)(2,1)S(1)} %get-tuple-element.23), channel_id=1, source_target_pairs={{4,0},{8,4},{12,8},{14,12},{10,14},{6,10},{2,6},{0,2},{5,1},{9,5},... | collective-permute-start | bytes 294920 | tf_op jit(solution)/shard_map/ppermute | solution.py:312
  40.3 1.0 %collective-permute-start.26 = (bf16[8,6144]{1,0:T(8,128)(2,1)S(1)}, bf16[8,6144]{1,0:T(8,128)(2,1)S(1)}, u32[]{:S(2)}, u32[]{:S(2)}) collective-permute-start(bf16[8,6144]{1,0:T(8,128)(2,1)S(1)} %get-tuple-element.19), channel_id=1, source_target_pairs={{0,4},{4,8},{8,12},{12,14},{14,10},{10,6},{6,2},{2,0},{1,5},{5,9},... | collective-permute-start | bytes 294920 | tf_op jit(solution)/shard_map/ppermute | solution.py:309
  41.4 1.7 %collective-permute-done.22.refs_0_ = bf16[8,6144]{1,0:T(8,128)(2,1)S(1)} collective-permute-done((bf16[8,6144]{1,0:T(8,128)(2,1)S(1)}, bf16[8,6144]{1,0:T(8,128)(2,1)S(1)}, u32[]{:S(2)}, u32[]{:S(2)}) %collective-permute-start.22) | collective-permute-done | bytes 98336 | tf_op jit(solution)/shard_map/ppermute | solution.py:312
  43.0 1.6 %collective-permute-start.23 = (bf16[8,6144]{1,0:T(8,128)(2,1)S(1)}, bf16[8,6144]{1,0:T(8,128)(2,1)S(1)}, u32[]{:S(2)}, u32[]{:S(2)}) collective-permute-start(bf16[8,6144]{1,0:T(8,128)(2,1)S(1)} %shard_map.125), channel_id=1, source_target_pairs={{4,0},{8,4},{12,8},{14,12},{10,14},{6,10},{2,6},{0,2},{5,1},{9,5},... | collective-permute-start | bytes 294920 | tf_op jit(solution)/shard_map/ppermute | solution.py:312
  44.6 1.3 %collective-permute-start.19 = (bf16[8,6144]{1,0:T(8,128)(2,1)S(1)}, bf16[8,6144]{1,0:T(8,128)(2,1)S(1)}, u32[]{:S(2)}, u32[]{:S(2)}) collective-permute-start(bf16[8,6144]{1,0:T(8,128)(2,1)S(1)} %get-tuple-element.27), channel_id=1, source_target_pairs={{4,0},{8,4},{12,8},{14,12},{10,14},{6,10},{2,6},{0,2},{5,1},{9,5},... | collective-permute-start | bytes 294920 | tf_op jit(solution)/shard_map/ppermute | solution.py:312
  46.0 0.7 %collective-permute-start.16 = (bf16[8,6144]{1,0:T(8,128)(2,1)S(1)}, bf16[8,6144]{1,0:T(8,128)(2,1)S(1)}, u32[]{:S(2)}, u32[]{:S(2)}) collective-permute-start(bf16[8,6144]{1,0:T(8,128)(2,1)S(1)} %shard_map.120), channel_id=1, source_target_pairs={{0,4},{4,8},{8,12},{12,14},{14,10},{10,6},{6,2},{2,0},{1,5},{5,9},... | collective-permute-start | bytes 294920 | tf_op jit(solution)/shard_map/ppermute | solution.py:309
  47.7 1.6 %collective-permute-start.24 = (bf16[8,6144]{1,0:T(8,128)(2,1)S(1)}, bf16[8,6144]{1,0:T(8,128)(2,1)S(1)}, u32[]{:S(2)}, u32[]{:S(2)}) collective-permute-start(bf16[8,6144]{1,0:T(8,128)(2,1)S(1)} %shard_map.126), channel_id=1, source_target_pairs={{4,0},{8,4},{12,8},{14,12},{10,14},{6,10},{2,6},{0,2},{5,1},{9,5},... | collective-permute-start | bytes 294920 | tf_op jit(solution)/shard_map/ppermute | solution.py:312
  49.3 0.7 %collective-permute-done.19.refs_0_ = bf16[8,6144]{1,0:T(8,128)(2,1)S(1)} collective-permute-done((bf16[8,6144]{1,0:T(8,128)(2,1)S(1)}, bf16[8,6144]{1,0:T(8,128)(2,1)S(1)}, u32[]{:S(2)}, u32[]{:S(2)}) %collective-permute-start.19) | collective-permute-done | bytes 98336 | tf_op jit(solution)/shard_map/ppermute | solution.py:312
  50.1 1.3 %collective-permute-start.20 = (bf16[8,6144]{1,0:T(8,128)(2,1)S(1)}, bf16[8,6144]{1,0:T(8,128)(2,1)S(1)}, u32[]{:S(2)}, u32[]{:S(2)}) collective-permute-start(bf16[8,6144]{1,0:T(8,128)(2,1)S(1)} %shard_map.123), channel_id=1, source_target_pairs={{4,0},{8,4},{12,8},{14,12},{10,14},{6,10},{2,6},{0,2},{5,1},{9,5},... | collective-permute-start | bytes 294920 | tf_op jit(solution)/shard_map/ppermute | solution.py:312
  51.4 0.8 %collective-permute-start.17 = (bf16[8,6144]{1,0:T(8,128)(2,1)S(1)}, bf16[8,6144]{1,0:T(8,128)(2,1)S(1)}, u32[]{:S(2)}, u32[]{:S(2)}) collective-permute-start(bf16[8,6144]{1,0:T(8,128)(2,1)S(1)} %shard_map.121), channel_id=1, source_target_pairs={{0,4},{4,8},{8,12},{12,14},{14,10},{10,6},{6,2},{2,0},{1,5},{5,9},... | collective-permute-start | bytes 294920 | tf_op jit(solution)/shard_map/ppermute | solution.py:309
  53.4 1.5 %collective-permute-start.25 = (bf16[8,6144]{1,0:T(8,128)(2,1)S(1)}, bf16[8,6144]{1,0:T(8,128)(2,1)S(1)}, u32[]{:S(2)}, u32[]{:S(2)}) collective-permute-start(bf16[8,6144]{1,0:T(8,128)(2,1)S(1)} %shard_map.127), channel_id=1, source_target_pairs={{4,0},{8,4},{12,8},{14,12},{10,14},{6,10},{2,6},{0,2},{5,1},{9,5},... | collective-permute-start | bytes 294920 | tf_op jit(solution)/shard_map/ppermute | solution.py:312
  55.0 1.1 %collective-permute-start.21 = (bf16[8,6144]{1,0:T(8,128)(2,1)S(1)}, bf16[8,6144]{1,0:T(8,128)(2,1)S(1)}, u32[]{:S(2)}, u32[]{:S(2)}) collective-permute-start(bf16[8,6144]{1,0:T(8,128)(2,1)S(1)} %shard_map.124), channel_id=1, source_target_pairs={{4,0},{8,4},{12,8},{14,12},{10,14},{6,10},{2,6},{0,2},{5,1},{9,5},... | collective-permute-start | bytes 294920 | tf_op jit(solution)/shard_map/ppermute | solution.py:312
  56.1 1.0 %collective-permute-start.18 = (bf16[8,6144]{1,0:T(8,128)(2,1)S(1)}, bf16[8,6144]{1,0:T(8,128)(2,1)S(1)}, u32[]{:S(2)}, u32[]{:S(2)}) collective-permute-start(bf16[8,6144]{1,0:T(8,128)(2,1)S(1)} %shard_map.122), channel_id=1, source_target_pairs={{0,4},{4,8},{8,12},{12,14},{14,10},{10,6},{6,2},{2,0},{1,5},{5,9},... | collective-permute-start | bytes 294920 | tf_op jit(solution)/shard_map/ppermute | solution.py:309
  58.2 1.4 %collective-permute-done.21.third_ref = bf16[8,6144]{1,0:T(8,128)(2,1)S(1)} collective-permute-done((bf16[8,6144]{1,0:T(8,128)(2,1)S(1)}, bf16[8,6144]{1,0:T(8,128)(2,1)S(1)}, u32[]{:S(2)}, u32[]{:S(2)}) %collective-permute-start.21) | collective-permute-done | bytes 98336 | tf_op jit(solution)/shard_map/ppermute | solution.py:312
  59.6 1.2 %collective-permute-done.18.second_ref = bf16[8,6144]{1,0:T(8,128)(2,1)S(1)} collective-permute-done((bf16[8,6144]{1,0:T(8,128)(2,1)S(1)}, bf16[8,6144]{1,0:T(8,128)(2,1)S(1)}, u32[]{:S(2)}, u32[]{:S(2)}) %collective-permute-start.18) | collective-permute-done | bytes 98336 | tf_op jit(solution)/shard_map/ppermute | solution.py:309
  60.8 1.0 %shard_map.131 = f32[16,6144]{1,0:T(8,128)} custom-call(f32[16,6144]{1,0:T(8,128)S(1)} %get-tuple-element.11.residual_ref, f32[16,16]{1,0:T(8,128)S(1)} %get-tuple-element.12.slots_ref, f32[16,2]{1,0:T(8,128)S(1)} %get-tuple-element.13.weights_ref, bf16[8,6144]{1,0:T(8,128)(2,1)S(1)} %get-tuple-element.32.first_ref, ...), custom_call_target="tpu_custom_call" | custom-call | tf_op jit(solution)/shard_map/pallas_call | solution.py:355
  (75 shorter events, 5.9 us)
Async XLA Ops:
  0.0 32.7 %slice-start.1 = ((s8[9437184]{0:T(1024)(128)(4,1)}), s8[4194304]{0:T(1024)(128)(4,1)S(1)}, s32[]{:S(2)}) async-start(s8[9437184]{0:T(1024)(128)(4,1)} %bitcast.15), calls=%async_computation.1 | async-start | bytes 8388608
  0.0 32.7 %slice-start.2 = ((s8[9437184]{0:T(1024)(128)(4,1)}), s8[1048576]{0:T(1024)(128)(4,1)S(1)}, s32[]{:S(2)}) async-start(s8[9437184]{0:T(1024)(128)(4,1)} %bitcast.15), calls=%async_computation.2 | async-start | bytes 2097152
  6.4 6.4 %collective-permute-start.1 = (bf16[8,6144]{1,0:T(8,128)(2,1)S(1)}, bf16[8,6144]{1,0:T(8,128)(2,1)S(1)}, u32[]{:S(2)}, u32[]{:S(2)}) collective-permute-start(bf16[8,6144]{1,0:T(8,128)(2,1)S(1)} %get-tuple-element.14), channel_id=1, source_target_pairs={{0,4},{4,8},{8,12},{12,14},{14,10},{10,6},{6,2},{2,0},{1,5},{5,9},... | collective-permute-start | bytes 294920 | tf_op jit(solution)/shard_map/ppermute | solution.py:309
  9.5 5.4 %collective-permute-start.2 = (bf16[8,6144]{1,0:T(8,128)(2,1)S(1)}, bf16[8,6144]{1,0:T(8,128)(2,1)S(1)}, u32[]{:S(2)}, u32[]{:S(2)}) collective-permute-start(bf16[8,6144]{1,0:T(8,128)(2,1)S(1)} %get-tuple-element.14), channel_id=1, source_target_pairs={{4,0},{8,4},{12,8},{14,12},{10,14},{6,10},{2,6},{0,2},{5,1},{9,5},... | collective-permute-start | bytes 294920 | tf_op jit(solution)/shard_map/ppermute | solution.py:312
  9.5 1.3 %collective-permute-start = (bf16[8,6144]{1,0:T(8,128)(2,1)S(1)}, bf16[8,6144]{1,0:T(8,128)(2,1)S(1)}, u32[]{:S(2)}, u32[]{:S(2)}) collective-permute-start(bf16[8,6144]{1,0:T(8,128)(2,1)S(1)} %get-tuple-element.15), channel_id=1, source_target_pairs={{0,1},{1,0},{2,3},{3,2},{4,5},{5,4},{6,7},{7,6},{8,9},{9,8},{10,11... | collective-permute-start | bytes 294920 | tf_op jit(solution)/shard_map/ppermute | solution.py:315
  10.8 5.6 %collective-permute-start.3 = (bf16[8,6144]{1,0:T(8,128)(2,1)S(1)}, bf16[8,6144]{1,0:T(8,128)(2,1)S(1)}, u32[]{:S(2)}, u32[]{:S(2)}) collective-permute-start(bf16[8,6144]{1,0:T(8,128)(2,1)S(1)} %collective-permute-done), channel_id=1, source_target_pairs={{0,4},{4,8},{8,12},{12,14},{14,10},{10,6},{6,2},{2,0},{1,5},{5,9},... | collective-permute-start | bytes 294920 | tf_op jit(solution)/shard_map/ppermute | solution.py:309
  12.8 5.5 %collective-permute-start.4 = (bf16[8,6144]{1,0:T(8,128)(2,1)S(1)}, bf16[8,6144]{1,0:T(8,128)(2,1)S(1)}, u32[]{:S(2)}, u32[]{:S(2)}) collective-permute-start(bf16[8,6144]{1,0:T(8,128)(2,1)S(1)} %collective-permute-done), channel_id=1, source_target_pairs={{4,0},{8,4},{12,8},{14,12},{10,14},{6,10},{2,6},{0,2},{5,1},{9,5},... | collective-permute-start | bytes 294920 | tf_op jit(solution)/shard_map/ppermute | solution.py:312
  12.9 5.6 %collective-permute-start.5 = (bf16[8,6144]{1,0:T(8,128)(2,1)S(1)}, bf16[8,6144]{1,0:T(8,128)(2,1)S(1)}, u32[]{:S(2)}, u32[]{:S(2)}) collective-permute-start(bf16[8,6144]{1,0:T(8,128)(2,1)S(1)} %collective-permute-done.1), channel_id=1, source_target_pairs={{0,4},{4,8},{8,12},{12,14},{14,10},{10,6},{6,2},{2,0},{1,5},{5,9},... | collective-permute-start | bytes 294920 | tf_op jit(solution)/shard_map/ppermute | solution.py:309
  15.0 5.5 %collective-permute-start.6 = (bf16[8,6144]{1,0:T(8,128)(2,1)S(1)}, bf16[8,6144]{1,0:T(8,128)(2,1)S(1)}, u32[]{:S(2)}, u32[]{:S(2)}) collective-permute-start(bf16[8,6144]{1,0:T(8,128)(2,1)S(1)} %collective-permute-done.2), channel_id=1, source_target_pairs={{4,0},{8,4},{12,8},{14,12},{10,14},{6,10},{2,6},{0,2},{5,1},{9,5},... | collective-permute-start | bytes 294920 | tf_op jit(solution)/shard_map/ppermute | solution.py:312
  16.4 10.6 %collective-permute-start.7 = (bf16[8,6144]{1,0:T(8,128)(2,1)S(1)}, bf16[8,6144]{1,0:T(8,128)(2,1)S(1)}, u32[]{:S(2)}, u32[]{:S(2)}) collective-permute-start(bf16[8,6144]{1,0:T(8,128)(2,1)S(1)} %collective-permute-done.3), channel_id=1, source_target_pairs={{0,4},{4,8},{8,12},{12,14},{14,10},{10,6},{6,2},{2,0},{1,5},{5,9},... | collective-permute-start | bytes 294920 | tf_op jit(solution)/shard_map/ppermute | solution.py:309
  18.3 5.3 %collective-permute-start.8 = (bf16[8,6144]{1,0:T(8,128)(2,1)S(1)}, bf16[8,6144]{1,0:T(8,128)(2,1)S(1)}, u32[]{:S(2)}, u32[]{:S(2)}) collective-permute-start(bf16[8,6144]{1,0:T(8,128)(2,1)S(1)} %collective-permute-done.4), channel_id=1, source_target_pairs={{4,0},{8,4},{12,8},{14,12},{10,14},{6,10},{2,6},{0,2},{5,1},{9,5},... | collective-permute-start | bytes 294920 | tf_op jit(solution)/shard_map/ppermute | solution.py:312
  18.5 8.9 %collective-permute-start.9 = (bf16[8,6144]{1,0:T(8,128)(2,1)S(1)}, bf16[8,6144]{1,0:T(8,128)(2,1)S(1)}, u32[]{:S(2)}, u32[]{:S(2)}) collective-permute-start(bf16[8,6144]{1,0:T(8,128)(2,1)S(1)} %collective-permute-done.5), channel_id=1, source_target_pairs={{0,4},{4,8},{8,12},{12,14},{14,10},{10,6},{6,2},{2,0},{1,5},{5,9},... | collective-permute-start | bytes 294920 | tf_op jit(solution)/shard_map/ppermute | solution.py:309
  20.5 7.3 %collective-permute-start.10 = (bf16[8,6144]{1,0:T(8,128)(2,1)S(1)}, bf16[8,6144]{1,0:T(8,128)(2,1)S(1)}, u32[]{:S(2)}, u32[]{:S(2)}) collective-permute-start(bf16[8,6144]{1,0:T(8,128)(2,1)S(1)} %collective-permute-done.6), channel_id=1, source_target_pairs={{4,0},{8,4},{12,8},{14,12},{10,14},{6,10},{2,6},{0,2},{5,1},{9,5},... | collective-permute-start | bytes 294920 | tf_op jit(solution)/shard_map/ppermute | solution.py:312
  23.7 7.9 %collective-permute-start.12 = (bf16[8,6144]{1,0:T(8,128)(2,1)S(1)}, bf16[8,6144]{1,0:T(8,128)(2,1)S(1)}, u32[]{:S(2)}, u32[]{:S(2)}) collective-permute-start(bf16[8,6144]{1,0:T(8,128)(2,1)S(1)} %collective-permute-done.8), channel_id=1, source_target_pairs={{4,0},{8,4},{12,8},{14,12},{10,14},{6,10},{2,6},{0,2},{5,1},{9,5},... | collective-permute-start | bytes 294920 | tf_op jit(solution)/shard_map/ppermute | solution.py:312
  24.2 8.5 %collective-permute-start.14 = (bf16[8,6144]{1,0:T(8,128)(2,1)S(1)}, bf16[8,6144]{1,0:T(8,128)(2,1)S(1)}, u32[]{:S(2)}, u32[]{:S(2)}) collective-permute-start(bf16[8,6144]{1,0:T(8,128)(2,1)S(1)} %collective-permute-done.8), channel_id=1, source_target_pairs={{8,0},{12,4},{14,8},{10,12},{6,14},{2,10},{0,6},{4,2},{9,1},{13,5}... | collective-permute-start | bytes 294920 | tf_op jit(solution)/shard_map/ppermute | solution.py:323
  27.0 4.6 %collective-permute-start.11 = (bf16[8,6144]{1,0:T(8,128)(2,1)S(1)}, bf16[8,6144]{1,0:T(8,128)(2,1)S(1)}, u32[]{:S(2)}, u32[]{:S(2)}) collective-permute-start(bf16[8,6144]{1,0:T(8,128)(2,1)S(1)} %collective-permute-done.7), channel_id=1, source_target_pairs={{0,4},{4,8},{8,12},{12,14},{14,10},{10,6},{6,2},{2,0},{1,5},{5,9},... | collective-permute-start | bytes 294920 | tf_op jit(solution)/shard_map/ppermute | solution.py:309
  27.4 5.2 %collective-permute-start.13 = (bf16[8,6144]{1,0:T(8,128)(2,1)S(1)}, bf16[8,6144]{1,0:T(8,128)(2,1)S(1)}, u32[]{:S(2)}, u32[]{:S(2)}) collective-permute-start(bf16[8,6144]{1,0:T(8,128)(2,1)S(1)} %collective-permute-done.9), channel_id=1, source_target_pairs={{0,4},{4,8},{8,12},{12,14},{14,10},{10,6},{6,2},{2,0},{1,5},{5,9},... | collective-permute-start | bytes 294920 | tf_op jit(solution)/shard_map/ppermute | solution.py:309
  38.2 4.8 %collective-permute-start.22 = (bf16[8,6144]{1,0:T(8,128)(2,1)S(1)}, bf16[8,6144]{1,0:T(8,128)(2,1)S(1)}, u32[]{:S(2)}, u32[]{:S(2)}) collective-permute-start(bf16[8,6144]{1,0:T(8,128)(2,1)S(1)} %get-tuple-element.23), channel_id=1, source_target_pairs={{4,0},{8,4},{12,8},{14,12},{10,14},{6,10},{2,6},{0,2},{5,1},{9,5},... | collective-permute-start | bytes 294920 | tf_op jit(solution)/shard_map/ppermute | solution.py:312
  39.9 6.1 %collective-permute-start.15 = (bf16[8,6144]{1,0:T(8,128)(2,1)S(1)}, bf16[8,6144]{1,0:T(8,128)(2,1)S(1)}, u32[]{:S(2)}, u32[]{:S(2)}) collective-permute-start(bf16[8,6144]{1,0:T(8,128)(2,1)S(1)} %get-tuple-element.31), channel_id=1, source_target_pairs={{0,4},{4,8},{8,12},{12,14},{14,10},{10,6},{6,2},{2,0},{1,5},{5,9},... | collective-permute-start | bytes 294920 | tf_op jit(solution)/shard_map/ppermute | solution.py:309
  40.3 6.4 %collective-permute-start.26 = (bf16[8,6144]{1,0:T(8,128)(2,1)S(1)}, bf16[8,6144]{1,0:T(8,128)(2,1)S(1)}, u32[]{:S(2)}, u32[]{:S(2)}) collective-permute-start(bf16[8,6144]{1,0:T(8,128)(2,1)S(1)} %get-tuple-element.19), channel_id=1, source_target_pairs={{0,4},{4,8},{8,12},{12,14},{14,10},{10,6},{6,2},{2,0},{1,5},{5,9},... | collective-permute-start | bytes 294920 | tf_op jit(solution)/shard_map/ppermute | solution.py:309
  43.0 4.7 %collective-permute-start.23 = (bf16[8,6144]{1,0:T(8,128)(2,1)S(1)}, bf16[8,6144]{1,0:T(8,128)(2,1)S(1)}, u32[]{:S(2)}, u32[]{:S(2)}) collective-permute-start(bf16[8,6144]{1,0:T(8,128)(2,1)S(1)} %shard_map.125), channel_id=1, source_target_pairs={{4,0},{8,4},{12,8},{14,12},{10,14},{6,10},{2,6},{0,2},{5,1},{9,5},... | collective-permute-start | bytes 294920 | tf_op jit(solution)/shard_map/ppermute | solution.py:312
  44.6 5.4 %collective-permute-start.19 = (bf16[8,6144]{1,0:T(8,128)(2,1)S(1)}, bf16[8,6144]{1,0:T(8,128)(2,1)S(1)}, u32[]{:S(2)}, u32[]{:S(2)}) collective-permute-start(bf16[8,6144]{1,0:T(8,128)(2,1)S(1)} %get-tuple-element.27), channel_id=1, source_target_pairs={{4,0},{8,4},{12,8},{14,12},{10,14},{6,10},{2,6},{0,2},{5,1},{9,5},... | collective-permute-start | bytes 294920 | tf_op jit(solution)/shard_map/ppermute | solution.py:312
  46.0 5.4 %collective-permute-start.16 = (bf16[8,6144]{1,0:T(8,128)(2,1)S(1)}, bf16[8,6144]{1,0:T(8,128)(2,1)S(1)}, u32[]{:S(2)}, u32[]{:S(2)}) collective-permute-start(bf16[8,6144]{1,0:T(8,128)(2,1)S(1)} %shard_map.120), channel_id=1, source_target_pairs={{0,4},{4,8},{8,12},{12,14},{14,10},{10,6},{6,2},{2,0},{1,5},{5,9},... | collective-permute-start | bytes 294920 | tf_op jit(solution)/shard_map/ppermute | solution.py:309
  46.8 6.0 %collective-permute-start.27 = (bf16[8,6144]{1,0:T(8,128)(2,1)S(1)}, bf16[8,6144]{1,0:T(8,128)(2,1)S(1)}, u32[]{:S(2)}, u32[]{:S(2)}) collective-permute-start(bf16[8,6144]{1,0:T(8,128)(2,1)S(1)} %shard_map.128), channel_id=1, source_target_pairs={{0,4},{4,8},{8,12},{12,14},{14,10},{10,6},{6,2},{2,0},{1,5},{5,9},... | collective-permute-start | bytes 294920 | tf_op jit(solution)/shard_map/ppermute | solution.py:309
  47.7 5.6 %collective-permute-start.24 = (bf16[8,6144]{1,0:T(8,128)(2,1)S(1)}, bf16[8,6144]{1,0:T(8,128)(2,1)S(1)}, u32[]{:S(2)}, u32[]{:S(2)}) collective-permute-start(bf16[8,6144]{1,0:T(8,128)(2,1)S(1)} %shard_map.126), channel_id=1, source_target_pairs={{4,0},{8,4},{12,8},{14,12},{10,14},{6,10},{2,6},{0,2},{5,1},{9,5},... | collective-permute-start | bytes 294920 | tf_op jit(solution)/shard_map/ppermute | solution.py:312
  50.1 4.9 %collective-permute-start.20 = (bf16[8,6144]{1,0:T(8,128)(2,1)S(1)}, bf16[8,6144]{1,0:T(8,128)(2,1)S(1)}, u32[]{:S(2)}, u32[]{:S(2)}) collective-permute-start(bf16[8,6144]{1,0:T(8,128)(2,1)S(1)} %shard_map.123), channel_id=1, source_target_pairs={{4,0},{8,4},{12,8},{14,12},{10,14},{6,10},{2,6},{0,2},{5,1},{9,5},... | collective-permute-start | bytes 294920 | tf_op jit(solution)/shard_map/ppermute | solution.py:312
  51.4 4.7 %collective-permute-start.17 = (bf16[8,6144]{1,0:T(8,128)(2,1)S(1)}, bf16[8,6144]{1,0:T(8,128)(2,1)S(1)}, u32[]{:S(2)}, u32[]{:S(2)}) collective-permute-start(bf16[8,6144]{1,0:T(8,128)(2,1)S(1)} %shard_map.121), channel_id=1, source_target_pairs={{0,4},{4,8},{8,12},{12,14},{14,10},{10,6},{6,2},{2,0},{1,5},{5,9},... | collective-permute-start | bytes 294920 | tf_op jit(solution)/shard_map/ppermute | solution.py:309
  52.8 4.7 %collective-permute-start.28 = (bf16[8,6144]{1,0:T(8,128)(2,1)S(1)}, bf16[8,6144]{1,0:T(8,128)(2,1)S(1)}, u32[]{:S(2)}, u32[]{:S(2)}) collective-permute-start(bf16[8,6144]{1,0:T(8,128)(2,1)S(1)} %shard_map.129), channel_id=1, source_target_pairs={{0,4},{4,8},{8,12},{12,14},{14,10},{10,6},{6,2},{2,0},{1,5},{5,9},... | collective-permute-start | bytes 294920 | tf_op jit(solution)/shard_map/ppermute | solution.py:309
  53.4 4.7 %collective-permute-start.25 = (bf16[8,6144]{1,0:T(8,128)(2,1)S(1)}, bf16[8,6144]{1,0:T(8,128)(2,1)S(1)}, u32[]{:S(2)}, u32[]{:S(2)}) collective-permute-start(bf16[8,6144]{1,0:T(8,128)(2,1)S(1)} %shard_map.127), channel_id=1, source_target_pairs={{4,0},{8,4},{12,8},{14,12},{10,14},{6,10},{2,6},{0,2},{5,1},{9,5},... | collective-permute-start | bytes 294920 | tf_op jit(solution)/shard_map/ppermute | solution.py:312
  55.0 4.7 %collective-permute-start.21 = (bf16[8,6144]{1,0:T(8,128)(2,1)S(1)}, bf16[8,6144]{1,0:T(8,128)(2,1)S(1)}, u32[]{:S(2)}, u32[]{:S(2)}) collective-permute-start(bf16[8,6144]{1,0:T(8,128)(2,1)S(1)} %shard_map.124), channel_id=1, source_target_pairs={{4,0},{8,4},{12,8},{14,12},{10,14},{6,10},{2,6},{0,2},{5,1},{9,5},... | collective-permute-start | bytes 294920 | tf_op jit(solution)/shard_map/ppermute | solution.py:312
  56.1 4.7 %collective-permute-start.18 = (bf16[8,6144]{1,0:T(8,128)(2,1)S(1)}, bf16[8,6144]{1,0:T(8,128)(2,1)S(1)}, u32[]{:S(2)}, u32[]{:S(2)}) collective-permute-start(bf16[8,6144]{1,0:T(8,128)(2,1)S(1)} %shard_map.122), channel_id=1, source_target_pairs={{0,4},{4,8},{8,12},{12,14},{14,10},{10,6},{6,2},{2,0},{1,5},{5,9},... | collective-permute-start | bytes 294920 | tf_op jit(solution)/shard_map/ppermute | solution.py:309
  58.1 2.7 %collective-permute-start.29 = (bf16[8,6144]{1,0:T(8,128)(2,1)S(1)}, bf16[8,6144]{1,0:T(8,128)(2,1)S(1)}, u32[]{:S(2)}, u32[]{:S(2)}) collective-permute-start(bf16[8,6144]{1,0:T(8,128)(2,1)S(1)} %shard_map.130), channel_id=1, source_target_pairs={{0,1},{1,0},{2,3},{3,2},{4,5},{5,4},{6,7},{7,6},{8,9},{9,8},{10,11... | collective-permute-start | bytes 294920 | tf_op jit(solution)/shard_map/ppermute | solution.py:354
  (4 other events, 41.1 us)

commit v5 on v4

--- a/solution.py
+++ b/solution.py
@@ -20,7 +20,27 @@
     return pltpu.with_memory_space_constraint(array, pltpu.HBM)
 
 
-def experts_kernel(rows_ref, gate_ref, upward_ref, act_ref):
+def load_kernel(after_ref, source_ref, held_ref, sem):
+    copy = pltpu.make_async_copy(source_ref, held_ref, sem)
+    copy.start()
+    copy.wait()
+
+
+def load(weights, after):
+    return pl.pallas_call(
+        load_kernel,
+        out_shape=pltpu.VMEM(weights.shape, weights.dtype),
+        in_specs=[pl.BlockSpec(memory_space=pl.ANY), pl.BlockSpec(memory_space=pltpu.HBM)],
+        out_specs=pl.BlockSpec(memory_space=pltpu.VMEM),
+        scratch_shapes=[pltpu.SemaphoreType.DMA],
+        compiler_params=pltpu.CompilerParams(vmem_limit_bytes=1 << 20),
+        cost_estimate=pl.CostEstimate(
+            flops=0, bytes_accessed=2 * weights.size, transcendentals=0
+        ),
+    )(after, in_hbm(weights))
+
+
+def experts_kernel(rows_ref, gate_ref, up_ref, act_ref):
     hidden = gate_ref.shape[1]
     step = math.gcd(hidden, 256)
     for at in range(0, hidden, step):
@@ -28,12 +48,13 @@
         gate_act = jnp.dot(
             rows_ref[...], gate_ref[:, columns], preferred_element_type=jnp.float32
         )
-        act_ref[:, columns] = (
-            gate_act / (1.0 + jnp.exp(-gate_act)) * upward_ref[:, columns]
-        ).astype(act_ref.dtype)
-
-
-def activate(rows, gate, upward):
+        upward = jnp.dot(rows_ref[...], up_ref[:, columns], preferred_element_type=jnp.float32)
+        act_ref[:, columns] = (gate_act / (1.0 + jnp.exp(-gate_act)) * upward).astype(
+            act_ref.dtype
+        )
+
+
+def activate(rows, gate, up):
     count, feat_width = rows.shape
     hidden = gate.shape[1]
     vmem = pl.BlockSpec(memory_space=pltpu.VMEM)
@@ -44,11 +65,11 @@
         out_specs=vmem,
         compiler_params=pltpu.CompilerParams(vmem_limit_bytes=8 << 20),
         cost_estimate=pl.CostEstimate(
-            flops=2 * count * feat_width * hidden,
-            bytes_accessed=2 * feat_width * hidden,
+            flops=4 * count * feat_width * hidden,
+            bytes_accessed=4 * feat_width * hidden,
             transcendentals=count * hidden,
         ),
-    )(rows, gate, upward)
+    )(rows, gate, up)
 
 
 def add_kernel(*refs):
@@ -139,52 +160,69 @@
     kv_width = key_ref.shape[2]
     kv_heads = kv_width // HEAD
     group = feat_width // kv_width
-    scale = 1.0 / math.sqrt(HEAD)
-    shape = (group * rows, rows * span)
+    scale = math.log2(math.e) / math.sqrt(HEAD)
+    eight = 8
+    half_span = eight * span
+    shape = (group * rows, half_span)
     column = lax.broadcasted_iota(jnp.int32, shape, 1)
-    request = lax.broadcasted_iota(jnp.int32, shape, 0) & (rows - 1)
-    first = request * span
+    first = (lax.broadcasted_iota(jnp.int32, shape, 0) & (eight - 1)) * span
     lengths = column_of(length_ref[...].astype(jnp.float32)).astype(jnp.int32)
     limit = first + jnp.concatenate([lengths] * group, 0)
     valid = (column >= first) & (column < limit)
-    total = jnp.zeros((rows, 1), jnp.float32)
-    for head in range(kv_heads):
+
+    def query_of(head):
+        wanted = range(head * group, (head + 1) * group)
+        return jnp.concatenate([query_ref[:, q * HEAD : (q + 1) * HEAD] for q in wanted], 0)
+
+    def scores_of(head):
         if head * 2 == kv_heads:
             copies[7].wait()
             copies[8].wait()
+        keys = key_ref[:, :, head * HEAD : (head + 1) * HEAD].reshape(rows * span, HEAD)
+        scores = lax.dot_general(
+            query_of(head), keys, (((1,), (1,)), ((), ())), preferred_element_type=jnp.float32
+        )
+        pieces = []
+        for at in range(0, group * rows, eight):
+            start = at % rows // eight * half_span
+            pieces.append(scores[at : at + eight, start : start + half_span])
+        return jnp.where(valid, jnp.concatenate(pieces, 0), -1e30)
+
+    total = jnp.zeros((rows, 1), jnp.float32)
+    empty = jnp.zeros((eight, half_span), jnp.float32)
+    scores = scores_of(0)
+    for head in range(kv_heads):
+        later = scores_of(head + 1) if head + 1 < kv_heads else None
         lanes = pl.ds(head * HEAD, HEAD)
-        wanted = [head * group + member for member in range(group)]
-        query = jnp.concatenate([query_ref[:, q * HEAD : (q + 1) * HEAD] for q in wanted], 0)
-        keys = key_ref[:, :, lanes].reshape(rows * span, HEAD)
-        scores = (
-            lax.dot_general(
-                query, keys, (((1,), (1,)), ((), ())), preferred_element_type=jnp.float32
-            )
-            * scale
-        )
-        scores = jnp.where(valid, scores, -1e30)
+        query = query_of(head).astype(jnp.float32)
         new_key = jnp.concatenate([new_key_ref[:, lanes].astype(jnp.float32)] * group, 0)
-        own_score = jnp.sum(query.astype(jnp.float32) * new_key, -1, keepdims=True) * scale
+        own_score = jnp.sum(query * new_key, -1, keepdims=True)
         top = jnp.maximum(jnp.max(scores, -1, keepdims=True), own_score)
-        powers = jnp.exp(scores - top)
-        own_power = jnp.exp(own_score - top)
+        powers = jnp.exp2((scores - top) * scale)
+        own_power = jnp.exp2((own_score - top) * scale)
         inverse = 1.0 / (jnp.sum(powers, -1, keepdims=True) + own_power)
-        attention = (powers * inverse).astype(jnp.bfloat16)
-        own_weight = (own_power * inverse).astype(jnp.bfloat16).astype(jnp.float32)
+        wide_rows = []
+        for at in range(0, group * rows, eight):
+            place = at % rows // eight
+            parts = [empty] * (rows // eight)
+            parts[place] = powers[at : at + eight]
+            wide_rows.append(jnp.concatenate(parts, 1))
+        attention = jnp.concatenate(wide_rows, 0).astype(jnp.bfloat16)
         if head == 0:
             for copy in copies[4:7]:
                 copy.wait()
         values = value_ref[:, :, lanes].reshape(rows * span, HEAD)
         mixed = jnp.dot(attention, values, preferred_element_type=jnp.float32)
         new_value = jnp.concatenate([new_value_ref[:, lanes].astype(jnp.float32)] * group, 0)
-        mixed = mixed + own_weight * new_value
-        for member, q in enumerate(wanted):
-            cols = pl.ds(q * HEAD, HEAD)
+        mixed = (mixed + own_power * new_value) * inverse
+        for member in range(group):
+            cols = pl.ds((head * group + member) * HEAD, HEAD)
             part = hidden_ref[:, cols].astype(jnp.float32) + mixed[
                 member * rows : (member + 1) * rows
             ]
             residual_ref[:, cols] = part
             total = total + jnp.sum(part, -1, keepdims=True)
+        scores = later
     centre = total * (1.0 / feat_width)
     spread = jnp.zeros((rows, 1), jnp.float32)
     wide = 1024
@@ -225,21 +263,42 @@
 
 
 def tail_kernel(
-    residual_ref, slots_ref, weights_ref, first_ref, second_ref, third_ref, back_ref, out_ref
+    residual_ref,
+    slots_ref,
+    weights_ref,
+    first_ref,
+    second_ref,
+    third_ref,
+    back_ref,
+    out_ref,
+    result_ref,
+    sems,
 ):
-    cap = back_ref.shape[0]
-    own = (
-        first_ref[...].astype(jnp.float32)
-        + second_ref[...].astype(jnp.float32)
-        + third_ref[...].astype(jnp.float32)
-    ).astype(jnp.bfloat16)
-    result = residual_ref[...]
-    for place, block in enumerate((own, back_ref[...])):
-        picks = slots_ref[place * cap : (place + 1) * cap, :].astype(jnp.bfloat16)
-        result = result + weights_ref[:, place : place + 1] * lax.dot_general(
-            picks, block, (((0,), (0,)), ((), ())), preferred_element_type=jnp.float32
-        )
-    out_ref[...] = result
+    cap, width = back_ref.shape
+    wide = width // sems.shape[0]
+    copies = []
+    for at in range(sems.shape[0]):
+        columns = slice(at * wide, (at + 1) * wide)
+        own = (
+            first_ref[:, columns].astype(jnp.float32)
+            + second_ref[:, columns].astype(jnp.float32)
+            + third_ref[:, columns].astype(jnp.float32)
+        ).astype(jnp.bfloat16)
+        result = residual_ref[:, columns]
+        for place, block in enumerate((own, back_ref[:, columns])):
+            picks = slots_ref[place * cap : (place + 1) * cap, :].astype(jnp.bfloat16)
+            result = result + weights_ref[:, place : place + 1] * lax.dot_general(
+                picks, block, (((0,), (0,)), ((), ())), preferred_element_type=jnp.float32
+            )
+        result_ref[:, columns] = result
+        copies.append(
+            pltpu.make_async_copy(
+                result_ref.at[:, columns], out_ref.at[:, columns], sems.at[at]
+            )
+        )
+        copies[-1].start()
+    for copy in copies:
+        copy.wait()
 
 
 def body(
@@ -322,13 +381,13 @@
             theirs_l.append(go_left(theirs_l[-1]))
     theirs_l.append(lax.ppermute(theirs_l[half - 2], "attn", left_two))
 
+    up = load(w_up[0], theirs_r[half - 2])
     blocks = [own, theirs]
     for step in range(1, half):
         blocks += [own_r[step], own_l[step], theirs_r[step], theirs_l[step]]
     blocks += [own_r[half], theirs_l[half]]
     rows = jnp.concatenate(blocks)
-    upward = jnp.dot(rows, w_up[0], preferred_element_type=jnp.float32)
-    active = activate(rows, gate, upward)
+    active = activate(rows, gate, up)
     share = jnp.dot(active, w_down[0], preferred_element_type=jnp.float32)
     share = share.astype(jnp.bfloat16).reshape(len(blocks), cap_slots, feat_width)
     own_share = {0: share[0], half: share[-2]}
@@ -356,7 +415,11 @@
         tail_kernel,
         out_shape=jax.ShapeDtypeStruct((row_count, feat_width), jnp.float32),
         in_specs=[vmem] * 7,
-        out_specs=vmem,
+        out_specs=pl.BlockSpec(memory_space=pltpu.HBM),
+        scratch_shapes=[
+            pltpu.VMEM((row_count, feat_width), jnp.float32),
+            pltpu.SemaphoreType.DMA((4,)),
+        ],
         compiler_params=pltpu.CompilerParams(vmem_limit_bytes=4 << 20),
     )(
         residual,

time: 62 us -> 60.9 us (0.982)
  Pallas kernels: 9.21 us -> 13.2 us
  waiting for transfers between devices: 17.3 us -> 14.7 us
  matrix products: 2.87 us -> 1.4 us
  local copies, waits for them, and re-layouts: 1.27 us -> 0.35 us
    ppermute x14, starting transfers between devices: 17 us -> 5.09 us  [go_right(): return lax.ppermute(block, 'attn', right)]
    ppermute x13, starting transfers between devices: 11 us -> 22.8 us  [go_left(): return lax.ppermute(block, 'attn', left)]
    ppermute x14, waiting for transfers between devices: 8.19 us -> 4.13 us  [go_right(): return lax.ppermute(block, 'attn', right)]
    pallas_call x0 -> x1, Pallas kernels: none -> 3.69 us  [load(): pl.pallas_call(load_kernel, out_shape=pltpu.VMEM(weights.shape, weights.d...]
    dot_general x1 -> x0, matrix products: 1.48 us -> none  [body(): upward = jnp.dot(rows, w_up[0], preferred_element_type=jnp.float32)]
    ppermute x13, waiting for transfers between devices: 7.86 us -> 9.26 us  [go_left(): return lax.ppermute(block, 'attn', left)]
    pallas_call x1, Pallas kernels: 1.44 us -> 2.76 us  [activate(): pl.pallas_call(experts_kernel, out_shape=jax.ShapeDtypeStruct((count, hid...]
    pallas_call x1, Pallas kernels: 6.43 us -> 5.5 us  [body(): pl.pallas_call(front_kernel, out_shape=(jax.ShapeDtypeStruct((row_count,...]
  transfers between devices with their start and end apart: 30 -> 30, of which waited for: 13 -> 13; matrix products, arithmetic and copies ran while one was open for 0% -> 0% of each run, Pallas kernels for 0% -> 7%
where the time goes in v5:
time: 60.9 us; the launch traced here: 60.7 us
  starting transfers between devices  30.8 us (51%)
  waiting for transfers between devices  14.7 us (24%)
  Pallas kernels  13.2 us (22%)
  matrix products  1.4 us (2%)
    ppermute x13, starting transfers between devices, go_left(): return lax.ppermute(block, 'attn', left)  22.8 us
    ppermute x13, waiting for transfers between devices, go_left(): return lax.ppermute(block, 'attn', left)  9.26 us
    pallas_call x1, Pallas kernels, body(): pl.pallas_call(front_kernel, out_shape=(jax.ShapeDtypeStruct((row_count,...  5.5 us
    ppermute x14, starting transfers between devices, go_right(): return lax.ppermute(block, 'attn', right)  5.09 us
    ppermute x14, waiting for transfers between devices, go_right(): return lax.ppermute(block, 'attn', right)  4.13 us
    pallas_call x1, Pallas kernels, load(): pl.pallas_call(load_kernel, out_shape=pltpu.VMEM(weights.shape, weights.d...  3.69 us
    ppermute x1, starting transfers between devices, body(): theirs_l.append(lax.ppermute(theirs_l[half - 2], 'attn', left_two))  2.79 us
    pallas_call x1, Pallas kernels, activate(): pl.pallas_call(experts_kernel, out_shape=jax.ShapeDtypeStruct((count, hid...  2.76 us
  transfers between devices with their start and end apart: 30, of which 13 were waited for; matrix products, arithmetic and copies ran while one was open for 0% of the time, Pallas kernels for 7%

profile of v5, /device:TPU:0, one launch (start us, length us, event | category | flops | bytes accessed | tf_op | source)
XLA Modules:
  0.0 60.7 jit_solution(11851083860642594536)
XLA Ops:
  0.0 5.5 %shard_map.118 = (f32[16,6144]{1,0:T(8,128)S(1)}, bf16[8,6144]{1,0:T(8,128)(2,1)S(1)}, bf16[8,6144]{1,0:T(8,128)(2,1)S(1)}, f32[16,16]{1,0:T(8,128)S(1)}, f32[16...) custom-call(s32[1]{0:T(128)} %bitcast.here_ref, bf16[16,6144]{1,0:T(8,128)(2,1)} %hidden_hbm.1, bf16[16,6144]{1,0:T(8,128)(2,1)} %query_hbm.1, ...), custom_call_target="tpu_custom_call" | custom-call | flops 1000000000 | bytes 40000000 | tf_op jit(solution)/shard_map/pallas_call | solution.py:335
  5.5 3.0 %collective-permute-start.2 = (bf16[8,6144]{1,0:T(8,128)(2,1)S(1)}, bf16[8,6144]{1,0:T(8,128)(2,1)S(1)}, u32[]{:S(2)}, u32[]{:S(2)}) collective-permute-start(bf16[8,6144]{1,0:T(8,128)(2,1)S(1)} %get-tuple-element.14), channel_id=1, source_target_pairs={{4,0},{8,4},{12,8},{14,12},{10,14},{6,10},{2,6},{0,2},{5,1},{9,5},... | collective-permute-start | bytes 294920 | tf_op jit(solution)/shard_map/ppermute | solution.py:371
  8.7 1.3 %collective-permute-done = bf16[8,6144]{1,0:T(8,128)(2,1)S(1)} collective-permute-done((bf16[8,6144]{1,0:T(8,128)(2,1)S(1)}, bf16[8,6144]{1,0:T(8,128)(2,1)S(1)}, u32[]{:S(2)}, u32[]{:S(2)}) %collective-permute-start) | collective-permute-done | bytes 98336 | tf_op jit(solution)/shard_map/ppermute | solution.py:374
  10.0 1.9 %collective-permute-start.4 = (bf16[8,6144]{1,0:T(8,128)(2,1)S(1)}, bf16[8,6144]{1,0:T(8,128)(2,1)S(1)}, u32[]{:S(2)}, u32[]{:S(2)}) collective-permute-start(bf16[8,6144]{1,0:T(8,128)(2,1)S(1)} %collective-permute-done), channel_id=1, source_target_pairs={{4,0},{8,4},{12,8},{14,12},{10,14},{6,10},{2,6},{0,2},{5,1},{9,5},... | collective-permute-start | bytes 294920 | tf_op jit(solution)/shard_map/ppermute | solution.py:371
  12.0 1.9 %collective-permute-start.6 = (bf16[8,6144]{1,0:T(8,128)(2,1)S(1)}, bf16[8,6144]{1,0:T(8,128)(2,1)S(1)}, u32[]{:S(2)}, u32[]{:S(2)}) collective-permute-start(bf16[8,6144]{1,0:T(8,128)(2,1)S(1)} %collective-permute-done.2), channel_id=1, source_target_pairs={{4,0},{8,4},{12,8},{14,12},{10,14},{6,10},{2,6},{0,2},{5,1},{9,5},... | collective-permute-start | bytes 294920 | tf_op jit(solution)/shard_map/ppermute | solution.py:371
  14.0 1.5 %collective-permute-done.4 = bf16[8,6144]{1,0:T(8,128)(2,1)S(1)} collective-permute-done((bf16[8,6144]{1,0:T(8,128)(2,1)S(1)}, bf16[8,6144]{1,0:T(8,128)(2,1)S(1)}, u32[]{:S(2)}, u32[]{:S(2)}) %collective-permute-start.4) | collective-permute-done | bytes 98336 | tf_op jit(solution)/shard_map/ppermute | solution.py:371
  15.6 1.8 %collective-permute-start.8 = (bf16[8,6144]{1,0:T(8,128)(2,1)S(1)}, bf16[8,6144]{1,0:T(8,128)(2,1)S(1)}, u32[]{:S(2)}, u32[]{:S(2)}) collective-permute-start(bf16[8,6144]{1,0:T(8,128)(2,1)S(1)} %collective-permute-done.4), channel_id=1, source_target_pairs={{4,0},{8,4},{12,8},{14,12},{10,14},{6,10},{2,6},{0,2},{5,1},{9,5},... | collective-permute-start | bytes 294920 | tf_op jit(solution)/shard_map/ppermute | solution.py:371
  17.6 1.8 %collective-permute-start.10 = (bf16[8,6144]{1,0:T(8,128)(2,1)S(1)}, bf16[8,6144]{1,0:T(8,128)(2,1)S(1)}, u32[]{:S(2)}, u32[]{:S(2)}) collective-permute-start(bf16[8,6144]{1,0:T(8,128)(2,1)S(1)} %collective-permute-done.6), channel_id=1, source_target_pairs={{4,0},{8,4},{12,8},{14,12},{10,14},{6,10},{2,6},{0,2},{5,1},{9,5},... | collective-permute-start | bytes 294920 | tf_op jit(solution)/shard_map/ppermute | solution.py:371
  19.7 1.4 %collective-permute-done.8 = bf16[8,6144]{1,0:T(8,128)(2,1)S(1)} collective-permute-done((bf16[8,6144]{1,0:T(8,128)(2,1)S(1)}, bf16[8,6144]{1,0:T(8,128)(2,1)S(1)}, u32[]{:S(2)}, u32[]{:S(2)}) %collective-permute-start.8) | collective-permute-done | bytes 98336 | tf_op jit(solution)/shard_map/ppermute | solution.py:371
  21.1 2.8 %collective-permute-start.14 = (bf16[8,6144]{1,0:T(8,128)(2,1)S(1)}, bf16[8,6144]{1,0:T(8,128)(2,1)S(1)}, u32[]{:S(2)}, u32[]{:S(2)}) collective-permute-start(bf16[8,6144]{1,0:T(8,128)(2,1)S(1)} %collective-permute-done.8), channel_id=1, source_target_pairs={{8,0},{12,4},{14,8},{10,12},{6,14},{2,10},{0,6},{4,2},{9,1},{13,5}... | collective-permute-start | bytes 294920 | tf_op jit(solution)/shard_map/ppermute | solution.py:382
  23.8 1.6 %collective-permute-start.12 = (bf16[8,6144]{1,0:T(8,128)(2,1)S(1)}, bf16[8,6144]{1,0:T(8,128)(2,1)S(1)}, u32[]{:S(2)}, u32[]{:S(2)}) collective-permute-start(bf16[8,6144]{1,0:T(8,128)(2,1)S(1)} %collective-permute-done.8), channel_id=1, source_target_pairs={{4,0},{8,4},{12,8},{14,12},{10,14},{6,10},{2,6},{0,2},{5,1},{9,5},... | collective-permute-start | bytes 294920 | tf_op jit(solution)/shard_map/ppermute | solution.py:371
  26.4 3.7 %shard_map.119.up_ref = bf16[6144,768]{1,0:T(8,128)(2,1)S(1)} custom-call(bf16[8,6144]{1,0:T(8,128)(2,1)S(1)} %collective-permute-done.7.after_ref, bf16[6144,768]{1,0:T(8,128)(2,1)} %bitcast.15), custom_call_target="tpu_custom_call" | custom-call | bytes 9437184 | tf_op jit(solution)/shard_map/pallas_call | solution.py:30
  30.2 0.9 %collective-permute-done.13 = bf16[8,6144]{1,0:T(8,128)(2,1)S(1)} collective-permute-done((bf16[8,6144]{1,0:T(8,128)(2,1)S(1)}, bf16[8,6144]{1,0:T(8,128)(2,1)S(1)}, u32[]{:S(2)}, u32[]{:S(2)}) %collective-permute-start.13) | collective-permute-done | bytes 98336 | tf_op jit(solution)/shard_map/ppermute | solution.py:368
  31.2 2.8 %shard_map.120 = bf16[128,768]{1,0:T(8,128)(2,1)S(1)} custom-call(bf16[128,6144]{1,0:T(8,128)(2,1)S(1)} %constant_dynamic-update-slice_fusion.rows_ref, bf16[6144,768]{1,0:T(8,128)(2,1)S(1)} %get-tuple-element.16.gate_ref, bf16[6144,768]{1,0:T(8,128)(2,1)S(1)} %shard_map.119.up_ref), custom_call_target="tpu_custom_call" | custom-call | flops 2415919104 | bytes 18874368 | tf_op jit(solution)/shard_map/pallas_call | solution.py:61
  34.0 1.4 %fusion.2 = bf16[128,6144]{1,0:T(8,128)(2,1)S(1)} fusion(bf16[128,768]{1,0:T(8,128)(2,1)S(1)} %shard_map.120, bf16[1,768,6144]{2,1,0:T(8,128)(2,1)S(1)} %bitcast.13), kind=kOutput, calls=%fused_computation.2 | convolution fusion | flops 1208745984 | bytes 11206656 | tf_op jit(solution)/shard_map/dot_general | solution.py:391
  35.6 1.8 %collective-permute-start.22 = (bf16[8,6144]{1,0:T(8,128)(2,1)S(1)}, bf16[8,6144]{1,0:T(8,128)(2,1)S(1)}, u32[]{:S(2)}, u32[]{:S(2)}) collective-permute-start(bf16[8,6144]{1,0:T(8,128)(2,1)S(1)} %get-tuple-element.23), channel_id=1, source_target_pairs={{4,0},{8,4},{12,8},{14,12},{10,14},{6,10},{2,6},{0,2},{5,1},{9,5},... | collective-permute-start | bytes 294920 | tf_op jit(solution)/shard_map/ppermute | solution.py:371
  38.1 3.1 %collective-permute-done.22.refs_0_ = bf16[8,6144]{1,0:T(8,128)(2,1)S(1)} collective-permute-done((bf16[8,6144]{1,0:T(8,128)(2,1)S(1)}, bf16[8,6144]{1,0:T(8,128)(2,1)S(1)}, u32[]{:S(2)}, u32[]{:S(2)}) %collective-permute-start.22) | collective-permute-done | bytes 98336 | tf_op jit(solution)/shard_map/ppermute | solution.py:371
  41.3 1.4 %collective-permute-start.23 = (bf16[8,6144]{1,0:T(8,128)(2,1)S(1)}, bf16[8,6144]{1,0:T(8,128)(2,1)S(1)}, u32[]{:S(2)}, u32[]{:S(2)}) collective-permute-start(bf16[8,6144]{1,0:T(8,128)(2,1)S(1)} %shard_map.126), channel_id=1, source_target_pairs={{4,0},{8,4},{12,8},{14,12},{10,14},{6,10},{2,6},{0,2},{5,1},{9,5},... | collective-permute-start | bytes 294920 | tf_op jit(solution)/shard_map/ppermute | solution.py:371
  42.6 1.5 %collective-permute-start.19 = (bf16[8,6144]{1,0:T(8,128)(2,1)S(1)}, bf16[8,6144]{1,0:T(8,128)(2,1)S(1)}, u32[]{:S(2)}, u32[]{:S(2)}) collective-permute-start(bf16[8,6144]{1,0:T(8,128)(2,1)S(1)} %get-tuple-element.27), channel_id=1, source_target_pairs={{4,0},{8,4},{12,8},{14,12},{10,14},{6,10},{2,6},{0,2},{5,1},{9,5},... | collective-permute-start | bytes 294920 | tf_op jit(solution)/shard_map/ppermute | solution.py:371
  44.2 0.5 collective-permute-start.16
  44.8 0.8 %collective-permute-start.27 = (bf16[8,6144]{1,0:T(8,128)(2,1)S(1)}, bf16[8,6144]{1,0:T(8,128)(2,1)S(1)}, u32[]{:S(2)}, u32[]{:S(2)}) collective-permute-start(bf16[8,6144]{1,0:T(8,128)(2,1)S(1)} %shard_map.129), channel_id=1, source_target_pairs={{0,4},{4,8},{8,12},{12,14},{14,10},{10,6},{6,2},{2,0},{1,5},{5,9},... | collective-permute-start | bytes 294920 | tf_op jit(solution)/shard_map/ppermute | solution.py:368
  45.6 1.0 %collective-permute-done.23.refs_0_ = bf16[8,6144]{1,0:T(8,128)(2,1)S(1)} collective-permute-done((bf16[8,6144]{1,0:T(8,128)(2,1)S(1)}, bf16[8,6144]{1,0:T(8,128)(2,1)S(1)}, u32[]{:S(2)}, u32[]{:S(2)}) %collective-permute-start.23) | collective-permute-done | bytes 98336 | tf_op jit(solution)/shard_map/ppermute | solution.py:371
  46.6 1.6 %collective-permute-start.24 = (bf16[8,6144]{1,0:T(8,128)(2,1)S(1)}, bf16[8,6144]{1,0:T(8,128)(2,1)S(1)}, u32[]{:S(2)}, u32[]{:S(2)}) collective-permute-start(bf16[8,6144]{1,0:T(8,128)(2,1)S(1)} %shard_map.127), channel_id=1, source_target_pairs={{4,0},{8,4},{12,8},{14,12},{10,14},{6,10},{2,6},{0,2},{5,1},{9,5},... | collective-permute-start | bytes 294920 | tf_op jit(solution)/shard_map/ppermute | solution.py:371
  48.2 1.2 %collective-permute-start.20 = (bf16[8,6144]{1,0:T(8,128)(2,1)S(1)}, bf16[8,6144]{1,0:T(8,128)(2,1)S(1)}, u32[]{:S(2)}, u32[]{:S(2)}) collective-permute-start(bf16[8,6144]{1,0:T(8,128)(2,1)S(1)} %shard_map.124), channel_id=1, source_target_pairs={{4,0},{8,4},{12,8},{14,12},{10,14},{6,10},{2,6},{0,2},{5,1},{9,5},... | collective-permute-start | bytes 294920 | tf_op jit(solution)/shard_map/ppermute | solution.py:371
  49.9 0.6 collective-permute-start.17
  50.4 0.7 %collective-permute-done.27.refs_0_ = bf16[8,6144]{1,0:T(8,128)(2,1)S(1)} collective-permute-done((bf16[8,6144]{1,0:T(8,128)(2,1)S(1)}, bf16[8,6144]{1,0:T(8,128)(2,1)S(1)}, u32[]{:S(2)}, u32[]{:S(2)}) %collective-permute-start.27) | collective-permute-done | bytes 98336 | tf_op jit(solution)/shard_map/ppermute | solution.py:368
  51.7 1.6 %collective-permute-start.25 = (bf16[8,6144]{1,0:T(8,128)(2,1)S(1)}, bf16[8,6144]{1,0:T(8,128)(2,1)S(1)}, u32[]{:S(2)}, u32[]{:S(2)}) collective-permute-start(bf16[8,6144]{1,0:T(8,128)(2,1)S(1)} %shard_map.128), channel_id=1, source_target_pairs={{4,0},{8,4},{12,8},{14,12},{10,14},{6,10},{2,6},{0,2},{5,1},{9,5},... | collective-permute-start | bytes 294920 | tf_op jit(solution)/shard_map/ppermute | solution.py:371
  53.3 1.7 %collective-permute-start.21 = (bf16[8,6144]{1,0:T(8,128)(2,1)S(1)}, bf16[8,6144]{1,0:T(8,128)(2,1)S(1)}, u32[]{:S(2)}, u32[]{:S(2)}) collective-permute-start(bf16[8,6144]{1,0:T(8,128)(2,1)S(1)} %shard_map.125), channel_id=1, source_target_pairs={{4,0},{8,4},{12,8},{14,12},{10,14},{6,10},{2,6},{0,2},{5,1},{9,5},... | collective-permute-start | bytes 294920 | tf_op jit(solution)/shard_map/ppermute | solution.py:371
  55.8 0.6 collective-permute-done.25.refs_1_
  56.5 1.5 %collective-permute-done.21.third_ref = bf16[8,6144]{1,0:T(8,128)(2,1)S(1)} collective-permute-done((bf16[8,6144]{1,0:T(8,128)(2,1)S(1)}, bf16[8,6144]{1,0:T(8,128)(2,1)S(1)}, u32[]{:S(2)}, u32[]{:S(2)}) %collective-permute-start.21) | collective-permute-done | bytes 98336 | tf_op jit(solution)/shard_map/ppermute | solution.py:371
  58.0 1.8 %collective-permute-done.18.second_ref = bf16[8,6144]{1,0:T(8,128)(2,1)S(1)} collective-permute-done((bf16[8,6144]{1,0:T(8,128)(2,1)S(1)}, bf16[8,6144]{1,0:T(8,128)(2,1)S(1)}, u32[]{:S(2)}, u32[]{:S(2)}) %collective-permute-start.18) | collective-permute-done | bytes 98336 | tf_op jit(solution)/shard_map/ppermute | solution.py:368
  59.7 1.0 %shard_map.132 = f32[16,6144]{1,0:T(8,128)} custom-call(f32[16,6144]{1,0:T(8,128)S(1)} %get-tuple-element.11.residual_ref, f32[16,16]{1,0:T(8,128)S(1)} %get-tuple-element.12.slots_ref, f32[16,2]{1,0:T(8,128)S(1)} %get-tuple-element.13.weights_ref, bf16[8,6144]{1,0:T(8,128)(2,1)S(1)} %get-tuple-element.32.first_ref, ...), custom_call_target="tpu_custom_call" | custom-call | tf_op jit(solution)/shard_map/pallas_call | solution.py:414
  (68 shorter events, 4.9 us)
Async XLA Ops:
  5.5 6.5 %collective-permute-start.2 = (bf16[8,6144]{1,0:T(8,128)(2,1)S(1)}, bf16[8,6144]{1,0:T(8,128)(2,1)S(1)}, u32[]{:S(2)}, u32[]{:S(2)}) collective-permute-start(bf16[8,6144]{1,0:T(8,128)(2,1)S(1)} %get-tuple-element.14), channel_id=1, source_target_pairs={{4,0},{8,4},{12,8},{14,12},{10,14},{6,10},{2,6},{0,2},{5,1},{9,5},... | collective-permute-start | bytes 294920 | tf_op jit(solution)/shard_map/ppermute | solution.py:371
  8.5 5.4 %collective-permute-start.1 = (bf16[8,6144]{1,0:T(8,128)(2,1)S(1)}, bf16[8,6144]{1,0:T(8,128)(2,1)S(1)}, u32[]{:S(2)}, u32[]{:S(2)}) collective-permute-start(bf16[8,6144]{1,0:T(8,128)(2,1)S(1)} %get-tuple-element.14), channel_id=1, source_target_pairs={{0,4},{4,8},{8,12},{12,14},{14,10},{10,6},{6,2},{2,0},{1,5},{5,9},... | collective-permute-start | bytes 294920 | tf_op jit(solution)/shard_map/ppermute | solution.py:368
  8.6 1.3 %collective-permute-start = (bf16[8,6144]{1,0:T(8,128)(2,1)S(1)}, bf16[8,6144]{1,0:T(8,128)(2,1)S(1)}, u32[]{:S(2)}, u32[]{:S(2)}) collective-permute-start(bf16[8,6144]{1,0:T(8,128)(2,1)S(1)} %get-tuple-element.15), channel_id=1, source_target_pairs={{0,1},{1,0},{2,3},{3,2},{4,5},{5,4},{6,7},{7,6},{8,9},{9,8},{10,11... | collective-permute-start | bytes 294920 | tf_op jit(solution)/shard_map/ppermute | solution.py:374
  10.0 5.6 %collective-permute-start.4 = (bf16[8,6144]{1,0:T(8,128)(2,1)S(1)}, bf16[8,6144]{1,0:T(8,128)(2,1)S(1)}, u32[]{:S(2)}, u32[]{:S(2)}) collective-permute-start(bf16[8,6144]{1,0:T(8,128)(2,1)S(1)} %collective-permute-done), channel_id=1, source_target_pairs={{4,0},{8,4},{12,8},{14,12},{10,14},{6,10},{2,6},{0,2},{5,1},{9,5},... | collective-permute-start | bytes 294920 | tf_op jit(solution)/shard_map/ppermute | solution.py:371
  11.9 5.5 %collective-permute-start.3 = (bf16[8,6144]{1,0:T(8,128)(2,1)S(1)}, bf16[8,6144]{1,0:T(8,128)(2,1)S(1)}, u32[]{:S(2)}, u32[]{:S(2)}) collective-permute-start(bf16[8,6144]{1,0:T(8,128)(2,1)S(1)} %collective-permute-done), channel_id=1, source_target_pairs={{0,4},{4,8},{8,12},{12,14},{14,10},{10,6},{6,2},{2,0},{1,5},{5,9},... | collective-permute-start | bytes 294920 | tf_op jit(solution)/shard_map/ppermute | solution.py:368
  12.0 5.6 %collective-permute-start.6 = (bf16[8,6144]{1,0:T(8,128)(2,1)S(1)}, bf16[8,6144]{1,0:T(8,128)(2,1)S(1)}, u32[]{:S(2)}, u32[]{:S(2)}) collective-permute-start(bf16[8,6144]{1,0:T(8,128)(2,1)S(1)} %collective-permute-done.2), channel_id=1, source_target_pairs={{4,0},{8,4},{12,8},{14,12},{10,14},{6,10},{2,6},{0,2},{5,1},{9,5},... | collective-permute-start | bytes 294920 | tf_op jit(solution)/shard_map/ppermute | solution.py:371
  13.9 5.5 %collective-permute-start.5 = (bf16[8,6144]{1,0:T(8,128)(2,1)S(1)}, bf16[8,6144]{1,0:T(8,128)(2,1)S(1)}, u32[]{:S(2)}, u32[]{:S(2)}) collective-permute-start(bf16[8,6144]{1,0:T(8,128)(2,1)S(1)} %collective-permute-done.1), channel_id=1, source_target_pairs={{0,4},{4,8},{8,12},{12,14},{14,10},{10,6},{6,2},{2,0},{1,5},{5,9},... | collective-permute-start | bytes 294920 | tf_op jit(solution)/shard_map/ppermute | solution.py:368
  15.6 5.5 %collective-permute-start.8 = (bf16[8,6144]{1,0:T(8,128)(2,1)S(1)}, bf16[8,6144]{1,0:T(8,128)(2,1)S(1)}, u32[]{:S(2)}, u32[]{:S(2)}) collective-permute-start(bf16[8,6144]{1,0:T(8,128)(2,1)S(1)} %collective-permute-done.4), channel_id=1, source_target_pairs={{4,0},{8,4},{12,8},{14,12},{10,14},{6,10},{2,6},{0,2},{5,1},{9,5},... | collective-permute-start | bytes 294920 | tf_op jit(solution)/shard_map/ppermute | solution.py:371
  17.4 8.0 %collective-permute-start.7 = (bf16[8,6144]{1,0:T(8,128)(2,1)S(1)}, bf16[8,6144]{1,0:T(8,128)(2,1)S(1)}, u32[]{:S(2)}, u32[]{:S(2)}) collective-permute-start(bf16[8,6144]{1,0:T(8,128)(2,1)S(1)} %collective-permute-done.3), channel_id=1, source_target_pairs={{0,4},{4,8},{8,12},{12,14},{14,10},{10,6},{6,2},{2,0},{1,5},{5,9},... | collective-permute-start | bytes 294920 | tf_op jit(solution)/shard_map/ppermute | solution.py:368
  17.6 8.8 %collective-permute-start.10 = (bf16[8,6144]{1,0:T(8,128)(2,1)S(1)}, bf16[8,6144]{1,0:T(8,128)(2,1)S(1)}, u32[]{:S(2)}, u32[]{:S(2)}) collective-permute-start(bf16[8,6144]{1,0:T(8,128)(2,1)S(1)} %collective-permute-done.6), channel_id=1, source_target_pairs={{4,0},{8,4},{12,8},{14,12},{10,14},{6,10},{2,6},{0,2},{5,1},{9,5},... | collective-permute-start | bytes 294920 | tf_op jit(solution)/shard_map/ppermute | solution.py:371
  19.4 6.5 %collective-permute-start.9 = (bf16[8,6144]{1,0:T(8,128)(2,1)S(1)}, bf16[8,6144]{1,0:T(8,128)(2,1)S(1)}, u32[]{:S(2)}, u32[]{:S(2)}) collective-permute-start(bf16[8,6144]{1,0:T(8,128)(2,1)S(1)} %collective-permute-done.5), channel_id=1, source_target_pairs={{0,4},{4,8},{8,12},{12,14},{14,10},{10,6},{6,2},{2,0},{1,5},{5,9},... | collective-permute-start | bytes 294920 | tf_op jit(solution)/shard_map/ppermute | solution.py:368
  21.1 10.1 %collective-permute-start.14 = (bf16[8,6144]{1,0:T(8,128)(2,1)S(1)}, bf16[8,6144]{1,0:T(8,128)(2,1)S(1)}, u32[]{:S(2)}, u32[]{:S(2)}) collective-permute-start(bf16[8,6144]{1,0:T(8,128)(2,1)S(1)} %collective-permute-done.8), channel_id=1, source_target_pairs={{8,0},{12,4},{14,8},{10,12},{6,14},{2,10},{0,6},{4,2},{9,1},{13,5}... | collective-permute-start | bytes 294920 | tf_op jit(solution)/shard_map/ppermute | solution.py:382
  23.8 6.3 %collective-permute-start.12 = (bf16[8,6144]{1,0:T(8,128)(2,1)S(1)}, bf16[8,6144]{1,0:T(8,128)(2,1)S(1)}, u32[]{:S(2)}, u32[]{:S(2)}) collective-permute-start(bf16[8,6144]{1,0:T(8,128)(2,1)S(1)} %collective-permute-done.8), channel_id=1, source_target_pairs={{4,0},{8,4},{12,8},{14,12},{10,14},{6,10},{2,6},{0,2},{5,1},{9,5},... | collective-permute-start | bytes 294920 | tf_op jit(solution)/shard_map/ppermute | solution.py:371
  25.4 4.7 %collective-permute-start.11 = (bf16[8,6144]{1,0:T(8,128)(2,1)S(1)}, bf16[8,6144]{1,0:T(8,128)(2,1)S(1)}, u32[]{:S(2)}, u32[]{:S(2)}) collective-permute-start(bf16[8,6144]{1,0:T(8,128)(2,1)S(1)} %collective-permute-done.7.after_ref), channel_id=1, source_target_pairs={{0,4},{4,8},{8,12},{12,14},{14,10},{10,6},{6,2},{2,0},{1,5},{5,9},... | collective-permute-start | bytes 294920 | tf_op jit(solution)/shard_map/ppermute | solution.py:368
  25.9 5.2 %collective-permute-start.13 = (bf16[8,6144]{1,0:T(8,128)(2,1)S(1)}, bf16[8,6144]{1,0:T(8,128)(2,1)S(1)}, u32[]{:S(2)}, u32[]{:S(2)}) collective-permute-start(bf16[8,6144]{1,0:T(8,128)(2,1)S(1)} %collective-permute-done.9), channel_id=1, source_target_pairs={{0,4},{4,8},{8,12},{12,14},{14,10},{10,6},{6,2},{2,0},{1,5},{5,9},... | collective-permute-start | bytes 294920 | tf_op jit(solution)/shard_map/ppermute | solution.py:368
  30.1 3.8 %slice-start = ((s8[9437184]{0:T(1024)(128)(4,1)}), s8[4194304]{0:T(1024)(128)(4,1)S(1)}, s32[]{:S(2)}) async-start(s8[9437184]{0:T(1024)(128)(4,1)} %bitcast.12), calls=%async_computation | async-start | bytes 8388608
  31.2 2.9 %slice-start.2 = ((s8[9437184]{0:T(1024)(128)(4,1)}), s8[1048576]{0:T(1024)(128)(4,1)S(1)}, s32[]{:S(2)}) async-start(s8[9437184]{0:T(1024)(128)(4,1)} %bitcast.12), calls=%async_computation.2 | async-start | bytes 2097152
  35.6 5.7 %collective-permute-start.22 = (bf16[8,6144]{1,0:T(8,128)(2,1)S(1)}, bf16[8,6144]{1,0:T(8,128)(2,1)S(1)}, u32[]{:S(2)}, u32[]{:S(2)}) collective-permute-start(bf16[8,6144]{1,0:T(8,128)(2,1)S(1)} %get-tuple-element.23), channel_id=1, source_target_pairs={{4,0},{8,4},{12,8},{14,12},{10,14},{6,10},{2,6},{0,2},{5,1},{9,5},... | collective-permute-start | bytes 294920 | tf_op jit(solution)/shard_map/ppermute | solution.py:371
  37.4 6.8 %collective-permute-start.15 = (bf16[8,6144]{1,0:T(8,128)(2,1)S(1)}, bf16[8,6144]{1,0:T(8,128)(2,1)S(1)}, u32[]{:S(2)}, u32[]{:S(2)}) collective-permute-start(bf16[8,6144]{1,0:T(8,128)(2,1)S(1)} %get-tuple-element.31), channel_id=1, source_target_pairs={{0,4},{4,8},{8,12},{12,14},{14,10},{10,6},{6,2},{2,0},{1,5},{5,9},... | collective-permute-start | bytes 294920 | tf_op jit(solution)/shard_map/ppermute | solution.py:368
  37.7 7.1 %collective-permute-start.26 = (bf16[8,6144]{1,0:T(8,128)(2,1)S(1)}, bf16[8,6144]{1,0:T(8,128)(2,1)S(1)}, u32[]{:S(2)}, u32[]{:S(2)}) collective-permute-start(bf16[8,6144]{1,0:T(8,128)(2,1)S(1)} %get-tuple-element.19), channel_id=1, source_target_pairs={{0,4},{4,8},{8,12},{12,14},{14,10},{10,6},{6,2},{2,0},{1,5},{5,9},... | collective-permute-start | bytes 294920 | tf_op jit(solution)/shard_map/ppermute | solution.py:368
  41.3 5.3 %collective-permute-start.23 = (bf16[8,6144]{1,0:T(8,128)(2,1)S(1)}, bf16[8,6144]{1,0:T(8,128)(2,1)S(1)}, u32[]{:S(2)}, u32[]{:S(2)}) collective-permute-start(bf16[8,6144]{1,0:T(8,128)(2,1)S(1)} %shard_map.126), channel_id=1, source_target_pairs={{4,0},{8,4},{12,8},{14,12},{10,14},{6,10},{2,6},{0,2},{5,1},{9,5},... | collective-permute-start | bytes 294920 | tf_op jit(solution)/shard_map/ppermute | solution.py:371
  42.6 5.5 %collective-permute-start.19 = (bf16[8,6144]{1,0:T(8,128)(2,1)S(1)}, bf16[8,6144]{1,0:T(8,128)(2,1)S(1)}, u32[]{:S(2)}, u32[]{:S(2)}) collective-permute-start(bf16[8,6144]{1,0:T(8,128)(2,1)S(1)} %get-tuple-element.27), channel_id=1, source_target_pairs={{4,0},{8,4},{12,8},{14,12},{10,14},{6,10},{2,6},{0,2},{5,1},{9,5},... | collective-permute-start | bytes 294920 | tf_op jit(solution)/shard_map/ppermute | solution.py:371
  44.2 5.6 %collective-permute-start.16 = (bf16[8,6144]{1,0:T(8,128)(2,1)S(1)}, bf16[8,6144]{1,0:T(8,128)(2,1)S(1)}, u32[]{:S(2)}, u32[]{:S(2)}) collective-permute-start(bf16[8,6144]{1,0:T(8,128)(2,1)S(1)} %shard_map.121), channel_id=1, source_target_pairs={{0,4},{4,8},{8,12},{12,14},{14,10},{10,6},{6,2},{2,0},{1,5},{5,9},... | collective-permute-start | bytes 294920 | tf_op jit(solution)/shard_map/ppermute | solution.py:368
  44.8 6.3 %collective-permute-start.27 = (bf16[8,6144]{1,0:T(8,128)(2,1)S(1)}, bf16[8,6144]{1,0:T(8,128)(2,1)S(1)}, u32[]{:S(2)}, u32[]{:S(2)}) collective-permute-start(bf16[8,6144]{1,0:T(8,128)(2,1)S(1)} %shard_map.129), channel_id=1, source_target_pairs={{0,4},{4,8},{8,12},{12,14},{14,10},{10,6},{6,2},{2,0},{1,5},{5,9},... | collective-permute-start | bytes 294920 | tf_op jit(solution)/shard_map/ppermute | solution.py:368
  46.6 5.1 %collective-permute-start.24 = (bf16[8,6144]{1,0:T(8,128)(2,1)S(1)}, bf16[8,6144]{1,0:T(8,128)(2,1)S(1)}, u32[]{:S(2)}, u32[]{:S(2)}) collective-permute-start(bf16[8,6144]{1,0:T(8,128)(2,1)S(1)} %shard_map.127), channel_id=1, source_target_pairs={{4,0},{8,4},{12,8},{14,12},{10,14},{6,10},{2,6},{0,2},{5,1},{9,5},... | collective-permute-start | bytes 294920 | tf_op jit(solution)/shard_map/ppermute | solution.py:371
  48.2 5.1 %collective-permute-start.20 = (bf16[8,6144]{1,0:T(8,128)(2,1)S(1)}, bf16[8,6144]{1,0:T(8,128)(2,1)S(1)}, u32[]{:S(2)}, u32[]{:S(2)}) collective-permute-start(bf16[8,6144]{1,0:T(8,128)(2,1)S(1)} %shard_map.124), channel_id=1, source_target_pairs={{4,0},{8,4},{12,8},{14,12},{10,14},{6,10},{2,6},{0,2},{5,1},{9,5},... | collective-permute-start | bytes 294920 | tf_op jit(solution)/shard_map/ppermute | solution.py:371
  49.9 5.2 %collective-permute-start.17 = (bf16[8,6144]{1,0:T(8,128)(2,1)S(1)}, bf16[8,6144]{1,0:T(8,128)(2,1)S(1)}, u32[]{:S(2)}, u32[]{:S(2)}) collective-permute-start(bf16[8,6144]{1,0:T(8,128)(2,1)S(1)} %shard_map.122), channel_id=1, source_target_pairs={{0,4},{4,8},{8,12},{12,14},{14,10},{10,6},{6,2},{2,0},{1,5},{5,9},... | collective-permute-start | bytes 294920 | tf_op jit(solution)/shard_map/ppermute | solution.py:368
  51.1 4.7 %collective-permute-start.28 = (bf16[8,6144]{1,0:T(8,128)(2,1)S(1)}, bf16[8,6144]{1,0:T(8,128)(2,1)S(1)}, u32[]{:S(2)}, u32[]{:S(2)}) collective-permute-start(bf16[8,6144]{1,0:T(8,128)(2,1)S(1)} %shard_map.130), channel_id=1, source_target_pairs={{0,4},{4,8},{8,12},{12,14},{14,10},{10,6},{6,2},{2,0},{1,5},{5,9},... | collective-permute-start | bytes 294920 | tf_op jit(solution)/shard_map/ppermute | solution.py:368
  51.7 4.7 %collective-permute-start.25 = (bf16[8,6144]{1,0:T(8,128)(2,1)S(1)}, bf16[8,6144]{1,0:T(8,128)(2,1)S(1)}, u32[]{:S(2)}, u32[]{:S(2)}) collective-permute-start(bf16[8,6144]{1,0:T(8,128)(2,1)S(1)} %shard_map.128), channel_id=1, source_target_pairs={{4,0},{8,4},{12,8},{14,12},{10,14},{6,10},{2,6},{0,2},{5,1},{9,5},... | collective-permute-start | bytes 294920 | tf_op jit(solution)/shard_map/ppermute | solution.py:371
  53.3 4.7 %collective-permute-start.21 = (bf16[8,6144]{1,0:T(8,128)(2,1)S(1)}, bf16[8,6144]{1,0:T(8,128)(2,1)S(1)}, u32[]{:S(2)}, u32[]{:S(2)}) collective-permute-start(bf16[8,6144]{1,0:T(8,128)(2,1)S(1)} %shard_map.125), channel_id=1, source_target_pairs={{4,0},{8,4},{12,8},{14,12},{10,14},{6,10},{2,6},{0,2},{5,1},{9,5},... | collective-permute-start | bytes 294920 | tf_op jit(solution)/shard_map/ppermute | solution.py:371
  55.1 4.7 %collective-permute-start.18 = (bf16[8,6144]{1,0:T(8,128)(2,1)S(1)}, bf16[8,6144]{1,0:T(8,128)(2,1)S(1)}, u32[]{:S(2)}, u32[]{:S(2)}) collective-permute-start(bf16[8,6144]{1,0:T(8,128)(2,1)S(1)} %shard_map.123), channel_id=1, source_target_pairs={{0,4},{4,8},{8,12},{12,14},{14,10},{10,6},{6,2},{2,0},{1,5},{5,9},... | collective-permute-start | bytes 294920 | tf_op jit(solution)/shard_map/ppermute | solution.py:368
  56.4 3.3 %collective-permute-start.29 = (bf16[8,6144]{1,0:T(8,128)(2,1)S(1)}, bf16[8,6144]{1,0:T(8,128)(2,1)S(1)}, u32[]{:S(2)}, u32[]{:S(2)}) collective-permute-start(bf16[8,6144]{1,0:T(8,128)(2,1)S(1)} %shard_map.131), channel_id=1, source_target_pairs={{0,1},{1,0},{2,3},{3,2},{4,5},{5,4},{6,7},{7,6},{8,9},{9,8},{10,11... | collective-permute-start | bytes 294920 | tf_op jit(solution)/shard_map/ppermute | solution.py:413
  (1 other events, 2.8 us)

commit v6 on v5

--- a/solution.py
+++ b/solution.py
@@ -201,6 +201,8 @@
         powers = jnp.exp2((scores - top) * scale)
         own_power = jnp.exp2((own_score - top) * scale)
         inverse = 1.0 / (jnp.sum(powers, -1, keepdims=True) + own_power)
+        powers = powers * inverse
+        own_weight = (own_power * inverse).astype(jnp.bfloat16).astype(jnp.float32)
         wide_rows = []
         for at in range(0, group * rows, eight):
             place = at % rows // eight
@@ -214,7 +216,7 @@
         values = value_ref[:, :, lanes].reshape(rows * span, HEAD)
         mixed = jnp.dot(attention, values, preferred_element_type=jnp.float32)
         new_value = jnp.concatenate([new_value_ref[:, lanes].astype(jnp.float32)] * group, 0)
-        mixed = (mixed + own_power * new_value) * inverse
+        mixed = mixed + own_weight * new_value
         for member in range(group):
             cols = pl.ds((head * group + member) * HEAD, HEAD)
             part = hidden_ref[:, cols].astype(jnp.float32) + mixed[
@@ -402,8 +404,11 @@
     own_from_r = own_share[1 - half]
     theirs_from_l = theirs_share[half - 1]
     for step in range(half - 1, 0, -1):
-        own_from_l = add(go_right(own_from_l), own_share[step])
-        theirs_from_r = add(go_left(theirs_from_r), theirs_share[-step])
+        from_l, from_r = go_right(own_from_l), go_left(theirs_from_r)
+        if step == half - 1:
+            own_from_r, _ = lax.optimization_barrier((own_from_r, from_l))
+        own_from_l = add(from_l, own_share[step])
+        theirs_from_r = add(from_r, theirs_share[-step])
         if step > 1:
             own_from_r = add(go_left(own_from_r), own_share[1 - step])
             theirs_from_l = add(go_right(theirs_from_l), theirs_share[step - 1])

time: 60.9 us -> 60.9 us (level)
  no operation moved by 1% of the time
where the time goes in v6:
time: 60.9 us; the launch traced here: 60.7 us
  starting transfers between devices  30.4 us (50%)
  waiting for transfers between devices  15 us (25%)
  Pallas kernels  13.2 us (22%)
  matrix products  1.4 us (2%)
    ppermute x13, starting transfers between devices, go_left(): return lax.ppermute(block, 'attn', left)  22.7 us
    ppermute x13, waiting for transfers between devices, go_left(): return lax.ppermute(block, 'attn', left)  9.42 us
    pallas_call x1, Pallas kernels, body(): pl.pallas_call(front_kernel, out_shape=(jax.ShapeDtypeStruct((row_count,...  5.5 us
    ppermute x14, starting transfers between devices, go_right(): return lax.ppermute(block, 'attn', right)  4.78 us
    ppermute x14, waiting for transfers between devices, go_right(): return lax.ppermute(block, 'attn', right)  4.33 us
    pallas_call x1, Pallas kernels, load(): pl.pallas_call(load_kernel, out_shape=pltpu.VMEM(weights.shape, weights.d...  3.69 us
    ppermute x1, starting transfers between devices, body(): theirs_l.append(lax.ppermute(theirs_l[half - 2], 'attn', left_two))  2.79 us
    pallas_call x1, Pallas kernels, activate(): pl.pallas_call(experts_kernel, out_shape=jax.ShapeDtypeStruct((count, hid...  2.76 us
  transfers between devices with their start and end apart: 30, of which 13 were waited for; matrix products, arithmetic and copies ran while one was open for 0% of the time, Pallas kernels for 7%

profile of v6, /device:TPU:0, one launch (start us, length us, event | category | flops | bytes accessed | tf_op | source)
XLA Modules:
  0.0 60.7 jit_solution(3530367113292769211)
XLA Ops:
  0.0 5.5 %shard_map.118 = (f32[16,6144]{1,0:T(8,128)S(1)}, bf16[8,6144]{1,0:T(8,128)(2,1)S(1)}, bf16[8,6144]{1,0:T(8,128)(2,1)S(1)}, f32[16,16]{1,0:T(8,128)S(1)}, f32[16...) custom-call(s32[1]{0:T(128)} %bitcast.here_ref, bf16[16,6144]{1,0:T(8,128)(2,1)} %hidden_hbm.1, bf16[16,6144]{1,0:T(8,128)(2,1)} %query_hbm.1, ...), custom_call_target="tpu_custom_call" | custom-call | flops 1000000000 | bytes 40000000 | tf_op jit(solution)/shard_map/pallas_call | solution.py:337
  5.5 3.0 %collective-permute-start.2 = (bf16[8,6144]{1,0:T(8,128)(2,1)S(1)}, bf16[8,6144]{1,0:T(8,128)(2,1)S(1)}, u32[]{:S(2)}, u32[]{:S(2)}) collective-permute-start(bf16[8,6144]{1,0:T(8,128)(2,1)S(1)} %get-tuple-element.15), channel_id=1, source_target_pairs={{4,0},{8,4},{12,8},{14,12},{10,14},{6,10},{2,6},{0,2},{5,1},{9,5},... | collective-permute-start | bytes 294920 | tf_op jit(solution)/shard_map/ppermute | solution.py:373
  8.7 1.3 %collective-permute-done = bf16[8,6144]{1,0:T(8,128)(2,1)S(1)} collective-permute-done((bf16[8,6144]{1,0:T(8,128)(2,1)S(1)}, bf16[8,6144]{1,0:T(8,128)(2,1)S(1)}, u32[]{:S(2)}, u32[]{:S(2)}) %collective-permute-start) | collective-permute-done | bytes 98336 | tf_op jit(solution)/shard_map/ppermute | solution.py:376
  10.0 1.9 %collective-permute-start.4 = (bf16[8,6144]{1,0:T(8,128)(2,1)S(1)}, bf16[8,6144]{1,0:T(8,128)(2,1)S(1)}, u32[]{:S(2)}, u32[]{:S(2)}) collective-permute-start(bf16[8,6144]{1,0:T(8,128)(2,1)S(1)} %collective-permute-done), channel_id=1, source_target_pairs={{4,0},{8,4},{12,8},{14,12},{10,14},{6,10},{2,6},{0,2},{5,1},{9,5},... | collective-permute-start | bytes 294920 | tf_op jit(solution)/shard_map/ppermute | solution.py:373
  12.0 1.9 %collective-permute-start.6 = (bf16[8,6144]{1,0:T(8,128)(2,1)S(1)}, bf16[8,6144]{1,0:T(8,128)(2,1)S(1)}, u32[]{:S(2)}, u32[]{:S(2)}) collective-permute-start(bf16[8,6144]{1,0:T(8,128)(2,1)S(1)} %collective-permute-done.2), channel_id=1, source_target_pairs={{4,0},{8,4},{12,8},{14,12},{10,14},{6,10},{2,6},{0,2},{5,1},{9,5},... | collective-permute-start | bytes 294920 | tf_op jit(solution)/shard_map/ppermute | solution.py:373
  14.0 1.5 %collective-permute-done.4 = bf16[8,6144]{1,0:T(8,128)(2,1)S(1)} collective-permute-done((bf16[8,6144]{1,0:T(8,128)(2,1)S(1)}, bf16[8,6144]{1,0:T(8,128)(2,1)S(1)}, u32[]{:S(2)}, u32[]{:S(2)}) %collective-permute-start.4) | collective-permute-done | bytes 98336 | tf_op jit(solution)/shard_map/ppermute | solution.py:373
  15.6 1.8 %collective-permute-start.8 = (bf16[8,6144]{1,0:T(8,128)(2,1)S(1)}, bf16[8,6144]{1,0:T(8,128)(2,1)S(1)}, u32[]{:S(2)}, u32[]{:S(2)}) collective-permute-start(bf16[8,6144]{1,0:T(8,128)(2,1)S(1)} %collective-permute-done.4), channel_id=1, source_target_pairs={{4,0},{8,4},{12,8},{14,12},{10,14},{6,10},{2,6},{0,2},{5,1},{9,5},... | collective-permute-start | bytes 294920 | tf_op jit(solution)/shard_map/ppermute | solution.py:373
  17.6 1.8 %collective-permute-start.10 = (bf16[8,6144]{1,0:T(8,128)(2,1)S(1)}, bf16[8,6144]{1,0:T(8,128)(2,1)S(1)}, u32[]{:S(2)}, u32[]{:S(2)}) collective-permute-start(bf16[8,6144]{1,0:T(8,128)(2,1)S(1)} %collective-permute-done.6), channel_id=1, source_target_pairs={{4,0},{8,4},{12,8},{14,12},{10,14},{6,10},{2,6},{0,2},{5,1},{9,5},... | collective-permute-start | bytes 294920 | tf_op jit(solution)/shard_map/ppermute | solution.py:373
  19.7 1.4 %collective-permute-done.8 = bf16[8,6144]{1,0:T(8,128)(2,1)S(1)} collective-permute-done((bf16[8,6144]{1,0:T(8,128)(2,1)S(1)}, bf16[8,6144]{1,0:T(8,128)(2,1)S(1)}, u32[]{:S(2)}, u32[]{:S(2)}) %collective-permute-start.8) | collective-permute-done | bytes 98336 | tf_op jit(solution)/shard_map/ppermute | solution.py:373
  21.1 2.8 %collective-permute-start.14 = (bf16[8,6144]{1,0:T(8,128)(2,1)S(1)}, bf16[8,6144]{1,0:T(8,128)(2,1)S(1)}, u32[]{:S(2)}, u32[]{:S(2)}) collective-permute-start(bf16[8,6144]{1,0:T(8,128)(2,1)S(1)} %collective-permute-done.8), channel_id=1, source_target_pairs={{8,0},{12,4},{14,8},{10,12},{6,14},{2,10},{0,6},{4,2},{9,1},{13,5}... | collective-permute-start | bytes 294920 | tf_op jit(solution)/shard_map/ppermute | solution.py:384
  23.8 1.6 %collective-permute-start.12 = (bf16[8,6144]{1,0:T(8,128)(2,1)S(1)}, bf16[8,6144]{1,0:T(8,128)(2,1)S(1)}, u32[]{:S(2)}, u32[]{:S(2)}) collective-permute-start(bf16[8,6144]{1,0:T(8,128)(2,1)S(1)} %collective-permute-done.8), channel_id=1, source_target_pairs={{4,0},{8,4},{12,8},{14,12},{10,14},{6,10},{2,6},{0,2},{5,1},{9,5},... | collective-permute-start | bytes 294920 | tf_op jit(solution)/shard_map/ppermute | solution.py:373
  25.9 0.5 collective-permute-start.13
  26.4 3.7 %shard_map.119.up_ref = bf16[6144,768]{1,0:T(8,128)(2,1)S(1)} custom-call(bf16[8,6144]{1,0:T(8,128)(2,1)S(1)} %collective-permute-done.7.after_ref, bf16[6144,768]{1,0:T(8,128)(2,1)} %bitcast.15), custom_call_target="tpu_custom_call" | custom-call | bytes 9437184 | tf_op jit(solution)/shard_map/pallas_call | solution.py:30
  30.2 0.9 %collective-permute-done.13 = bf16[8,6144]{1,0:T(8,128)(2,1)S(1)} collective-permute-done((bf16[8,6144]{1,0:T(8,128)(2,1)S(1)}, bf16[8,6144]{1,0:T(8,128)(2,1)S(1)}, u32[]{:S(2)}, u32[]{:S(2)}) %collective-permute-start.13) | collective-permute-done | bytes 98336 | tf_op jit(solution)/shard_map/ppermute | solution.py:370
  31.2 2.8 %shard_map.120 = bf16[128,768]{1,0:T(8,128)(2,1)S(1)} custom-call(bf16[128,6144]{1,0:T(8,128)(2,1)S(1)} %constant_dynamic-update-slice_fusion.rows_ref, bf16[6144,768]{1,0:T(8,128)(2,1)S(1)} %get-tuple-element.17.gate_ref, bf16[6144,768]{1,0:T(8,128)(2,1)S(1)} %shard_map.119.up_ref), custom_call_target="tpu_custom_call" | custom-call | flops 2415919104 | bytes 18874368 | tf_op jit(solution)/shard_map/pallas_call | solution.py:61
  34.0 1.4 %fusion.2 = bf16[128,6144]{1,0:T(8,128)(2,1)S(1)} fusion(bf16[128,768]{1,0:T(8,128)(2,1)S(1)} %shard_map.120, bf16[1,768,6144]{2,1,0:T(8,128)(2,1)S(1)} %bitcast.13), kind=kOutput, calls=%fused_computation.2 | convolution fusion | flops 1208745984 | bytes 11206656 | tf_op jit(solution)/shard_map/dot_general | solution.py:393
  35.6 1.8 %collective-permute-start.22 = (bf16[8,6144]{1,0:T(8,128)(2,1)S(1)}, bf16[8,6144]{1,0:T(8,128)(2,1)S(1)}, u32[]{:S(2)}, u32[]{:S(2)}) collective-permute-start(bf16[8,6144]{1,0:T(8,128)(2,1)S(1)} %get-tuple-element.25), channel_id=1, source_target_pairs={{4,0},{8,4},{12,8},{14,12},{10,14},{6,10},{2,6},{0,2},{5,1},{9,5},... | collective-permute-start | bytes 294920 | tf_op jit(solution)/shard_map/ppermute | solution.py:373
  37.7 0.5 collective-permute-start.26
  38.1 3.1 %collective-permute-done.22.refs_0_ = bf16[8,6144]{1,0:T(8,128)(2,1)S(1)} collective-permute-done((bf16[8,6144]{1,0:T(8,128)(2,1)S(1)}, bf16[8,6144]{1,0:T(8,128)(2,1)S(1)}, u32[]{:S(2)}, u32[]{:S(2)}) %collective-permute-start.22) | collective-permute-done | bytes 98336 | tf_op jit(solution)/shard_map/ppermute | solution.py:373
  41.3 1.1 %collective-permute-start.23 = (bf16[8,6144]{1,0:T(8,128)(2,1)S(1)}, bf16[8,6144]{1,0:T(8,128)(2,1)S(1)}, u32[]{:S(2)}, u32[]{:S(2)}) collective-permute-start(bf16[8,6144]{1,0:T(8,128)(2,1)S(1)} %shard_map.126), channel_id=1, source_target_pairs={{4,0},{8,4},{12,8},{14,12},{10,14},{6,10},{2,6},{0,2},{5,1},{9,5},... | collective-permute-start | bytes 294920 | tf_op jit(solution)/shard_map/ppermute | solution.py:373
  42.4 1.8 %collective-permute-start.19 = (bf16[8,6144]{1,0:T(8,128)(2,1)S(1)}, bf16[8,6144]{1,0:T(8,128)(2,1)S(1)}, u32[]{:S(2)}, u32[]{:S(2)}) collective-permute-start(bf16[8,6144]{1,0:T(8,128)(2,1)S(1)} %get-tuple-element.18), channel_id=1, source_target_pairs={{4,0},{8,4},{12,8},{14,12},{10,14},{6,10},{2,6},{0,2},{5,1},{9,5},... | collective-permute-start | bytes 294920 | tf_op jit(solution)/shard_map/ppermute | solution.py:373
  44.5 1.0 %collective-permute-start.27 = (bf16[8,6144]{1,0:T(8,128)(2,1)S(1)}, bf16[8,6144]{1,0:T(8,128)(2,1)S(1)}, u32[]{:S(2)}, u32[]{:S(2)}) collective-permute-start(bf16[8,6144]{1,0:T(8,128)(2,1)S(1)} %shard_map.129), channel_id=1, source_target_pairs={{0,4},{4,8},{8,12},{12,14},{14,10},{10,6},{6,2},{2,0},{1,5},{5,9},... | collective-permute-start | bytes 294920 | tf_op jit(solution)/shard_map/ppermute | solution.py:370
  45.6 1.0 %collective-permute-done.23.refs_0_ = bf16[8,6144]{1,0:T(8,128)(2,1)S(1)} collective-permute-done((bf16[8,6144]{1,0:T(8,128)(2,1)S(1)}, bf16[8,6144]{1,0:T(8,128)(2,1)S(1)}, u32[]{:S(2)}, u32[]{:S(2)}) %collective-permute-start.23) | collective-permute-done | bytes 98336 | tf_op jit(solution)/shard_map/ppermute | solution.py:373
  46.6 1.5 %collective-permute-start.24 = (bf16[8,6144]{1,0:T(8,128)(2,1)S(1)}, bf16[8,6144]{1,0:T(8,128)(2,1)S(1)}, u32[]{:S(2)}, u32[]{:S(2)}) collective-permute-start(bf16[8,6144]{1,0:T(8,128)(2,1)S(1)} %shard_map.127), channel_id=1, source_target_pairs={{4,0},{8,4},{12,8},{14,12},{10,14},{6,10},{2,6},{0,2},{5,1},{9,5},... | collective-permute-start | bytes 294920 | tf_op jit(solution)/shard_map/ppermute | solution.py:373
  48.1 1.3 %collective-permute-start.20 = (bf16[8,6144]{1,0:T(8,128)(2,1)S(1)}, bf16[8,6144]{1,0:T(8,128)(2,1)S(1)}, u32[]{:S(2)}, u32[]{:S(2)}) collective-permute-start(bf16[8,6144]{1,0:T(8,128)(2,1)S(1)} %shard_map.124), channel_id=1, source_target_pairs={{4,0},{8,4},{12,8},{14,12},{10,14},{6,10},{2,6},{0,2},{5,1},{9,5},... | collective-permute-start | bytes 294920 | tf_op jit(solution)/shard_map/ppermute | solution.py:373
  50.2 0.9 %collective-permute-done.27.refs_0_ = bf16[8,6144]{1,0:T(8,128)(2,1)S(1)} collective-permute-done((bf16[8,6144]{1,0:T(8,128)(2,1)S(1)}, bf16[8,6144]{1,0:T(8,128)(2,1)S(1)}, u32[]{:S(2)}, u32[]{:S(2)}) %collective-permute-start.27) | collective-permute-done | bytes 98336 | tf_op jit(solution)/shard_map/ppermute | solution.py:370
  51.7 1.6 %collective-permute-start.25 = (bf16[8,6144]{1,0:T(8,128)(2,1)S(1)}, bf16[8,6144]{1,0:T(8,128)(2,1)S(1)}, u32[]{:S(2)}, u32[]{:S(2)}) collective-permute-start(bf16[8,6144]{1,0:T(8,128)(2,1)S(1)} %shard_map.128), channel_id=1, source_target_pairs={{4,0},{8,4},{12,8},{14,12},{10,14},{6,10},{2,6},{0,2},{5,1},{9,5},... | collective-permute-start | bytes 294920 | tf_op jit(solution)/shard_map/ppermute | solution.py:373
  53.3 1.7 %collective-permute-start.21 = (bf16[8,6144]{1,0:T(8,128)(2,1)S(1)}, bf16[8,6144]{1,0:T(8,128)(2,1)S(1)}, u32[]{:S(2)}, u32[]{:S(2)}) collective-permute-start(bf16[8,6144]{1,0:T(8,128)(2,1)S(1)} %shard_map.125), channel_id=1, source_target_pairs={{4,0},{8,4},{12,8},{14,12},{10,14},{6,10},{2,6},{0,2},{5,1},{9,5},... | collective-permute-start | bytes 294920 | tf_op jit(solution)/shard_map/ppermute | solution.py:373
  55.8 0.6 collective-permute-done.25.refs_1_
  56.5 1.5 %collective-permute-done.21.third_ref = bf16[8,6144]{1,0:T(8,128)(2,1)S(1)} collective-permute-done((bf16[8,6144]{1,0:T(8,128)(2,1)S(1)}, bf16[8,6144]{1,0:T(8,128)(2,1)S(1)}, u32[]{:S(2)}, u32[]{:S(2)}) %collective-permute-start.21) | collective-permute-done | bytes 98336 | tf_op jit(solution)/shard_map/ppermute | solution.py:373
  58.0 1.7 %collective-permute-done.18.second_ref = bf16[8,6144]{1,0:T(8,128)(2,1)S(1)} collective-permute-done((bf16[8,6144]{1,0:T(8,128)(2,1)S(1)}, bf16[8,6144]{1,0:T(8,128)(2,1)S(1)}, u32[]{:S(2)}, u32[]{:S(2)}) %collective-permute-start.18) | collective-permute-done | bytes 98336 | tf_op jit(solution)/shard_map/ppermute | solution.py:370
  59.7 1.0 %shard_map.132 = f32[16,6144]{1,0:T(8,128)} custom-call(f32[16,6144]{1,0:T(8,128)S(1)} %get-tuple-element.12.residual_ref, f32[16,16]{1,0:T(8,128)S(1)} %get-tuple-element.13.slots_ref, f32[16,2]{1,0:T(8,128)S(1)} %get-tuple-element.14.weights_ref, bf16[8,6144]{1,0:T(8,128)(2,1)S(1)} %get-tuple-element.34.first_ref, ...), custom_call_target="tpu_custom_call" | custom-call | tf_op jit(solution)/shard_map/pallas_call | solution.py:419
  (68 shorter events, 4.7 us)
Async XLA Ops:
  5.5 6.5 %collective-permute-start.2 = (bf16[8,6144]{1,0:T(8,128)(2,1)S(1)}, bf16[8,6144]{1,0:T(8,128)(2,1)S(1)}, u32[]{:S(2)}, u32[]{:S(2)}) collective-permute-start(bf16[8,6144]{1,0:T(8,128)(2,1)S(1)} %get-tuple-element.15), channel_id=1, source_target_pairs={{4,0},{8,4},{12,8},{14,12},{10,14},{6,10},{2,6},{0,2},{5,1},{9,5},... | collective-permute-start | bytes 294920 | tf_op jit(solution)/shard_map/ppermute | solution.py:373
  8.5 5.4 %collective-permute-start.1 = (bf16[8,6144]{1,0:T(8,128)(2,1)S(1)}, bf16[8,6144]{1,0:T(8,128)(2,1)S(1)}, u32[]{:S(2)}, u32[]{:S(2)}) collective-permute-start(bf16[8,6144]{1,0:T(8,128)(2,1)S(1)} %get-tuple-element.15), channel_id=1, source_target_pairs={{0,4},{4,8},{8,12},{12,14},{14,10},{10,6},{6,2},{2,0},{1,5},{5,9},... | collective-permute-start | bytes 294920 | tf_op jit(solution)/shard_map/ppermute | solution.py:370
  8.6 1.3 %collective-permute-start = (bf16[8,6144]{1,0:T(8,128)(2,1)S(1)}, bf16[8,6144]{1,0:T(8,128)(2,1)S(1)}, u32[]{:S(2)}, u32[]{:S(2)}) collective-permute-start(bf16[8,6144]{1,0:T(8,128)(2,1)S(1)} %get-tuple-element.16), channel_id=1, source_target_pairs={{0,1},{1,0},{2,3},{3,2},{4,5},{5,4},{6,7},{7,6},{8,9},{9,8},{10,11... | collective-permute-start | bytes 294920 | tf_op jit(solution)/shard_map/ppermute | solution.py:376
  10.0 5.6 %collective-permute-start.4 = (bf16[8,6144]{1,0:T(8,128)(2,1)S(1)}, bf16[8,6144]{1,0:T(8,128)(2,1)S(1)}, u32[]{:S(2)}, u32[]{:S(2)}) collective-permute-start(bf16[8,6144]{1,0:T(8,128)(2,1)S(1)} %collective-permute-done), channel_id=1, source_target_pairs={{4,0},{8,4},{12,8},{14,12},{10,14},{6,10},{2,6},{0,2},{5,1},{9,5},... | collective-permute-start | bytes 294920 | tf_op jit(solution)/shard_map/ppermute | solution.py:373
  11.9 5.5 %collective-permute-start.3 = (bf16[8,6144]{1,0:T(8,128)(2,1)S(1)}, bf16[8,6144]{1,0:T(8,128)(2,1)S(1)}, u32[]{:S(2)}, u32[]{:S(2)}) collective-permute-start(bf16[8,6144]{1,0:T(8,128)(2,1)S(1)} %collective-permute-done), channel_id=1, source_target_pairs={{0,4},{4,8},{8,12},{12,14},{14,10},{10,6},{6,2},{2,0},{1,5},{5,9},... | collective-permute-start | bytes 294920 | tf_op jit(solution)/shard_map/ppermute | solution.py:370
  12.0 5.6 %collective-permute-start.6 = (bf16[8,6144]{1,0:T(8,128)(2,1)S(1)}, bf16[8,6144]{1,0:T(8,128)(2,1)S(1)}, u32[]{:S(2)}, u32[]{:S(2)}) collective-permute-start(bf16[8,6144]{1,0:T(8,128)(2,1)S(1)} %collective-permute-done.2), channel_id=1, source_target_pairs={{4,0},{8,4},{12,8},{14,12},{10,14},{6,10},{2,6},{0,2},{5,1},{9,5},... | collective-permute-start | bytes 294920 | tf_op jit(solution)/shard_map/ppermute | solution.py:373
  13.9 5.5 %collective-permute-start.5 = (bf16[8,6144]{1,0:T(8,128)(2,1)S(1)}, bf16[8,6144]{1,0:T(8,128)(2,1)S(1)}, u32[]{:S(2)}, u32[]{:S(2)}) collective-permute-start(bf16[8,6144]{1,0:T(8,128)(2,1)S(1)} %collective-permute-done.1), channel_id=1, source_target_pairs={{0,4},{4,8},{8,12},{12,14},{14,10},{10,6},{6,2},{2,0},{1,5},{5,9},... | collective-permute-start | bytes 294920 | tf_op jit(solution)/shard_map/ppermute | solution.py:370
  15.6 5.5 %collective-permute-start.8 = (bf16[8,6144]{1,0:T(8,128)(2,1)S(1)}, bf16[8,6144]{1,0:T(8,128)(2,1)S(1)}, u32[]{:S(2)}, u32[]{:S(2)}) collective-permute-start(bf16[8,6144]{1,0:T(8,128)(2,1)S(1)} %collective-permute-done.4), channel_id=1, source_target_pairs={{4,0},{8,4},{12,8},{14,12},{10,14},{6,10},{2,6},{0,2},{5,1},{9,5},... | collective-permute-start | bytes 294920 | tf_op jit(solution)/shard_map/ppermute | solution.py:373
  17.4 8.0 %collective-permute-start.7 = (bf16[8,6144]{1,0:T(8,128)(2,1)S(1)}, bf16[8,6144]{1,0:T(8,128)(2,1)S(1)}, u32[]{:S(2)}, u32[]{:S(2)}) collective-permute-start(bf16[8,6144]{1,0:T(8,128)(2,1)S(1)} %collective-permute-done.3), channel_id=1, source_target_pairs={{0,4},{4,8},{8,12},{12,14},{14,10},{10,6},{6,2},{2,0},{1,5},{5,9},... | collective-permute-start | bytes 294920 | tf_op jit(solution)/shard_map/ppermute | solution.py:370
  17.6 8.8 %collective-permute-start.10 = (bf16[8,6144]{1,0:T(8,128)(2,1)S(1)}, bf16[8,6144]{1,0:T(8,128)(2,1)S(1)}, u32[]{:S(2)}, u32[]{:S(2)}) collective-permute-start(bf16[8,6144]{1,0:T(8,128)(2,1)S(1)} %collective-permute-done.6), channel_id=1, source_target_pairs={{4,0},{8,4},{12,8},{14,12},{10,14},{6,10},{2,6},{0,2},{5,1},{9,5},... | collective-permute-start | bytes 294920 | tf_op jit(solution)/shard_map/ppermute | solution.py:373
  19.4 6.5 %collective-permute-start.9 = (bf16[8,6144]{1,0:T(8,128)(2,1)S(1)}, bf16[8,6144]{1,0:T(8,128)(2,1)S(1)}, u32[]{:S(2)}, u32[]{:S(2)}) collective-permute-start(bf16[8,6144]{1,0:T(8,128)(2,1)S(1)} %collective-permute-done.5), channel_id=1, source_target_pairs={{0,4},{4,8},{8,12},{12,14},{14,10},{10,6},{6,2},{2,0},{1,5},{5,9},... | collective-permute-start | bytes 294920 | tf_op jit(solution)/shard_map/ppermute | solution.py:370
  21.1 10.1 %collective-permute-start.14 = (bf16[8,6144]{1,0:T(8,128)(2,1)S(1)}, bf16[8,6144]{1,0:T(8,128)(2,1)S(1)}, u32[]{:S(2)}, u32[]{:S(2)}) collective-permute-start(bf16[8,6144]{1,0:T(8,128)(2,1)S(1)} %collective-permute-done.8), channel_id=1, source_target_pairs={{8,0},{12,4},{14,8},{10,12},{6,14},{2,10},{0,6},{4,2},{9,1},{13,5}... | collective-permute-start | bytes 294920 | tf_op jit(solution)/shard_map/ppermute | solution.py:384
  23.8 6.3 %collective-permute-start.12 = (bf16[8,6144]{1,0:T(8,128)(2,1)S(1)}, bf16[8,6144]{1,0:T(8,128)(2,1)S(1)}, u32[]{:S(2)}, u32[]{:S(2)}) collective-permute-start(bf16[8,6144]{1,0:T(8,128)(2,1)S(1)} %collective-permute-done.8), channel_id=1, source_target_pairs={{4,0},{8,4},{12,8},{14,12},{10,14},{6,10},{2,6},{0,2},{5,1},{9,5},... | collective-permute-start | bytes 294920 | tf_op jit(solution)/shard_map/ppermute | solution.py:373
  25.4 4.7 %collective-permute-start.11 = (bf16[8,6144]{1,0:T(8,128)(2,1)S(1)}, bf16[8,6144]{1,0:T(8,128)(2,1)S(1)}, u32[]{:S(2)}, u32[]{:S(2)}) collective-permute-start(bf16[8,6144]{1,0:T(8,128)(2,1)S(1)} %collective-permute-done.7.after_ref), channel_id=1, source_target_pairs={{0,4},{4,8},{8,12},{12,14},{14,10},{10,6},{6,2},{2,0},{1,5},{5,9},... | collective-permute-start | bytes 294920 | tf_op jit(solution)/shard_map/ppermute | solution.py:370
  25.9 5.2 %collective-permute-start.13 = (bf16[8,6144]{1,0:T(8,128)(2,1)S(1)}, bf16[8,6144]{1,0:T(8,128)(2,1)S(1)}, u32[]{:S(2)}, u32[]{:S(2)}) collective-permute-start(bf16[8,6144]{1,0:T(8,128)(2,1)S(1)} %collective-permute-done.9), channel_id=1, source_target_pairs={{0,4},{4,8},{8,12},{12,14},{14,10},{10,6},{6,2},{2,0},{1,5},{5,9},... | collective-permute-start | bytes 294920 | tf_op jit(solution)/shard_map/ppermute | solution.py:370
  30.1 3.8 %slice-start = ((s8[9437184]{0:T(1024)(128)(4,1)}), s8[4194304]{0:T(1024)(128)(4,1)S(1)}, s32[]{:S(2)}) async-start(s8[9437184]{0:T(1024)(128)(4,1)} %bitcast.12), calls=%async_computation | async-start | bytes 8388608
  31.2 2.9 %slice-start.2 = ((s8[9437184]{0:T(1024)(128)(4,1)}), s8[1048576]{0:T(1024)(128)(4,1)S(1)}, s32[]{:S(2)}) async-start(s8[9437184]{0:T(1024)(128)(4,1)} %bitcast.12), calls=%async_computation.2 | async-start | bytes 2097152
  35.6 5.7 %collective-permute-start.22 = (bf16[8,6144]{1,0:T(8,128)(2,1)S(1)}, bf16[8,6144]{1,0:T(8,128)(2,1)S(1)}, u32[]{:S(2)}, u32[]{:S(2)}) collective-permute-start(bf16[8,6144]{1,0:T(8,128)(2,1)S(1)} %get-tuple-element.25), channel_id=1, source_target_pairs={{4,0},{8,4},{12,8},{14,12},{10,14},{6,10},{2,6},{0,2},{5,1},{9,5},... | collective-permute-start | bytes 294920 | tf_op jit(solution)/shard_map/ppermute | solution.py:373
  37.4 5.0 %collective-permute-start.15 = (bf16[8,6144]{1,0:T(8,128)(2,1)S(1)}, bf16[8,6144]{1,0:T(8,128)(2,1)S(1)}, u32[]{:S(2)}, u32[]{:S(2)}) collective-permute-start(bf16[8,6144]{1,0:T(8,128)(2,1)S(1)} %get-tuple-element.33), channel_id=1, source_target_pairs={{0,4},{4,8},{8,12},{12,14},{14,10},{10,6},{6,2},{2,0},{1,5},{5,9},... | collective-permute-start | bytes 294920 | tf_op jit(solution)/shard_map/ppermute | solution.py:370
  37.7 6.8 %collective-permute-start.26 = (bf16[8,6144]{1,0:T(8,128)(2,1)S(1)}, bf16[8,6144]{1,0:T(8,128)(2,1)S(1)}, u32[]{:S(2)}, u32[]{:S(2)}) collective-permute-start(bf16[8,6144]{1,0:T(8,128)(2,1)S(1)} %get-tuple-element.21), channel_id=1, source_target_pairs={{0,4},{4,8},{8,12},{12,14},{14,10},{10,6},{6,2},{2,0},{1,5},{5,9},... | collective-permute-start | bytes 294920 | tf_op jit(solution)/shard_map/ppermute | solution.py:370
  41.3 5.3 %collective-permute-start.23 = (bf16[8,6144]{1,0:T(8,128)(2,1)S(1)}, bf16[8,6144]{1,0:T(8,128)(2,1)S(1)}, u32[]{:S(2)}, u32[]{:S(2)}) collective-permute-start(bf16[8,6144]{1,0:T(8,128)(2,1)S(1)} %shard_map.126), channel_id=1, source_target_pairs={{4,0},{8,4},{12,8},{14,12},{10,14},{6,10},{2,6},{0,2},{5,1},{9,5},... | collective-permute-start | bytes 294920 | tf_op jit(solution)/shard_map/ppermute | solution.py:373
  42.4 5.7 %collective-permute-start.19 = (bf16[8,6144]{1,0:T(8,128)(2,1)S(1)}, bf16[8,6144]{1,0:T(8,128)(2,1)S(1)}, u32[]{:S(2)}, u32[]{:S(2)}) collective-permute-start(bf16[8,6144]{1,0:T(8,128)(2,1)S(1)} %get-tuple-element.18), channel_id=1, source_target_pairs={{4,0},{8,4},{12,8},{14,12},{10,14},{6,10},{2,6},{0,2},{5,1},{9,5},... | collective-permute-start | bytes 294920 | tf_op jit(solution)/shard_map/ppermute | solution.py:373
  44.2 5.6 %collective-permute-start.16 = (bf16[8,6144]{1,0:T(8,128)(2,1)S(1)}, bf16[8,6144]{1,0:T(8,128)(2,1)S(1)}, u32[]{:S(2)}, u32[]{:S(2)}) collective-permute-start(bf16[8,6144]{1,0:T(8,128)(2,1)S(1)} %shard_map.121), channel_id=1, source_target_pairs={{0,4},{4,8},{8,12},{12,14},{14,10},{10,6},{6,2},{2,0},{1,5},{5,9},... | collective-permute-start | bytes 294920 | tf_op jit(solution)/shard_map/ppermute | solution.py:370
  44.5 6.6 %collective-permute-start.27 = (bf16[8,6144]{1,0:T(8,128)(2,1)S(1)}, bf16[8,6144]{1,0:T(8,128)(2,1)S(1)}, u32[]{:S(2)}, u32[]{:S(2)}) collective-permute-start(bf16[8,6144]{1,0:T(8,128)(2,1)S(1)} %shard_map.129), channel_id=1, source_target_pairs={{0,4},{4,8},{8,12},{12,14},{14,10},{10,6},{6,2},{2,0},{1,5},{5,9},... | collective-permute-start | bytes 294920 | tf_op jit(solution)/shard_map/ppermute | solution.py:370
  46.6 5.1 %collective-permute-start.24 = (bf16[8,6144]{1,0:T(8,128)(2,1)S(1)}, bf16[8,6144]{1,0:T(8,128)(2,1)S(1)}, u32[]{:S(2)}, u32[]{:S(2)}) collective-permute-start(bf16[8,6144]{1,0:T(8,128)(2,1)S(1)} %shard_map.127), channel_id=1, source_target_pairs={{4,0},{8,4},{12,8},{14,12},{10,14},{6,10},{2,6},{0,2},{5,1},{9,5},... | collective-permute-start | bytes 294920 | tf_op jit(solution)/shard_map/ppermute | solution.py:373
  48.1 5.2 %collective-permute-start.20 = (bf16[8,6144]{1,0:T(8,128)(2,1)S(1)}, bf16[8,6144]{1,0:T(8,128)(2,1)S(1)}, u32[]{:S(2)}, u32[]{:S(2)}) collective-permute-start(bf16[8,6144]{1,0:T(8,128)(2,1)S(1)} %shard_map.124), channel_id=1, source_target_pairs={{4,0},{8,4},{12,8},{14,12},{10,14},{6,10},{2,6},{0,2},{5,1},{9,5},... | collective-permute-start | bytes 294920 | tf_op jit(solution)/shard_map/ppermute | solution.py:373
  49.8 5.2 %collective-permute-start.17 = (bf16[8,6144]{1,0:T(8,128)(2,1)S(1)}, bf16[8,6144]{1,0:T(8,128)(2,1)S(1)}, u32[]{:S(2)}, u32[]{:S(2)}) collective-permute-start(bf16[8,6144]{1,0:T(8,128)(2,1)S(1)} %shard_map.122), channel_id=1, source_target_pairs={{0,4},{4,8},{8,12},{12,14},{14,10},{10,6},{6,2},{2,0},{1,5},{5,9},... | collective-permute-start | bytes 294920 | tf_op jit(solution)/shard_map/ppermute | solution.py:370
  51.1 4.7 %collective-permute-start.28 = (bf16[8,6144]{1,0:T(8,128)(2,1)S(1)}, bf16[8,6144]{1,0:T(8,128)(2,1)S(1)}, u32[]{:S(2)}, u32[]{:S(2)}) collective-permute-start(bf16[8,6144]{1,0:T(8,128)(2,1)S(1)} %shard_map.130), channel_id=1, source_target_pairs={{0,4},{4,8},{8,12},{12,14},{14,10},{10,6},{6,2},{2,0},{1,5},{5,9},... | collective-permute-start | bytes 294920 | tf_op jit(solution)/shard_map/ppermute | solution.py:370
  51.7 4.7 %collective-permute-start.25 = (bf16[8,6144]{1,0:T(8,128)(2,1)S(1)}, bf16[8,6144]{1,0:T(8,128)(2,1)S(1)}, u32[]{:S(2)}, u32[]{:S(2)}) collective-permute-start(bf16[8,6144]{1,0:T(8,128)(2,1)S(1)} %shard_map.128), channel_id=1, source_target_pairs={{4,0},{8,4},{12,8},{14,12},{10,14},{6,10},{2,6},{0,2},{5,1},{9,5},... | collective-permute-start | bytes 294920 | tf_op jit(solution)/shard_map/ppermute | solution.py:373
  53.3 4.7 %collective-permute-start.21 = (bf16[8,6144]{1,0:T(8,128)(2,1)S(1)}, bf16[8,6144]{1,0:T(8,128)(2,1)S(1)}, u32[]{:S(2)}, u32[]{:S(2)}) collective-permute-start(bf16[8,6144]{1,0:T(8,128)(2,1)S(1)} %shard_map.125), channel_id=1, source_target_pairs={{4,0},{8,4},{12,8},{14,12},{10,14},{6,10},{2,6},{0,2},{5,1},{9,5},... | collective-permute-start | bytes 294920 | tf_op jit(solution)/shard_map/ppermute | solution.py:373
  55.0 4.7 %collective-permute-start.18 = (bf16[8,6144]{1,0:T(8,128)(2,1)S(1)}, bf16[8,6144]{1,0:T(8,128)(2,1)S(1)}, u32[]{:S(2)}, u32[]{:S(2)}) collective-permute-start(bf16[8,6144]{1,0:T(8,128)(2,1)S(1)} %shard_map.123), channel_id=1, source_target_pairs={{0,4},{4,8},{8,12},{12,14},{14,10},{10,6},{6,2},{2,0},{1,5},{5,9},... | collective-permute-start | bytes 294920 | tf_op jit(solution)/shard_map/ppermute | solution.py:370
  56.4 3.3 %collective-permute-start.29 = (bf16[8,6144]{1,0:T(8,128)(2,1)S(1)}, bf16[8,6144]{1,0:T(8,128)(2,1)S(1)}, u32[]{:S(2)}, u32[]{:S(2)}) collective-permute-start(bf16[8,6144]{1,0:T(8,128)(2,1)S(1)} %shard_map.131), channel_id=1, source_target_pairs={{0,1},{1,0},{2,3},{3,2},{4,5},{5,4},{6,7},{7,6},{8,9},{9,8},{10,11... | collective-permute-start | bytes 294920 | tf_op jit(solution)/shard_map/ppermute | solution.py:418
  (1 other events, 2.8 us)
